TPU v7x, 32 devices: a whole 2x2x4 slice. The times are simulated.
32 devices in a mesh: tok: 8 (over z, x), hid: 4 (over y, core).
Axes of the slice: x: 2, y: 2, z: 4, core: 2. Of those that a mesh axis runs over, the one named last changes fastest.
Arguments:
- tokens: bfloat16 [8192, 1152], P('tok', 'hid'), may hold values from -6 to 6
- picture: int32 [8192], replicated, may hold values from -1 to 87, as said below
- cotangent: bfloat16 [8192, 1152], P('tok', 'hid'), may hold values from -6 to 6
- first_gain: float32 [2, 1152], P(None, 'hid'), may hold values from 0.25 to 1.75
- first_shift: float32 [2, 1152], P(None, 'hid'), may hold values from -1.5 to 1.5
- query_weight: bfloat16 [2, 1152, 1152], P(None, 'tok', 'hid'), may hold values from -0.1875 to 0.1875
- query_bias: float32 [2, 1152], P(None, 'hid'), may hold values from -1.5 to 1.5
- key_weight: bfloat16 [2, 1152, 1152], P(None, 'tok', 'hid'), may hold values from -0.1875 to 0.1875
- value_weight: bfloat16 [2, 1152, 1152], P(None, 'tok', 'hid'), may hold values from -0.1875 to 0.1875
- value_bias: float32 [2, 1152], P(None, 'hid'), may hold values from -1.5 to 1.5
- output_weight: bfloat16 [2, 1152, 1152], P(None, 'hid', 'tok'), may hold values from -0.75 to 0.75
- output_bias: float32 [2, 1152], P(None, 'hid'), may hold values from -1.5 to 1.5
- second_gain: float32 [2, 1152], P(None, 'hid'), may hold values from 0.25 to 1.75
- second_shift: float32 [2, 1152], P(None, 'hid'), may hold values from -1.5 to 1.5
- up_weight: bfloat16 [2, 1152, 4304], P(None, 'tok', 'hid'), may hold values from -0.1875 to 0.1875
- up_bias: float32 [2, 4304], P(None, 'hid'), may hold values from -1.5 to 1.5
- down_weight: bfloat16 [2, 4304, 1152], P(None, 'hid', 'tok'), may hold values from -0.09375 to 0.09375
- down_bias: float32 [2, 1152], P(None, 'hid'), may hold values from -1.5 to 1.5
Outputs:
- final_rows: float32 [8192, 1152], P('tok', 'hid')
- grad_tokens: float32 [8192, 1152], P('tok', 'hid')
- grad_first_gain: float32 [2, 1152], P(None, 'hid')
- grad_first_shift: float32 [2, 1152], P(None, 'hid')
- grad_query_weight: float32 [2, 1152, 1152], P(None, 'tok', 'hid')
- grad_query_bias: float32 [2, 1152], P(None, 'hid')
- grad_key_weight: float32 [2, 1152, 1152], P(None, 'tok', 'hid')
- grad_value_weight: float32 [2, 1152, 1152], P(None, 'tok', 'hid')
- grad_value_bias: float32 [2, 1152], P(None, 'hid')
- grad_output_weight: float32 [2, 1152, 1152], P(None, 'hid', 'tok')
- grad_output_bias: float32 [2, 1152], P(None, 'hid')
- grad_second_gain: float32 [2, 1152], P(None, 'hid')
- grad_second_shift: float32 [2, 1152], P(None, 'hid')
- grad_up_weight: float32 [2, 1152, 4304], P(None, 'tok', 'hid')
- grad_up_bias: float32 [2, 4304], P(None, 'hid')
- grad_down_weight: float32 [2, 4304, 1152], P(None, 'hid', 'tok')
- grad_down_bias: float32 [2, 1152], P(None, 'hid')
Inputs may be any that keep to these rules, and one draw needn't show every extreme that they name: Tokens come in packed rows of 2048: tokens r * 2048 to (r + 1) * 2048 - 1 form row r. A row holds whole pictures of 100 to 1024 tokens in a row, each with its own number, then one or more padding tokens numbered -1 at its end. In every row one picture holds tokens on both sides of the row's middle.
All inputs are finite; a program needn't handle non-finite values.
Results may differ from a plain program's by a relative error of at most 0.03.
Values may be sent and summed in bfloat16 or wider, within the bound.
A program may use at most 192 MiB of HBM per device.

v0:
```python
import jax
import jax.numpy as jnp
from jax import lax
from jax.sharding import PartitionSpec as P

D = 1152
HEAD_DIM = 72


eps_norm = 1e-06
gelu_factor = 0.7978845608028654
masked_fill = -1e30
across = (((1,), (1,)), ((), ()))
downward = (((0,), (0,)), ((), ()))


def partner(block, axis, distance):
    count = lax.axis_size(axis)
    route = []
    for low in range(count):
        high = low | 1 << distance
        if high != low and high < count:
            route += [(low, high), (high, low)]
    return lax.ppermute(block, axis, route)


def gelu_tanh(hidden):
    return (
        0.5
        * hidden
        * (1.0 + jnp.tanh(gelu_factor * (hidden + 0.044715 * hidden * hidden * hidden)))
    )


def fetch_layer(weights, layer_index):
    query_part, key_part, value_part, output_part, up_part, down_part = weights
    return (
        lax.all_gather(query_part[layer_index], "tok", axis=0, tiled=True),
        lax.all_gather(key_part[layer_index], "tok", axis=0, tiled=True),
        lax.all_gather(value_part[layer_index], "tok", axis=0, tiled=True),
        lax.all_gather(output_part[layer_index], "tok", axis=1, tiled=True),
        lax.all_gather(up_part[layer_index], "tok", axis=0, tiled=True),
        lax.all_gather(down_part[layer_index], "tok", axis=1, tiled=True),
    )


def normalize(residual, gain, shift):
    whole, gains, shifts = (
        lax.all_gather(residual.astype(jnp.bfloat16), "hid", axis=1, tiled=True).astype(
            residual.dtype
        ),
        lax.all_gather(gain.astype(jnp.bfloat16), "hid", axis=0, tiled=True).astype(gain.dtype),
        lax.all_gather(shift.astype(jnp.bfloat16), "hid", axis=0, tiled=True).astype(shift.dtype),
    )
    row_mean = jnp.mean(whole, axis=1, keepdims=True)
    centred = whole - row_mean
    inverse = lax.rsqrt(jnp.mean(centred * centred, axis=1, keepdims=True) + eps_norm)
    return ((centred * inverse * gains + shifts).astype(jnp.bfloat16), row_mean, inverse)


def column_sum(partial_value):
    return lax.psum_scatter(
        partial_value.astype(jnp.bfloat16), "hid", scatter_dimension=1, tiled=True
    ).astype(jnp.float32)


def spread_rows(gradient):
    return lax.all_gather(gradient, "hid", axis=1, tiled=True)


def norm_backward(grad_normed, residual, row_mean, inverse, gain):
    scaled = (residual - row_mean) * inverse
    grad_scaled = grad_normed * gain
    first_total, second_total = lax.psum(
        (jnp.sum(grad_scaled, axis=1), jnp.sum(grad_scaled * scaled, axis=1)), "hid"
    )
    grad_residual = inverse * (
        grad_scaled - first_total[:, None] / D - scaled * second_total[:, None] / D
    )
    return (grad_residual, jnp.sum(grad_normed * scaled, axis=0), jnp.sum(grad_normed, axis=0))


def tile_layout(queries):
    row_count = queries.shape[0]
    block_rows = min(512, row_count)
    return (row_count, block_rows, row_count // block_rows, queries.shape[1] // HEAD_DIM)


def attend_forward(queries, all_keys, all_values, own_ids, key_ids):
    row_count, block_rows, block_count, head_count = tile_layout(queries)
    factor = HEAD_DIM ** (-0.5)

    def one_tile(tile_index):
        head_index = tile_index // block_count
        block_index = tile_index % block_count
        query_tile = lax.dynamic_slice(
            queries, (block_index * block_rows, head_index * HEAD_DIM), (block_rows, HEAD_DIM)
        )
        key_tile = lax.dynamic_slice_in_dim(all_keys, head_index * HEAD_DIM, HEAD_DIM, 1)
        value_tile = lax.dynamic_slice_in_dim(all_values, head_index * HEAD_DIM, HEAD_DIM, 1)
        query_ids = lax.dynamic_slice_in_dim(own_ids, block_index * block_rows, block_rows)
        scores = (
            lax.dot_general(query_tile, key_tile, across, preferred_element_type=jnp.float32)
            * factor
        )
        scores = jnp.where(query_ids[:, None] == key_ids[None, :], scores, masked_fill)
        highest = jnp.max(scores, axis=1, keepdims=True)
        powers = jnp.exp(scores - highest)
        totals = jnp.sum(powers, axis=1, keepdims=True)
        probs_low = (powers / totals).astype(jnp.bfloat16)
        mixture = jnp.dot(probs_low, value_tile, preferred_element_type=jnp.float32)
        return (mixture, (highest + jnp.log(totals))[:, 0])

    mixture, logsum = lax.map(one_tile, jnp.arange(head_count * block_count, dtype=jnp.int32))
    mixture = mixture.reshape(head_count, block_count, block_rows, HEAD_DIM).transpose(1, 2, 0, 3)
    return (mixture.reshape(row_count, head_count * HEAD_DIM), logsum)


def attend_backward(queries, all_keys, all_values, grad_mixture, logsum, own_ids, key_ids):
    row_count, block_rows, block_count, head_count = tile_layout(queries)
    key_count = all_keys.shape[0]
    factor = HEAD_DIM ** (-0.5)

    def one_tile(tile_index):
        head_index = tile_index // block_count
        block_index = tile_index % block_count
        query_tile = lax.dynamic_slice(
            queries, (block_index * block_rows, head_index * HEAD_DIM), (block_rows, HEAD_DIM)
        )
        grad_tile = lax.dynamic_slice(
            grad_mixture, (block_index * block_rows, head_index * HEAD_DIM), (block_rows, HEAD_DIM)
        )
        key_tile = lax.dynamic_slice_in_dim(all_keys, head_index * HEAD_DIM, HEAD_DIM, 1)
        value_tile = lax.dynamic_slice_in_dim(all_values, head_index * HEAD_DIM, HEAD_DIM, 1)
        query_ids = lax.dynamic_slice_in_dim(own_ids, block_index * block_rows, block_rows)
        scores = (
            lax.dot_general(query_tile, key_tile, across, preferred_element_type=jnp.float32)
            * factor
        )
        scores = jnp.where(query_ids[:, None] == key_ids[None, :], scores, masked_fill)
        probs = jnp.exp(scores - logsum[tile_index][:, None])
        grad_probs = lax.dot_general(
            grad_tile, value_tile, across, preferred_element_type=jnp.float32
        )
        delta = jnp.sum(probs * grad_probs, axis=1, keepdims=True)
        grad_scores = (probs * (grad_probs - delta)).astype(jnp.bfloat16)
        grad_query = jnp.dot(grad_scores, key_tile, preferred_element_type=jnp.float32) * factor
        grad_key = (
            lax.dot_general(grad_scores, query_tile, downward, preferred_element_type=jnp.float32)
            * factor
        )
        grad_value = lax.dot_general(
            probs.astype(jnp.bfloat16), grad_tile, downward, preferred_element_type=jnp.float32
        )
        return (grad_query, grad_key, grad_value)

    grad_query, grad_key, grad_value = lax.map(
        one_tile, jnp.arange(head_count * block_count, dtype=jnp.int32)
    )
    grad_query = grad_query.reshape(head_count, block_count, block_rows, HEAD_DIM).transpose(
        1, 2, 0, 3
    )
    grad_query = grad_query.reshape(row_count, head_count * HEAD_DIM)
    grad_key = (
        grad_key.reshape(head_count, block_count, key_count, HEAD_DIM)
        .sum(axis=1)
        .transpose(1, 0, 2)
    )
    grad_value = (
        grad_value.reshape(head_count, block_count, key_count, HEAD_DIM)
        .sum(axis=1)
        .transpose(1, 0, 2)
    )
    return (
        grad_query,
        grad_key.reshape(key_count, head_count * HEAD_DIM),
        grad_value.reshape(key_count, head_count * HEAD_DIM),
    )


def body(
    tokens,
    picture,
    cotangent,
    first_gain,
    first_shift,
    query_weight,
    query_bias,
    key_weight,
    value_weight,
    value_bias,
    output_weight,
    output_bias,
    second_gain,
    second_shift,
    up_weight,
    up_bias,
    down_weight,
    down_bias,
):
    row_count = tokens.shape[0]
    layer_count = query_weight.shape[0]
    head_cols = query_bias.shape[1]
    weights = (query_weight, key_weight, value_weight, output_weight, up_weight, down_weight)
    location = lax.axis_index("tok")
    own_ids = lax.dynamic_slice_in_dim(picture, location * row_count, row_count)
    far_ids = lax.dynamic_slice_in_dim(picture, jnp.bitwise_xor(location, 1) * row_count, row_count)
    key_ids = jnp.concatenate([own_ids, far_ids])
    residual = tokens.astype(jnp.float32)
    saved = []
    for layer_index in range(layer_count):
        fetched = fetch_layer(weights, layer_index)
        query_full, key_full, value_full, output_full, up_full, down_full = fetched
        normed, mean_one, inverse_one = normalize(
            residual, first_gain[layer_index], first_shift[layer_index]
        )
        queries = (
            jnp.dot(normed, query_full, preferred_element_type=jnp.float32)
            + query_bias[layer_index]
        ).astype(jnp.bfloat16)
        key_rows = jnp.dot(normed, key_full, preferred_element_type=jnp.float32).astype(
            jnp.bfloat16
        )
        value_rows = (
            jnp.dot(normed, value_full, preferred_element_type=jnp.float32)
            + value_bias[layer_index]
        ).astype(jnp.bfloat16)
        far_pair = partner(jnp.stack([key_rows, value_rows]), "tok", 0)
        all_keys = jnp.concatenate([key_rows, far_pair[0]])
        all_values = jnp.concatenate([value_rows, far_pair[1]])
        mixture, logsum = attend_forward(queries, all_keys, all_values, own_ids, key_ids)
        mixture = mixture.astype(jnp.bfloat16)
        after = (
            residual
            + column_sum(jnp.dot(mixture, output_full, preferred_element_type=jnp.float32))
            + output_bias[layer_index]
        )
        normed_two, mean_two, inverse_two = normalize(
            after, second_gain[layer_index], second_shift[layer_index]
        )
        hidden = (
            jnp.dot(normed_two, up_full, preferred_element_type=jnp.float32) + up_bias[layer_index]
        )
        active = gelu_tanh(hidden).astype(jnp.bfloat16)
        kept = None
        saved.append(
            (
                residual,
                mean_one,
                inverse_one,
                normed,
                queries,
                all_keys,
                all_values,
                logsum,
                mixture,
                after,
                mean_two,
                inverse_two,
                normed_two,
                hidden,
                active,
                kept,
            )
        )
        residual = (
            after
            + column_sum(jnp.dot(active, down_full, preferred_element_type=jnp.float32))
            + down_bias[layer_index]
        )
    final_rows = residual
    gradient = cotangent.astype(jnp.float32)
    weight_grads = [None] * layer_count
    narrow_grads = [None] * layer_count
    broad_grads = [None] * layer_count
    for layer_index in reversed(range(layer_count)):
        (
            residual,
            mean_one,
            inverse_one,
            normed,
            queries,
            all_keys,
            all_values,
            logsum,
            mixture,
            after,
            mean_two,
            inverse_two,
            normed_two,
            hidden,
            active,
            kept,
        ) = saved[layer_index]
        fetched = fetch_layer(weights, layer_index)
        query_full, key_full, value_full, output_full, up_full, down_full = fetched
        grad_down = gradient.astype(jnp.bfloat16)
        down_rows = spread_rows(grad_down)
        grad_active = lax.dot_general(
            down_rows, down_full, across, preferred_element_type=jnp.float32
        )
        down_term = lax.dot_general(active, down_rows, downward, preferred_element_type=jnp.float32)
        grad_hidden = jax.vjp(gelu_tanh, hidden)[1](grad_active)[0].astype(jnp.bfloat16)
        grad_normed_two = column_sum(
            lax.dot_general(grad_hidden, up_full, across, preferred_element_type=jnp.float32)
        )
        grad_after, second_gain_grad, second_shift_grad = norm_backward(
            grad_normed_two, after, mean_two, inverse_two, second_gain[layer_index]
        )
        grad_after = gradient + grad_after
        grad_output = grad_after.astype(jnp.bfloat16)
        output_rows = spread_rows(grad_output)
        output_term = lax.dot_general(
            mixture, output_rows, downward, preferred_element_type=jnp.float32
        )
        grad_mixture = lax.dot_general(
            output_rows, output_full, across, preferred_element_type=jnp.float32
        ).astype(jnp.bfloat16)
        grad_queries, grad_keys, grad_values = attend_backward(
            queries, all_keys, all_values, grad_mixture, logsum, own_ids, key_ids
        )
        back_pair = partner(
            jnp.stack([grad_keys[row_count:], grad_values[row_count:]]).astype(jnp.bfloat16),
            "tok",
            0,
        ).astype(jnp.float32)
        grad_queries = grad_queries.astype(jnp.bfloat16)
        grad_keys = (grad_keys[:row_count] + back_pair[0]).astype(jnp.bfloat16)
        grad_values = (grad_values[:row_count] + back_pair[1]).astype(jnp.bfloat16)
        grad_normed = column_sum(
            lax.dot_general(grad_queries, query_full, across, preferred_element_type=jnp.float32)
            + lax.dot_general(grad_keys, key_full, across, preferred_element_type=jnp.float32)
            + lax.dot_general(grad_values, value_full, across, preferred_element_type=jnp.float32)
        )
        grad_residual, first_gain_grad, first_shift_grad = norm_backward(
            grad_normed, residual, mean_one, inverse_one, first_gain[layer_index]
        )
        input_sum = lax.psum_scatter(
            jnp.concatenate(
                [
                    lax.dot_general(
                        normed, grad_queries, downward, preferred_element_type=jnp.float32
                    ),
                    lax.dot_general(
                        normed, grad_keys, downward, preferred_element_type=jnp.float32
                    ),
                    lax.dot_general(
                        normed, grad_values, downward, preferred_element_type=jnp.float32
                    ),
                    lax.dot_general(
                        normed_two, grad_hidden, downward, preferred_element_type=jnp.float32
                    ),
                ],
                axis=1,
            ).astype(jnp.bfloat16),
            "tok",
            scatter_dimension=0,
            tiled=True,
        ).astype(jnp.float32)
        output_sum, down_sum = (
            lax.psum_scatter(
                output_term.astype(jnp.bfloat16), "tok", scatter_dimension=1, tiled=True
            ).astype(jnp.float32),
            lax.psum_scatter(
                down_term.astype(jnp.bfloat16), "tok", scatter_dimension=1, tiled=True
            ).astype(jnp.float32),
        )
        weight_grads[layer_index] = (input_sum, output_sum, down_sum)
        narrow_grads[layer_index] = jnp.stack(
            [
                first_gain_grad,
                first_shift_grad,
                jnp.sum(grad_queries.astype(jnp.float32), axis=0),
                jnp.sum(grad_values.astype(jnp.float32), axis=0),
                jnp.sum(grad_output.astype(jnp.float32), axis=0),
                second_gain_grad,
                second_shift_grad,
                jnp.sum(grad_down.astype(jnp.float32), axis=0),
            ]
        )
        broad_grads[layer_index] = jnp.sum(grad_hidden.astype(jnp.float32), axis=0)
        gradient = grad_after + grad_residual
    narrow_total, broad_total = lax.psum((jnp.stack(narrow_grads), jnp.stack(broad_grads)), "tok")
    stacked_input = jnp.stack([stored[0] for stored in weight_grads])
    stacked_output = jnp.stack([stored[1] for stored in weight_grads])
    stacked_down = jnp.stack([stored[2] for stored in weight_grads])
    return (
        final_rows,
        gradient,
        narrow_total[:, 0],
        narrow_total[:, 1],
        stacked_input[:, :, :head_cols],
        narrow_total[:, 2],
        stacked_input[:, :, head_cols : 2 * head_cols],
        stacked_input[:, :, 2 * head_cols : 3 * head_cols],
        narrow_total[:, 3],
        stacked_output,
        narrow_total[:, 4],
        narrow_total[:, 5],
        narrow_total[:, 6],
        stacked_input[:, :, 3 * head_cols :],
        broad_total,
        stacked_down,
        narrow_total[:, 7],
    )


def solution(mesh):
    in_specs = (
        P("tok", "hid"),
        P(),
        P("tok", "hid"),
        P(None, "hid"),
        P(None, "hid"),
        P(None, "tok", "hid"),
        P(None, "hid"),
        P(None, "tok", "hid"),
        P(None, "tok", "hid"),
        P(None, "hid"),
        P(None, "hid", "tok"),
        P(None, "hid"),
        P(None, "hid"),
        P(None, "hid"),
        P(None, "tok", "hid"),
        P(None, "hid"),
        P(None, "hid", "tok"),
        P(None, "hid"),
    )
    out_specs = (
        P("tok", "hid"),
        P("tok", "hid"),
        P(None, "hid"),
        P(None, "hid"),
        P(None, "tok", "hid"),
        P(None, "hid"),
        P(None, "tok", "hid"),
        P(None, "tok", "hid"),
        P(None, "hid"),
        P(None, "hid", "tok"),
        P(None, "hid"),
        P(None, "hid"),
        P(None, "hid"),
        P(None, "tok", "hid"),
        P(None, "hid"),
        P(None, "hid", "tok"),
        P(None, "hid"),
    )
    return jax.shard_map(body, mesh=mesh, in_specs=in_specs, out_specs=out_specs, check_vma=False)
```

profile of v0, /device:TPU:0, one launch (start us, length us, event | category | flops | bytes accessed | tf_op | source)
XLA Modules:
  0.0 1929.2 jit_solution(7097213809589875604)
XLA Ops:
  15.9 14.3 all-reduce.13
  38.0 33.0 %all-gather.3 = bf16[1,1152,288]{2,1,0:T(8,128)(2,1)S(1)} all-gather(bf16[1,144,288]{2,1,0:T(8,128)(2,1)S(1)} %get-tuple-element.1043), channel_id=5, replica_groups=mesh['tok'=8,'hid'=4] {'tok'}, dimensions={1}, use_global_device_ids=true | all-gather | bytes 746496 | tf_op jit(solution)/shard_map/all_gather | solution.py:40
  71.0 31.9 %all-gather.2 = bf16[1,1152,288]{2,1,0:T(8,128)(2,1)S(1)} all-gather(bf16[1,144,288]{2,1,0:T(8,128)(2,1)S(1)} %get-tuple-element.1041), channel_id=4, replica_groups=mesh['tok'=8,'hid'=4] {'tok'}, dimensions={1}, use_global_device_ids=true | all-gather | bytes 746496 | tf_op jit(solution)/shard_map/all_gather | solution.py:39
  113.5 49.2 %all-gather.4 = bf16[1,288,1152]{1,2,0:T(8,128)(2,1)} all-gather(bf16[1,288,144]{1,2,0:T(8,128)(2,1)S(1)} %get-tuple-element.1039), channel_id=6, replica_groups=mesh['tok'=8,'hid'=4] {'tok'}, dimensions={2}, use_global_device_ids=true | all-gather | bytes 746496 | tf_op jit(solution)/shard_map/all_gather | solution.py:41
  162.8 32.3 %all-gather.1 = bf16[1,1152,288]{2,1,0:T(8,128)(2,1)S(1)} all-gather(bf16[1,144,288]{2,1,0:T(8,128)(2,1)S(1)} %get-tuple-element.1045), channel_id=3, replica_groups=mesh['tok'=8,'hid'=4] {'tok'}, dimensions={1}, use_global_device_ids=true | all-gather | bytes 746496 | tf_op jit(solution)/shard_map/all_gather | solution.py:38
  204.6 63.3 %while.60 = (s32[]{:T(128)}, bf16[8,512,72]{1,2,0:T(8,128)(2,1)}, f32[8,512]{1,0:T(8,128)S(1)}, s32[8]{0:T(128)S(1)}, s32[1024]{0:T(1024)S(1)}, /*index=5*/s32[2...) while((s32[]{:T(128)}, bf16[8,512,72]{1,2,0:T(8,128)(2,1)}, ...), condition=%wide.region_5.6_spmd, body=%wide.region_2.5_spmd.sunk | while | flops 311426592 | bytes 13946840 | solution.py:114
  275.1 32.2 %reduce-scatter.19.cloned.1.call-done = bf16[1024,288]{0,1:T(8,128)(2,1)} async-done(((bf16[1024,1152]{0,1:T(8,128)(2,1)}), bf16[1024,288]{0,1:T(8,128)(2,1)}) %reduce-scatter.19.cloned.1.call-update) | async-done | bytes 589840 | tf_op jit(solution)/shard_map/reduce_scatter | solution.py:62
  312.2 21.4 %all-gather.31.cloned.1.call-done = bf16[1024,1152]{0,1:T(8,128)(2,1)} async-done(((bf16[1024,288]{0,1:T(8,128)(2,1)}), bf16[1024,1152]{0,1:T(8,128)(2,1)}) %all-gather.31.cloned.1.call-update) | async-done | bytes 2359312 | tf_op jit(solution)/shard_map/all_gather | solution.py:49
  336.7 54.8 %all-gather.45.cloned.1.call-done = bf16[1,1152,1076]{2,1,0:T(8,128)(2,1)} async-done(((bf16[1,144,1076]{2,1,0:T(8,128)(2,1)}), bf16[1,1152,1076]{2,1,0:T(8,128)(2,1)}) %all-gather.45.cloned.1.call-update) | async-done | bytes 2479120 | tf_op jit(solution)/shard_map/all_gather | solution.py:42
  391.5 7.8 convolution_add_fusion.5
  399.3 48.7 %all-gather.47.cloned.1.call-done = bf16[1,1076,1152]{1,2,0:T(8,128)(2,1)} async-done(((bf16[1,1076,144]{1,2,0:T(8,128)(2,1)}), bf16[1,1076,1152]{1,2,0:T(8,128)(2,1)}) %all-gather.47.cloned.1.call-update) | async-done | bytes 2479120 | tf_op jit(solution)/shard_map/all_gather | solution.py:43
  447.9 7.9 convolution_convert_fusion.9
  457.1 30.6 %reduce-scatter.21.cloned.1.call-done = bf16[1024,288]{0,1:T(8,128)(2,1)} async-done(((bf16[1024,1152]{0,1:T(8,128)(2,1)}), bf16[1024,288]{0,1:T(8,128)(2,1)}) %reduce-scatter.21.cloned.1.call-update) | async-done | bytes 589840 | tf_op jit(solution)/shard_map/reduce_scatter | solution.py:62
  490.0 32.5 %all-gather.11 = bf16[1,1152,288]{2,1,0:T(8,128)(2,1)S(1)} all-gather(bf16[1,144,288]{2,1,0:T(8,128)(2,1)S(1)} %copy-done.67), channel_id=13, replica_groups=mesh['tok'=8,'hid'=4] {'tok'}, dimensions={1}, use_global_device_ids=true | all-gather | bytes 746496 | tf_op jit(solution)/shard_map/all_gather | solution.py:40
  522.5 32.5 %all-gather.10 = bf16[1,1152,288]{2,1,0:T(8,128)(2,1)S(1)} all-gather(bf16[1,144,288]{2,1,0:T(8,128)(2,1)S(1)} %copy-done.66), channel_id=12, replica_groups=mesh['tok'=8,'hid'=4] {'tok'}, dimensions={1}, use_global_device_ids=true | all-gather | bytes 746496 | tf_op jit(solution)/shard_map/all_gather | solution.py:39
  565.0 50.0 %all-gather.12 = bf16[1,288,1152]{1,2,0:T(8,128)(2,1)} all-gather(bf16[1,288,144]{1,2,0:T(8,128)(2,1)} %get-tuple-element.1038), channel_id=14, replica_groups=mesh['tok'=8,'hid'=4] {'tok'}, dimensions={2}, use_global_device_ids=true | all-gather | bytes 746496 | tf_op jit(solution)/shard_map/all_gather | solution.py:41
  615.0 32.0 %all-gather.9 = bf16[1,1152,288]{2,1,0:T(8,128)(2,1)S(1)} all-gather(bf16[1,144,288]{2,1,0:T(8,128)(2,1)} %get-tuple-element.1044), channel_id=11, replica_groups=mesh['tok'=8,'hid'=4] {'tok'}, dimensions={1}, use_global_device_ids=true | all-gather | bytes 746496 | tf_op jit(solution)/shard_map/all_gather | solution.py:38
  661.2 80.9 %while.61 = (s32[]{:T(128)}, bf16[8,512,72]{1,2,0:T(8,128)(2,1)}, f32[8,512]{1,0:T(8,128)}, s32[8]{0:T(128)}, s32[1024]{0:T(1024)S(1)}, /*index=5*/s32[2048]{0:T...) while((s32[]{:T(128)}, bf16[8,512,72]{1,2,0:T(8,128)(2,1)}, ...), condition=%wide.region_15.16_spmd, body=%wide.region_12.15_spmd.sunk | while | flops 311426592 | bytes 13946840 | solution.py:114
  677.0 3.1 fusion.272
  747.8 33.3 %reduce-scatter.23.cloned.1.call-done = bf16[1024,288]{0,1:T(8,128)(2,1)} async-done(((bf16[1024,1152]{0,1:T(8,128)(2,1)}), bf16[1024,288]{0,1:T(8,128)(2,1)}) %reduce-scatter.23.cloned.1.call-update) | async-done | bytes 589840 | tf_op jit(solution)/shard_map/reduce_scatter | solution.py:62
  785.6 21.8 %all-gather.35.cloned.1.call-done = bf16[1024,1152]{0,1:T(8,128)(2,1)} async-done(((bf16[1024,288]{0,1:T(8,128)(2,1)}), bf16[1024,1152]{0,1:T(8,128)(2,1)}) %all-gather.35.cloned.1.call-update) | async-done | bytes 2359312 | tf_op jit(solution)/shard_map/all_gather | solution.py:49
  810.5 54.8 %all-gather.49.cloned.1.call-done = bf16[1,1152,1076]{2,1,0:T(8,128)(2,1)} async-done(((bf16[1,144,1076]{2,1,0:T(8,128)(2,1)}), bf16[1,1152,1076]{2,1,0:T(8,128)(2,1)}) %all-gather.49.cloned.1.call-update) | async-done | bytes 2479120 | tf_op jit(solution)/shard_map/all_gather | solution.py:42
  865.3 7.8 convolution_add_fusion.4
  873.1 16.5 all-gather.37.cloned.1.call-done
  889.6 57.9 %all-gather.51.cloned.1.call-done = bf16[1,1076,1152]{1,2,0:T(8,128)(2,1)} async-done(((bf16[1,1076,144]{1,2,0:T(8,128)(2,1)}), bf16[1,1076,1152]{1,2,0:T(8,128)(2,1)}) %all-gather.51.cloned.1.call-update) | async-done | bytes 2479120 | tf_op jit(solution)/shard_map/all_gather | solution.py:43
  947.5 10.2 convert_reduce_fusion.4
  959.1 4.4 convolution_convert_fusion.7
  963.6 31.7 %reduce-scatter.27.cloned.1.call-done = bf16[1024,288]{0,1:T(8,128)(2,1)} async-done(((bf16[1024,1152]{0,1:T(8,128)(2,1)}), bf16[1024,288]{0,1:T(8,128)(2,1)}) %reduce-scatter.27.cloned.1.call-update) | async-done | bytes 589840 | tf_op jit(solution)/shard_map/reduce_scatter | solution.py:62
  997.7 5.8 all-reduce.12
  1003.6 3.4 convert_reduce_fusion.11
  1007.2 25.1 %all-gather.39.cloned.1.call-done = bf16[1024,1152]{0,1:T(8,128)(2,1)} async-done(((bf16[1024,288]{0,1:T(8,128)(2,1)}), bf16[1024,1152]{0,1:T(8,128)(2,1)}) %all-gather.39.cloned.1.call-update) | async-done | bytes 2359312 | tf_op jit(solution)/shard_map/all_gather | solution.py:68
  1032.3 3.7 convolution_convert_fusion.19
  1042.3 133.1 %while.62 = (s32[]{:T(128)}, bf16[8,512,72]{1,2,0:T(8,128)(2,1)}, f32[8,2048,72]{1,2,0:T(8,128)}, f32[8,2048,72]{1,2,0:T(8,128)}, s32[8]{0:T(128)S(1)}, /*index=...) while((s32[]{:T(128)}, bf16[8,512,72]{1,2,0:T(8,128)(2,1)}, ...), condition=%wide.region_27.28_spmd, body=%wide.region_25.27_spmd.sunk | while | flops 765644288 | bytes 34795048 | solution.py:157
  1175.4 3.1 bitcast_reduce_fusion.2
  1183.6 24.5 %collective-permute-done.2 = bf16[2,1024,288]{1,2,0:T(8,128)(2,1)S(1)} collective-permute-done((bf16[2,1024,288]{1,2,0:T(8,128)(2,1)S(1)}, bf16[2,1024,288]{1,2,0:T(8,128)(2,1)S(1)}, u32[]{:S(2)}, u32[]{:S(2)}) %collective-permute-start.2) | collective-permute-done | bytes 1179680 | tf_op jit(solution)/shard_map/ppermute | solution.py:24
  1215.1 7.9 convolution_convert_fusion.8
  1223.1 25.0 %reduce-scatter.29.cloned.1.call-done = bf16[1024,288]{0,1:T(8,128)(2,1)} async-done(((bf16[1024,1152]{0,1:T(8,128)(2,1)}), bf16[1024,288]{0,1:T(8,128)(2,1)}) %reduce-scatter.29.cloned.1.call-update) | async-done | bytes 589840 | tf_op jit(solution)/shard_map/reduce_scatter | solution.py:62
  1250.2 5.8 all-reduce.11
  1256.1 27.6 %reduce-scatter.25.cloned.1.call-done = bf16[1024,288]{0,1:T(8,128)(2,1)} async-done(((bf16[1024,1152]{0,1:T(8,128)(2,1)}), bf16[1024,288]{0,1:T(8,128)(2,1)}) %reduce-scatter.25.cloned.1.call-update) | async-done | bytes 589840 | tf_op jit(solution)/shard_map/reduce_scatter | solution.py:62
  1283.7 4.9 convert_reduce_fusion.14
  1288.7 24.2 %all-gather.41.cloned.1.call-done = bf16[1024,1152]{0,1:T(8,128)(2,1)} async-done(((bf16[1024,288]{0,1:T(8,128)(2,1)}), bf16[1024,1152]{0,1:T(8,128)(2,1)}) %all-gather.41.cloned.1.call-update) | async-done | bytes 2359312 | tf_op jit(solution)/shard_map/all_gather | solution.py:68
  1312.9 9.5 convert_reduce_fusion.5
  1323.8 4.5 convolution_convert_fusion.6
  1328.4 33.2 %reduce-scatter.31.cloned.1.call-done = bf16[1024,288]{0,1:T(8,128)(2,1)} async-done(((bf16[1024,1152]{0,1:T(8,128)(2,1)}), bf16[1024,288]{0,1:T(8,128)(2,1)}) %reduce-scatter.31.cloned.1.call-update) | async-done | bytes 589840 | tf_op jit(solution)/shard_map/reduce_scatter | solution.py:62
  1363.4 6.3 all-reduce.10
  1372.4 5.7 convolution_convert_fusion.2
  1384.1 6.7 copy.145
  1390.9 7.9 convolution_convert_fusion
  1399.0 7.9 convolution_convert_fusion.1
  1408.0 4.4 convolution_convert_fusion.10
  1412.5 3.5 convolution_convert_fusion.18
  1421.6 128.6 %while.63 = (s32[]{:T(128)}, bf16[8,512,72]{1,2,0:T(8,128)(2,1)S(1)}, f32[8,2048,72]{1,2,0:T(8,128)}, f32[8,2048,72]{1,2,0:T(8,128)}, s32[8]{0:T(128)S(1)}, /*in...) while((s32[]{:T(128)}, ...), condition=%wide.region_42.43_spmd, body=%wide.region_40.42_spmd.sunk | while | flops 765644288 | bytes 34795048 | solution.py:157
  1550.1 3.3 bitcast_reduce_fusion
  1563.4 24.5 %collective-permute-done.3 = bf16[2,1024,288]{1,2,0:T(8,128)(2,1)} collective-permute-done((bf16[2,1024,288]{1,2,0:T(8,128)(2,1)}, bf16[2,1024,288]{1,2,0:T(8,128)(2,1)}, u32[]{:S(2)}, u32[]{:S(2)}) %collective-permute-start.3) | collective-permute-done | bytes 1179680 | tf_op jit(solution)/shard_map/ppermute | solution.py:24
  1597.2 5.9 convolution_convert_fusion.3
  1608.8 6.7 copy.143
  1619.5 27.5 %reduce-scatter.39.cloned.1.call-done = bf16[1076,144]{0,1:T(8,128)(2,1)} async-done(((bf16[1076,1152]{0,1:T(8,128)(2,1)}), bf16[1076,144]{0,1:T(8,128)(2,1)}) %reduce-scatter.39.cloned.1.call-update) | async-done | bytes 309904 | tf_op jit(solution)/shard_map/reduce_scatter | solution.py:364
  1650.7 60.5 %reduce-scatter.37.cloned.1.call-done = bf16[288,144]{0,1:T(8,128)(2,1)} async-done(((bf16[288,1152]{0,1:T(8,128)(2,1)}), bf16[288,144]{0,1:T(8,128)(2,1)}) %reduce-scatter.37.cloned.1.call-update) | async-done | bytes 82960 | tf_op jit(solution)/shard_map/reduce_scatter | solution.py:361
  1711.2 63.9 %reduce-scatter.35.cloned.1.call-done = bf16[288,144]{0,1:T(8,128)(2,1)} async-done(((bf16[288,1152]{0,1:T(8,128)(2,1)}), bf16[288,144]{0,1:T(8,128)(2,1)}) %reduce-scatter.35.cloned.1.call-update) | async-done | bytes 82960 | tf_op jit(solution)/shard_map/reduce_scatter | solution.py:361
  1776.9 33.0 %reduce-scatter.33.cloned.1.call-done = bf16[1024,288]{0,1:T(8,128)(2,1)} async-done(((bf16[1024,1152]{0,1:T(8,128)(2,1)}), bf16[1024,288]{0,1:T(8,128)(2,1)}) %reduce-scatter.33.cloned.1.call-update) | async-done | bytes 589840 | tf_op jit(solution)/shard_map/reduce_scatter | solution.py:62
  1811.5 5.9 all-reduce.9
  1817.5 40.9 %all-reduce.8 = (f32[2,8,288]{2,0,1:T(2,128)S(1)}, f32[2,1076]{1,0:T(2,128)}) all-reduce(f32[2,8,288]{2,0,1:T(2,128)S(1)} %pad_maximum_fusion.11, f32[2,1076]{1,0:T(2,128)S(1)} %pad_maximum_fusion.12), channel_id=1, replica_groups=mesh['tok'=8,'hid'=4] {'tok'}, use_global_device_ids=true, to_apply=%region_68.69 | all-reduce | flops 6760 | bytes 54080 | tf_op jit(solution)/shard_map/psum | solution.py:383
  1859.0 3.1 fusion.126
  1862.1 47.9 %reduce-scatter.43.cloned.1.call-done = bf16[144,1940]{1,0:T(8,128)(2,1)} async-done(((bf16[1152,1940]{1,0:T(8,128)(2,1)}), bf16[144,1940]{1,0:T(8,128)(2,1)}) %reduce-scatter.43.cloned.1.call-update) | async-done | bytes 558736
  (749 shorter events, 480.9 us)
Async XLA Ops:
  7.2 95.7 %all-gather.29.cloned.1.call-start = ((), (), s32[]{:S(2)}) async-start(), calls=%async_computation.14 | async-start | bytes 2949120 | tf_op jit(solution)/shard_map/all_gather | solution.py:49
  7.9 299.3 %reduce-scatter.19.cloned.1.call-start = ((), (), s32[]{:S(2)}) async-start(), calls=%async_computation.15 | async-start | bytes 2949120 | tf_op jit(solution)/shard_map/reduce_scatter | solution.py:62
  71.0 37.3 %copy-start.31 = (bf16[1,1152,288]{2,1,0:T(8,128)(2,1)}, bf16[1,1152,288]{2,1,0:T(8,128)(2,1)S(1)}, u32[]{:S(2)}) copy-start(bf16[1,1152,288]{2,1,0:T(8,128)(2,1)S(1)} %all-gather.3) | copy-start | bytes 1990660
  110.8 89.0 %collective-permute-start = (bf16[2,1024,288]{1,2,0:T(8,128)(2,1)}, bf16[2,1024,288]{1,2,0:T(8,128)(2,1)S(1)}, u32[]{:S(2)}, u32[]{:S(2)}) collective-permute-start(bf16[2,1024,288]{1,2,0:T(8,128)(2,1)} %pad_maximum_fusion.2), channel_id=1, source_target_pairs={{0,4},{4,0},{8,12},{12,8},{16,20},{20,16},{24,28},{28,24},{1,5},{5... | collective-permute-start | bytes 3538952 | tf_op jit(solution)/shard_map/ppermute | solution.py:24
  273.8 33.5 %copy-start.2 = (bf16[1024,288]{0,1:T(8,128)(2,1)S(1)}, bf16[1024,288]{0,1:T(8,128)(2,1)}, u32[]{:S(2)}) copy-start(bf16[1024,288]{0,1:T(8,128)(2,1)} %param.26) | copy-start | bytes 1769476
  273.8 35.6 %copy-start.60 = (bf16[2,144,1076]{2,1,0:T(8,128)(2,1)S(1)}, bf16[2,144,1076]{2,1,0:T(8,128)(2,1)}, u32[]{:S(2)}) copy-start(bf16[2,144,1076]{2,1,0:T(8,128)(2,1)} %param.40) | copy-start | bytes 1859332
  273.8 36.6 %copy-start.61 = (bf16[2,1076,144]{1,2,0:T(8,128)(2,1)S(1)}, bf16[2,1076,144]{1,2,0:T(8,128)(2,1)}, u32[]{:S(2)}) copy-start(bf16[2,1076,144]{1,2,0:T(8,128)(2,1)} %param.42) | copy-start | bytes 1859332
  273.8 59.8 %all-gather.31.cloned.1.call-start = ((), (), s32[]{:S(2)}) async-start(), calls=%async_computation.16 | async-start | bytes 2949120 | tf_op jit(solution)/shard_map/all_gather | solution.py:49
  275.1 212.7 %copy-start.75 = (f32[288]{0:T(512)}, f32[288]{0:T(512)S(1)}, u32[]{:S(2)}) copy-start(f32[288]{0:T(512)S(1)} %get-tuple-element.892) | copy-start | bytes 3460
  309.4 82.1 %all-gather.45.cloned.1.call-start = ((), (), s32[]{:S(2)}) async-start(), calls=%async_computation.34 | async-start | bytes 2985984 | tf_op jit(solution)/shard_map/all_gather | solution.py:42
  310.3 137.6 %all-gather.47.cloned.1.call-start = ((), (), s32[]{:S(2)}) async-start(), calls=%async_computation.35 | async-start | bytes 2985984 | tf_op jit(solution)/shard_map/all_gather | solution.py:43
  311.3 176.4 %reduce-scatter.21.cloned.1.call-start = ((), (), s32[]{:S(2)}) async-start(), calls=%async_computation.17 | async-start | bytes 2949120 | tf_op jit(solution)/shard_map/reduce_scatter | solution.py:62
  311.5 79.9 %copy-start.99 = (f32[1152]{0:T(1024)}, f32[1152]{0:T(1024)S(1)}, u32[]{:S(2)}) copy-start(f32[1152]{0:T(1024)S(1)} %convert_element_type.460) | copy-start | bytes 13828
  311.6 79.9 %copy-start.101 = (f32[1152]{0:T(1024)}, f32[1152]{0:T(1024)S(1)}, u32[]{:S(2)}) copy-start(f32[1152]{0:T(1024)S(1)} %convert_element_type.377) | copy-start | bytes 13828
  336.0 63.3 %copy-start.73 = (f32[1024]{0:T(1024)}, f32[1024]{0:T(1024)S(1)}, u32[]{:S(2)}) copy-start(f32[1024]{0:T(1024)S(1)} %broadcast_multiply_fusion.6) | copy-start | bytes 12292
  336.7 62.6 %copy-start.81 = (f32[1024]{0:T(1024)}, f32[1024]{0:T(1024)S(1)}, u32[]{:S(2)}) copy-start(f32[1024]{0:T(1024)S(1)} %add_rsqrt_fusion.2) | copy-start | bytes 12292
  455.9 34.2 %copy-start.67 = (bf16[1,144,288]{2,1,0:T(8,128)(2,1)S(1)}, bf16[1,144,288]{2,1,0:T(8,128)(2,1)}, u32[]{:S(2)}) copy-start(bf16[1,144,288]{2,1,0:T(8,128)(2,1)} %get-tuple-element.1042) | copy-start | bytes 248836
  455.9 99.1 %all-gather.33.cloned.1.call-start = ((), (), s32[]{:S(2)}) async-start(), calls=%async_computation.18 | async-start | bytes 2949120 | tf_op jit(solution)/shard_map/all_gather | solution.py:49
  487.7 34.8 %copy-start.66 = (bf16[1,144,288]{2,1,0:T(8,128)(2,1)S(1)}, bf16[1,144,288]{2,1,0:T(8,128)(2,1)}, u32[]{:S(2)}) copy-start(bf16[1,144,288]{2,1,0:T(8,128)(2,1)} %get-tuple-element.1040) | copy-start | bytes 248836
  490.0 291.2 %reduce-scatter.23.cloned.1.call-start = ((), (), s32[]{:S(2)}) async-start(), calls=%async_computation.19 | async-start | bytes 2949120 | tf_op jit(solution)/shard_map/reduce_scatter | solution.py:62
  522.5 37.9 %copy-start.33 = (bf16[1,1152,288]{2,1,0:T(8,128)(2,1)}, bf16[1,1152,288]{2,1,0:T(8,128)(2,1)S(1)}, u32[]{:S(2)}) copy-start(bf16[1,1152,288]{2,1,0:T(8,128)(2,1)S(1)} %all-gather.11) | copy-start | bytes 1990660
  561.8 86.1 %copy-start.48 = (bf16[1024,1152]{0,1:T(8,128)(2,1)S(1)}, bf16[1024,1152]{0,1:T(8,128)(2,1)}, u32[]{:S(2)}) copy-start(bf16[1024,1152]{0,1:T(8,128)(2,1)} %copy-done.47) | copy-start | bytes 7077892
  563.0 88.2 %collective-permute-start.1 = (bf16[2,1024,288]{1,2,0:T(8,128)(2,1)}, bf16[2,1024,288]{1,2,0:T(8,128)(2,1)}, u32[]{:S(2)}, u32[]{:S(2)}) collective-permute-start(bf16[2,1024,288]{1,2,0:T(8,128)(2,1)} %pad_maximum_fusion.5), channel_id=1, source_target_pairs={{0,4},{4,0},{8,12},{12,8},{16,20},{20,16},{24,28},{28,24},{1,5},{5... | collective-permute-start | bytes 3538952 | tf_op jit(solution)/shard_map/ppermute | solution.py:24
  747.7 33.4 %copy-start.87 = (f32[288]{0:T(512)S(1)}, f32[288]{0:T(512)}, u32[]{:S(2)}) copy-start(f32[288]{0:T(512)} %get-tuple-element.893) | copy-start | bytes 3460
  747.7 37.8 %copy-start.110 = (bf16[1152]{0:T(1024)(128)(2,1)S(1)}, bf16[1152]{0:T(1024)(128)(2,1)}, u32[]{:S(2)}) copy-start(bf16[1152]{0:T(1024)(128)(2,1)} %get-tuple-element.998) | copy-start | bytes 6916
  747.8 37.8 %copy-start.109 = (bf16[1152]{0:T(1024)(128)(2,1)S(1)}, bf16[1152]{0:T(1024)(128)(2,1)}, u32[]{:S(2)}) copy-start(bf16[1152]{0:T(1024)(128)(2,1)} %get-tuple-element.999) | copy-start | bytes 6916
  747.8 59.7 %all-gather.35.cloned.1.call-start = ((), (), s32[]{:S(2)}) async-start(), calls=%async_computation.20 | async-start | bytes 2949120 | tf_op jit(solution)/shard_map/all_gather | solution.py:49
  783.2 82.1 %all-gather.49.cloned.1.call-start = ((), (), s32[]{:S(2)}) async-start(), calls=%async_computation.36 | async-start | bytes 2985984 | tf_op jit(solution)/shard_map/all_gather | solution.py:42
  783.8 105.8 %all-gather.37.cloned.1.call-start = ((), (), s32[]{:S(2)}) async-start(), calls=%async_computation.22 | async-start | bytes 2949120 | tf_op jit(solution)/shard_map/all_gather | solution.py:68
  784.5 163.0 %all-gather.51.cloned.1.call-start = ((), (), s32[]{:S(2)}) async-start(), calls=%async_computation.37 | async-start | bytes 2985984 | tf_op jit(solution)/shard_map/all_gather | solution.py:43
  785.1 210.2 %reduce-scatter.27.cloned.1.call-start = ((), (), s32[]{:S(2)}) async-start(), calls=%async_computation.23 | async-start | bytes 2949120 | tf_op jit(solution)/shard_map/reduce_scatter | solution.py:62
  785.6 79.7 %copy-start.98 = (f32[1076]{0:T(1024)S(1)}, f32[1076]{0:T(1024)}, u32[]{:S(2)}) copy-start(f32[1076]{0:T(1024)} %get-tuple-element.881) | copy-start | bytes 12916
  963.5 68.8 %all-gather.39.cloned.1.call-start = ((), (), s32[]{:S(2)}) async-start(), calls=%async_computation.24 | async-start | bytes 2949120 | tf_op jit(solution)/shard_map/all_gather | solution.py:68
  1007.0 241.1 %reduce-scatter.29.cloned.1.call-start = ((), (), s32[]{:S(2)}) async-start(), calls=%async_computation.25 | async-start | bytes 2949120 | tf_op jit(solution)/shard_map/reduce_scatter | solution.py:62
  1179.9 28.2 %collective-permute-start.2 = (bf16[2,1024,288]{1,2,0:T(8,128)(2,1)S(1)}, bf16[2,1024,288]{1,2,0:T(8,128)(2,1)S(1)}, u32[]{:S(2)}, u32[]{:S(2)}) collective-permute-start(bf16[2,1024,288]{1,2,0:T(8,128)(2,1)S(1)} %pad_maximum_fusion.8), channel_id=1, source_target_pairs={{0,4},{4,0},{8,12},{12,8},{16,20},{20,16},{24,28},{28,24},{1,5},{5... | collective-permute-start | bytes 3538952 | tf_op jit(solution)/shard_map/ppermute | solution.py:24
  1214.8 68.9 %reduce-scatter.25.cloned.1.call-start = ((), (), s32[]{:S(2)}) async-start(), calls=%async_computation.21 | async-start | bytes 2949120 | tf_op jit(solution)/shard_map/reduce_scatter | solution.py:62
  1223.0 60.7 %copy-start.28 = (bf16[1024,288]{0,1:T(8,128)(2,1)S(1)}, bf16[1024,288]{0,1:T(8,128)(2,1)}, u32[]{:S(2)}) copy-start(bf16[1024,288]{0,1:T(8,128)(2,1)} %param.28) | copy-start | bytes 1769476
  1223.0 60.7 %copy-start.29 = (bf16[1024,288]{0,1:T(8,128)(2,1)S(1)}, bf16[1024,288]{0,1:T(8,128)(2,1)}, u32[]{:S(2)}) copy-start(bf16[1024,288]{0,1:T(8,128)(2,1)} %reduce-scatter.27.cloned.1.call-done) | copy-start | bytes 1769476
  1223.0 60.7 %copy-start.106 = (f32[288]{0:T(512)S(1)}, f32[288]{0:T(512)}, u32[]{:S(2)}) copy-start(f32[288]{0:T(512)} %get-tuple-element.882) | copy-start | bytes 3460
  1223.0 89.9 %all-gather.41.cloned.1.call-start = ((), (), s32[]{:S(2)}) async-start(), calls=%async_computation.26 | async-start | bytes 2949120 | tf_op jit(solution)/shard_map/all_gather | solution.py:68
  1288.6 35.2 %copy-start.114 = (bf16[1,1152,1076]{2,1,0:T(8,128)(2,1)S(1)}, bf16[1,1152,1076]{2,1,0:T(8,128)(2,1)}, u32[]{:S(2)}) copy-start(bf16[1,1152,1076]{2,1,0:T(8,128)(2,1)} %all-gather.45.cloned.1.call-done) | copy-start | bytes 7437316
  1288.7 72.9 %reduce-scatter.31.cloned.1.call-start = ((), (), s32[]{:S(2)}) async-start(), calls=%async_computation.27 | async-start | bytes 2949120 | tf_op jit(solution)/shard_map/reduce_scatter | solution.py:62
  1323.8 37.8 %copy-start.74 = (f32[1024]{0:T(1024)S(1)}, f32[1024]{0:T(1024)}, u32[]{:S(2)}) copy-start(f32[1024]{0:T(1024)} %copy-done.73) | copy-start | bytes 12292
  1323.8 37.8 %copy-start.82 = (f32[1024]{0:T(1024)S(1)}, f32[1024]{0:T(1024)}, u32[]{:S(2)}) copy-start(f32[1024]{0:T(1024)} %copy-done.81) | copy-start | bytes 12292
  1323.8 37.8 %copy-start.84 = (f32[288]{0:T(512)S(1)}, f32[288]{0:T(512)}, u32[]{:S(2)}) copy-start(f32[288]{0:T(512)} %copy-done.83) | copy-start | bytes 3460
  1328.3 33.3 %copy-start.3 = (bf16[1024,288]{0,1:T(8,128)(2,1)S(1)}, bf16[1024,288]{0,1:T(8,128)(2,1)}, u32[]{:S(2)}) copy-start(bf16[1024,288]{0,1:T(8,128)(2,1)} %param.26) | copy-start | bytes 1769476
  1328.3 33.3 %copy-start.9 = (bf16[1024,288]{0,1:T(8,128)(2,1)S(1)}, bf16[1024,288]{0,1:T(8,128)(2,1)}, u32[]{:S(2)}) copy-start(bf16[1024,288]{0,1:T(8,128)(2,1)} %reduce-scatter.19.cloned.1.call-done) | copy-start | bytes 1769476
  1328.3 33.3 %copy-start.76 = (f32[288]{0:T(512)S(1)}, f32[288]{0:T(512)}, u32[]{:S(2)}) copy-start(f32[288]{0:T(512)} %copy-done.75) | copy-start | bytes 3460
  1328.3 41.4 %copy-start.11 = (f32[1024,288]{0,1:T(8,128)S(1)}, f32[1024,288]{0,1:T(8,128)}, u32[]{:S(2)}) copy-start(f32[1024,288]{0,1:T(8,128)} %get-tuple-element.1002) | copy-start | bytes 3538948
  1328.4 84.2 %all-gather.43.cloned.1.call-start = ((), (), s32[]{:S(2)}) async-start(), calls=%async_computation.28 | async-start | bytes 2949120 | tf_op jit(solution)/shard_map/all_gather | solution.py:68
  1372.4 244.9 %reduce-scatter.45.cloned.1.call-start = ((), (), s32[]{:S(2)}) async-start(), calls=%async_computation.39 | async-start | bytes 5308416
  1390.8 228.7 %reduce-scatter.41.cloned.1.call-start = ((), (), s32[]{:S(2)}) async-start(), calls=%async_computation.33 | async-start | bytes 2985984 | tf_op jit(solution)/shard_map/reduce_scatter | solution.py:364
  1398.8 248.2 %reduce-scatter.39.cloned.1.call-start = ((), (), s32[]{:S(2)}) async-start(), calls=%async_computation.32 | async-start | bytes 2985984 | tf_op jit(solution)/shard_map/reduce_scatter | solution.py:364
  1406.9 304.2 %reduce-scatter.37.cloned.1.call-start = ((), (), s32[]{:S(2)}) async-start(), calls=%async_computation.31 | async-start | bytes 995328 | tf_op jit(solution)/shard_map/reduce_scatter | solution.py:361
  1412.4 362.7 %reduce-scatter.35.cloned.1.call-start = ((), (), s32[]{:S(2)}) async-start(), calls=%async_computation.30 | async-start | bytes 995328 | tf_op jit(solution)/shard_map/reduce_scatter | solution.py:361
  1556.1 31.8 %collective-permute-start.3 = (bf16[2,1024,288]{1,2,0:T(8,128)(2,1)}, bf16[2,1024,288]{1,2,0:T(8,128)(2,1)}, u32[]{:S(2)}, u32[]{:S(2)}) collective-permute-start(bf16[2,1024,288]{1,2,0:T(8,128)(2,1)} %pad_maximum_fusion.9), channel_id=1, source_target_pairs={{0,4},{4,0},{8,12},{12,8},{16,20},{20,16},{24,28},{28,24},{1,5},{5... | collective-permute-start | bytes 3538952 | tf_op jit(solution)/shard_map/ppermute | solution.py:24
  1561.7 248.2 %reduce-scatter.33.cloned.1.call-start = ((), (), s32[]{:S(2)}) async-start(), calls=%async_computation.29 | async-start | bytes 2949120 | tf_op jit(solution)/shard_map/reduce_scatter | solution.py:62
  1596.5 313.5 %reduce-scatter.43.cloned.1.call-start = ((), (), s32[]{:S(2)}) async-start(), calls=%async_computation.38 | async-start | bytes 5308416
  1617.2 192.6 %copy-start.70 = (f32[1024]{0:T(1024)S(1)}, f32[1024]{0:T(1024)}, u32[]{:S(2)}) copy-start(f32[1024]{0:T(1024)} %copy-done.69) | copy-start | bytes 12292
  1617.3 192.6 %copy-start.78 = (f32[1024]{0:T(1024)S(1)}, f32[1024]{0:T(1024)}, u32[]{:S(2)}) copy-start(f32[1024]{0:T(1024)} %copy-done.77) | copy-start | bytes 12292
  1617.3 192.6 %copy-start.90 = (f32[288]{0:T(512)S(1)}, f32[288]{0:T(512)}, u32[]{:S(2)}) copy-start(f32[288]{0:T(512)} %copy-done.89) | copy-start | bytes 3460
  1619.5 239.5 %copy-start.12 = (f32[1024,288]{0,1:T(8,128)S(1)}, f32[1024,288]{0,1:T(8,128)}, u32[]{:S(2)}) copy-start(f32[1024,288]{0,1:T(8,128)} %get-tuple-element.1002) | copy-start | bytes 3538948
  1619.5 239.5 %copy-start.24 = (bf16[1024,288]{0,1:T(8,128)(2,1)S(1)}, bf16[1024,288]{0,1:T(8,128)(2,1)}, u32[]{:S(2)}) copy-start(bf16[1024,288]{0,1:T(8,128)(2,1)} %reduce-scatter.31.cloned.1.call-done) | copy-start | bytes 1769476
  1862.1 51.7 %copy-start.16 = (bf16[144,1940]{0,1:T(8,128)(2,1)S(1)}, bf16[144,1940]{0,1:T(8,128)(2,1)}, u32[]{:S(2)}) copy-start(bf16[144,1940]{0,1:T(8,128)(2,1)} %copy.146) | copy-start | bytes 1676164
  (85 other events, 377.7 us)
Sparse Core Ops, SparseCore 0:
  9.6 27.1 all-gather.28
  273.9 33.2 reduce-scatter.18
  309.5 24.0 all-gather.30
  336.4 55.0 all-gather.44
  394.3 53.5 all-gather.46
  456.0 31.6 reduce-scatter.20
  490.1 24.0 all-gather.32
  747.9 33.2 reduce-scatter.22
  783.3 24.0 all-gather.34
  810.2 55.0 all-gather.48
  866.9 22.6 all-gather.36
  892.4 55.0 all-gather.50
  963.7 31.6 reduce-scatter.26
  1007.1 25.1 all-gather.38
  1214.9 33.0 reduce-scatter.28
  1250.6 33.0 reduce-scatter.24
  1288.8 24.0 all-gather.40
  1328.5 33.0 reduce-scatter.30
  1372.5 25.1 all-gather.42
  1401.6 95.4 reduce-scatter.44
  1501.2 72.7 reduce-scatter.40
  1577.7 69.2 reduce-scatter.38
  1650.8 60.3 reduce-scatter.36
  1714.8 60.2 reduce-scatter.34
  1777.8 31.9 reduce-scatter.32
  1813.3 96.6 reduce-scatter.42
where the time goes:
time: 1940 us; the launch traced here: 1930 us
  waiting for transfers between devices  823 us (42%)
  blocking collectives  372 us (19%)
  matrix products  366 us (19%)
  local copies, waits for them, and re-layouts  141 us (7%)
  loops' own time  105 us (5%)
  other arithmetic  95.3 us (5%)
    reduce_scatter x8, waiting for transfers between devices, column_sum(): lax.psum_scatter(partial_value.astype(jnp.bfloat16), 'hid', scatter_dimen...  247 us
    reduce_scatter x2, waiting for transfers between devices, body(): lax.psum_scatter(output_term.astype(jnp.bfloat16), 'tok', scatter_dimensi...  124 us
    all_gather x2, waiting for transfers between devices, fetch_layer(): lax.all_gather(up_part[layer_index], 'tok', axis=0, tiled=True)  110 us
    all_gather x2, waiting for transfers between devices, fetch_layer(): lax.all_gather(down_part[layer_index], 'tok', axis=1, tiled=True)  107 us
    all_gather x2, blocking collectives, fetch_layer(): lax.all_gather(output_part[layer_index], 'tok', axis=1, tiled=True)  99.2 us
    dot_general x32, matrix products, one_tile(): lax.dot_general(query_tile, key_tile, across, preferred_element_type=jnp....  67 us
    all_gather x4, waiting for transfers between devices, spread_rows(): return lax.all_gather(gradient, 'hid', axis=1, tiled=True)  65.8 us
    all_gather x2, blocking collectives, fetch_layer(): lax.all_gather(value_part[layer_index], 'tok', axis=0, tiled=True)  65.5 us
  transfers between devices with their start and end apart: 30, of which 23 were waited for; matrix products, arithmetic and copies ran while one was open for 13% of the time, Pallas kernels for 0%

commit v1 on v0

v1 whole, which is shorter than its diff:
```python
import functools

import jax
import jax.numpy as jnp
from jax import lax
from jax.experimental import pallas as pl
from jax.experimental.pallas import tpu as pltpu
from jax.sharding import PartitionSpec as P

HEAD_DIM = 72
LANES = 128
KEYS = 256
EPS = 1e-06
GELU = 0.7978845608028654
CUBE = 0.044715
MASKED = -1e30
LOG2E = 1.4426950408889634
LN2 = 0.6931471805599453
NN = (((1,), (0,)), ((), ()))
NT = (((1,), (1,)), ((), ()))
TN = (((0,), (0,)), ((), ()))
MESH = pl.DeviceIdType.MESH
BF = jnp.bfloat16
F32 = jnp.float32
VMEM_LIMIT = 60 * 1024 * 1024


def dot(left, right, dims=NN):
    return lax.dot_general(left, right, dims, preferred_element_type=F32)


def micros(duration):
    return pl.CostEstimate(flops=duration * 10**9, bytes_accessed=0, transcendentals=0)


def flat(value):
    return value.reshape(value.shape[0] * value.shape[1], value.shape[2])


class Net:
    def __init__(self, send_sems, recv_sems):
        tok, hid = lax.axis_index("tok"), lax.axis_index("hid")
        near = hid + 1 - 2 * lax.rem(hid, 2)
        self.tok, self.hid = tok, hid
        self.core = (tok, near)
        self.far = (tok, lax.rem(hid + 2, 4))
        self.far_core = (tok, lax.rem(near + 2, 4))
        self.half = (tok + 1 - 2 * lax.rem(tok, 2), hid)
        self.low, self.high = lax.rem(tok, 2), lax.div(tok, 2)
        self.send_sems, self.recv_sems = send_sems, recv_sems
        self.copies = []

    def row(self, high):
        return (high * 2 + self.low, self.hid)

    def rows(self, count):
        return [self.row(lax.rem(self.high + step, count)) for step in range(1, count)]

    def barrier(self, devices):
        sem = pltpu.get_barrier_semaphore()
        for device in devices:
            pl.semaphore_signal(sem, inc=1, device_id=device, device_id_type=MESH)
        pl.semaphore_wait(sem, len(devices))

    def copy(self, source, target, device):
        index = len(self.copies)
        made = pltpu.make_async_remote_copy(
            src_ref=source,
            dst_ref=target,
            send_sem=self.send_sems.at[index],
            recv_sem=self.recv_sems.at[index],
            device_id=device,
            device_id_type=MESH,
        )
        self.copies.append(made)
        made.start()
        return made

    def finish(self, waited=()):
        done = [id(made) for made in waited]
        for made in self.copies:
            if id(made) not in done:
                made.wait_send()


def norm_parts(rows):
    centred = rows - jnp.mean(rows, axis=1, keepdims=True)
    inverse = lax.rsqrt(jnp.mean(centred * centred, axis=1, keepdims=True) + EPS)
    return centred * inverse, inverse


def norm_back(rows, gain, grad):
    scaled, inverse = norm_parts(rows)
    inner = grad * gain
    first = jnp.mean(inner, axis=1, keepdims=True)
    second = jnp.mean(inner * scaled, axis=1, keepdims=True)
    return (
        inverse * (inner - first - scaled * second),
        jnp.sum(grad * scaled, axis=0, keepdims=True),
        jnp.sum(grad, axis=0, keepdims=True),
    )


def gather_send(net, full, chunk):
    near = net.copy(full.at[0, chunk], full.at[1, chunk], net.core)
    far = net.copy(full.at[0, chunk], full.at[2, chunk], net.far)
    return near, far


def gather_pass(net, full, chunk, far):
    far.wait_recv()
    return net.copy(full.at[2, chunk], full.at[3, chunk], net.core)


def scatter_scratch(rows, width, chunks):
    return [
        pltpu.VMEM((rows, width), F32),
        pltpu.VMEM((rows, width), F32),
    ] + [pltpu.VMEM((rows, width), BF)] * 6


class Scatter:
    def __init__(self, net, scratch):
        self.net = net
        self.hold, self.total, self.cs0, self.cr0, self.ys, self.yr, self.cs1, self.cr1 = scratch
        self.first, self.second = {}, {}

    def far_part(self, key, chunk, partial):
        rows = partial.shape[0] // 2
        self.hold[chunk] = partial[:rows]
        self.cs0[chunk] = partial[rows:].astype(BF)
        self.first[key] = self.net.copy(self.cs0.at[chunk], self.cr0.at[chunk], self.net.core)

    def far_send(self, key, chunk):
        self.first[key].wait_recv()
        self.ys[chunk] = (self.hold[chunk] + self.cr0[chunk].astype(F32)).astype(BF)
        self.second[key] = self.net.copy(self.ys.at[chunk], self.yr.at[chunk], self.net.far)

    def near_part(self, partial):
        rows = partial.shape[0] // 2
        self.total[...] = partial[:rows]
        self.cs1[...] = partial[rows:].astype(BF)
        self.near = self.net.copy(self.cs1, self.cr1, self.net.core)

    def near_done(self):
        self.near.wait_recv()
        self.total[...] += self.cr1[...].astype(F32)

    def result(self, key, chunk):
        self.second[key].wait_recv()
        return self.total[chunk] + self.yr[chunk].astype(F32)


def chunks_of(rows, count):
    step = rows // count
    return [pl.ds(index * step, step) for index in range(count)]


def weight_grad(left, right, out):
    width = left.shape[2]
    tile = 384

    def one(index, carry):
        columns = pl.ds(pl.multiple_of(index * tile, tile), tile)
        out[columns, :] = dot(flat(left[:, :, columns]), flat(right[...]), TN).astype(out.dtype)
        return carry

    lax.fori_loop(0, width // tile, one, 0)


def project_kernel(
    x, vec, weight, bias, normed, queries, pairs, far_pairs, send_sems, recv_sems, *, factor
):
    net = Net(send_sems, recv_sems)
    rows, width = x.shape
    pair_cols = pairs.shape[2]
    all_cols = pair_cols + queries.shape[2]
    parts = chunks_of(rows, 2)
    net.barrier([net.core, net.far, net.half])
    scaled, _ = norm_parts(x[...])
    normed[0] = (scaled * vec[0:1] + vec[1:2]).astype(BF)
    sent = [gather_send(net, normed, chunk) for chunk in parts]
    arrived = []

    def project(slot):
        result = dot(normed[slot], weight[:, :all_cols]) + bias[...]
        pairs[slot] = result[:, :pair_cols].astype(BF)
        queries[slot] = (result[:, pair_cols:] * factor).astype(BF)
        arrived.append(net.copy(pairs.at[slot], far_pairs.at[slot], net.half))

    project(0)
    for near, _ in sent:
        near.wait_recv()
    project(1)
    passed = [gather_pass(net, normed, chunk, far) for chunk, (_, far) in zip(parts, sent)]
    project(2)
    for one in passed:
        one.wait_recv()
    project(3)
    for one in arrived:
        one.wait_recv()
    net.finish()


def project(x, vec, weight, bias, head_cols):
    rows, width = x.shape
    shapes = [
        jax.ShapeDtypeStruct((4, rows, width), BF),
        jax.ShapeDtypeStruct((4, rows, head_cols), BF),
        jax.ShapeDtypeStruct((4, rows, 2 * head_cols), BF),
        jax.ShapeDtypeStruct((4, rows, 2 * head_cols), BF),
    ]
    space = pl.BlockSpec(memory_space=pltpu.VMEM)
    return pl.pallas_call(
        functools.partial(project_kernel, factor=HEAD_DIM ** (-0.5) * LOG2E),
        name="project",
        cost_estimate=micros(44),
        out_shape=shapes,
        in_specs=[space] * 4,
        out_specs=[space] * 4,
        scratch_shapes=[pltpu.SemaphoreType.DMA((12,)), pltpu.SemaphoreType.DMA((12,))],
        compiler_params=pltpu.CompilerParams(
            collective_id=0, has_side_effects=True, vmem_limit_bytes=VMEM_LIMIT
        ),
    )(x, vec, weight, bias)


def head_pick(width, head):
    row = lax.broadcasted_iota(jnp.int32, (width, LANES), 0)
    lane = lax.broadcasted_iota(jnp.int32, (width, LANES), 1)
    return ((row == lane + head * HEAD_DIM) & (lane < HEAD_DIM)).astype(BF)


def as_rows(columns):
    rows = columns[0].shape[0]
    lane = lax.broadcasted_iota(jnp.int32, (rows, LANES), 1)
    together = jnp.zeros((rows, LANES), F32)
    for head, column in enumerate(columns):
        together = jnp.where(lane == head, column, together)
    return together.T[:8]


def load_pairs(meta, own_pairs, far_pairs, key_scratch, value_scratch, heads):
    rows = own_pairs.shape[1]
    head_cols = heads * HEAD_DIM
    hid, half = meta[0], meta[1]
    for which, source in ((0, own_pairs), (1, far_pairs)):
        for slot in range(4):
            block = jnp.bitwise_xor(hid, slot)
            place = jnp.bitwise_xor(half, which) * 4 + block
            start = pl.ds(pl.multiple_of(place * rows, rows), rows)
            both = source[slot]
            for head in range(heads):
                key = dot(both, head_pick(2 * head_cols, head))
                key_scratch[head, start, :] = key.astype(BF)
                value = dot(both, head_pick(2 * head_cols, head + heads))
                value_scratch[head, start, :] = value.astype(BF)


def attend_kernel(
    meta, queries, own_pairs, far_pairs, query_ids, key_ids, mixture, logsum,
    key_scratch, value_scratch, score_scratch, high_scratch, total_scratch, sum_scratch, query_scratch,
    *, heads
):
    rows = queries.shape[1]
    head_cols = heads * HEAD_DIM
    load_pairs(meta, own_pairs, far_pairs, key_scratch, value_scratch, heads)

    def one_block(block, carry):
        slot = jnp.bitwise_xor(meta[0], block)
        first, last = meta[2 + 2 * block], meta[3 + 2 * block]
        own = pl.ds(pl.multiple_of(block * rows, rows), rows)
        ids = query_ids[own, :]
        for head in range(heads):
            query_scratch[head] = dot(queries[slot], head_pick(head_cols, head)).astype(BF)
        high_scratch[...] = jnp.full_like(high_scratch, -3e38)
        sum_scratch[...] = jnp.zeros_like(sum_scratch)
        total_scratch[...] = jnp.zeros_like(total_scratch)

        def scores_of(key_block, inner):
            keys = pl.ds(pl.multiple_of(key_block * KEYS, KEYS), KEYS)
            same = ids == key_ids[:, keys]
            for head in range(heads):
                scores = dot(query_scratch[head], key_scratch[head, keys, :], NT)
                scores = jnp.where(same, scores, MASKED)
                score_scratch[head, :, keys] = scores
                high = high_scratch[head]
                for lane in range(0, KEYS, LANES):
                    high = jnp.maximum(high, scores[:, lane : lane + LANES])
                high_scratch[head] = high
            return inner

        lax.fori_loop(first, last, scores_of, 0)
        for head in range(heads):
            high_scratch[head] = jnp.broadcast_to(
                jnp.max(high_scratch[head], axis=1, keepdims=True), (rows, LANES)
            )

        def sums_of(key_block, inner):
            keys = pl.ds(pl.multiple_of(key_block * KEYS, KEYS), KEYS)
            for head in range(heads):
                high = high_scratch[head]
                high = jnp.concatenate([high] * (KEYS // LANES), axis=1)
                powers = jnp.exp2(score_scratch[head, :, keys] - high)
                total = total_scratch[head]
                for lane in range(0, KEYS, LANES):
                    total += powers[:, lane : lane + LANES]
                total_scratch[head] = total
                sum_scratch[head] += dot(powers.astype(BF), value_scratch[head, keys, :])
            return inner

        lax.fori_loop(first, last, sums_of, 0)
        result = jnp.zeros((rows, head_cols), F32)
        columns = []
        for head in range(heads):
            sums = sum_scratch[head]
            total = jnp.sum(total_scratch[head], axis=1, keepdims=True)
            columns.append(high_scratch[head][:, :1] + jnp.log2(total))
            mixed = (sums / total).astype(BF)
            result += dot(mixed, head_pick(head_cols, head), NT)
        mixture[slot] = result.astype(BF)
        logsum[:, own] = as_rows(columns)
        return carry

    lax.fori_loop(0, 4, one_block, 0)


def attend(meta, queries, own_pairs, far_pairs, query_ids, key_ids):
    _, rows, head_cols = queries.shape
    heads = head_cols // HEAD_DIM
    own, count = 4 * rows, 8 * rows
    space = pl.BlockSpec(memory_space=pltpu.VMEM)
    return pl.pallas_call(
        functools.partial(attend_kernel, heads=heads),
        name="attend",
        cost_estimate=micros(22),
        out_shape=[
            jax.ShapeDtypeStruct((4, rows, head_cols), BF),
            jax.ShapeDtypeStruct((8, own), F32),
        ],
        in_specs=[pl.BlockSpec(memory_space=pltpu.SMEM)] + [space] * 5,
        out_specs=[space] * 2,
        scratch_shapes=[
            pltpu.VMEM((heads, count, LANES), BF),
            pltpu.VMEM((heads, count, LANES), BF),
            pltpu.VMEM((heads, rows, count), F32),
            pltpu.VMEM((heads, rows, LANES), F32),
            pltpu.VMEM((heads, rows, LANES), F32),
            pltpu.VMEM((heads, rows, LANES), F32),
            pltpu.VMEM((heads, rows, LANES), BF),
        ],
        compiler_params=pltpu.CompilerParams(vmem_limit_bytes=VMEM_LIMIT),
    )(meta, queries, own_pairs, far_pairs, query_ids, key_ids)


def attend_back_kernel(
    meta, queries, own_pairs, far_pairs, query_ids, key_ids, grad_mixture, logsum,
    grad_queries, grad_own, grad_far,
    key_scratch, value_scratch, grad_key, grad_value, grad_query, query_scratch, grad_scratch,
    prob_scratch, grad_prob_scratch, delta_scratch,
    *, heads
):
    rows = queries.shape[1]
    head_cols = heads * HEAD_DIM
    load_pairs(meta, own_pairs, far_pairs, key_scratch, value_scratch, heads)
    grad_key[...] = jnp.zeros_like(grad_key)
    grad_value[...] = jnp.zeros_like(grad_value)

    def one_block(block, carry):
        slot = jnp.bitwise_xor(meta[0], block)
        first, last = meta[2 + 2 * block], meta[3 + 2 * block]
        own = pl.ds(pl.multiple_of(block * rows, rows), rows)
        ids = query_ids[:, own]
        for head in range(heads):
            pick = head_pick(head_cols, head)
            query_scratch[head] = dot(queries[slot], pick).astype(BF)
            grad_scratch[head] = dot(grad_mixture[slot], pick).astype(BF)
        logs = logsum[:, own]
        grad_query[...] = jnp.zeros_like(grad_query)
        delta_scratch[...] = jnp.zeros_like(delta_scratch)

        def probs_of(key_block, inner):
            keys = pl.ds(pl.multiple_of(key_block * KEYS, KEYS), KEYS)
            same = key_ids[keys, :] == ids
            for head in range(heads):
                grad = grad_scratch[head]
                scores = dot(key_scratch[head, keys, :], query_scratch[head], NT)
                probs = jnp.where(same, jnp.exp2(scores - logs[head : head + 1]), 0.0)
                grad_probs = dot(value_scratch[head, keys, :], grad, NT)
                prob_scratch[head, keys, :] = probs
                grad_prob_scratch[head, keys, :] = grad_probs
                delta_scratch[head] += jnp.sum((probs * grad_probs).reshape(KEYS // 8, 8, rows), axis=0)
                grad_value[head, keys, :] += dot(probs.astype(BF), grad)
            return inner

        lax.fori_loop(first, last, probs_of, 0)
        for head in range(heads):
            delta_scratch[head, 0:1] = jnp.sum(delta_scratch[head], axis=0, keepdims=True)

        def one_key(key_block, inner):
            keys = pl.ds(pl.multiple_of(key_block * KEYS, KEYS), KEYS)
            for head in range(heads):
                delta = delta_scratch[head, 0:1]
                grad_scores = prob_scratch[head, keys, :] * (grad_prob_scratch[head, keys, :] - delta)
                grad_scores = grad_scores.astype(BF)
                grad_key[head, keys, :] += dot(grad_scores, query_scratch[head])
                grad_query[head] += dot(grad_scores, key_scratch[head, keys, :], TN)
            return inner

        lax.fori_loop(first, last, one_key, 0)
        result = jnp.zeros((rows, head_cols), F32)
        for head in range(heads):
            scaled = (grad_query[head] * HEAD_DIM ** (-0.5)).astype(BF)
            result += dot(scaled, head_pick(head_cols, head), NT)
        grad_queries[slot] = result.astype(BF)
        return carry

    lax.fori_loop(0, 4, one_block, 0)
    hid, half = meta[0], meta[1]
    for which, target in ((0, grad_own), (1, grad_far)):
        for slot in range(4):
            place = jnp.bitwise_xor(half, which) * 4 + jnp.bitwise_xor(hid, slot)
            start = pl.ds(pl.multiple_of(place * rows, rows), rows)
            keys = jnp.zeros((rows, head_cols), F32)
            values = jnp.zeros((rows, head_cols), F32)
            for head in range(heads):
                pick = head_pick(head_cols, head)
                keys += dot((grad_key[head, start, :] * LN2).astype(BF), pick, NT)
                values += dot(grad_value[head, start, :].astype(BF), pick, NT)
            target[slot, :, :head_cols] = keys.astype(BF)
            target[slot, :, head_cols:] = values.astype(BF)


def attend_back(meta, queries, own_pairs, far_pairs, query_ids, key_ids, grad_mixture, logsum):
    _, rows, head_cols = queries.shape
    heads = head_cols // HEAD_DIM
    count = 8 * rows
    space = pl.BlockSpec(memory_space=pltpu.VMEM)
    return pl.pallas_call(
        functools.partial(attend_back_kernel, heads=heads),
        name="attend_back",
        cost_estimate=micros(37),
        out_shape=[
            jax.ShapeDtypeStruct((4, rows, head_cols), BF),
            jax.ShapeDtypeStruct((4, rows, 2 * head_cols), BF),
            jax.ShapeDtypeStruct((4, rows, 2 * head_cols), BF),
        ],
        in_specs=[pl.BlockSpec(memory_space=pltpu.SMEM)] + [space] * 7,
        out_specs=[space] * 3,
        scratch_shapes=[
            pltpu.VMEM((heads, count, LANES), BF),
            pltpu.VMEM((heads, count, LANES), BF),
            pltpu.VMEM((heads, count, LANES), F32),
            pltpu.VMEM((heads, count, LANES), F32),
            pltpu.VMEM((heads, rows, LANES), F32),
            pltpu.VMEM((heads, rows, LANES), BF),
            pltpu.VMEM((heads, rows, LANES), BF),
            pltpu.VMEM((heads, count, rows), F32),
            pltpu.VMEM((heads, count, rows), F32),
            pltpu.VMEM((heads, 8, rows), F32),
        ],
        compiler_params=pltpu.CompilerParams(vmem_limit_bytes=VMEM_LIMIT),
    )(meta, queries, own_pairs, far_pairs, query_ids, key_ids, grad_mixture, logsum)


def mlp_kernel(
    mixture, x, vec, out_weight, up_weight, up_bias, down_weight,
    x_next, after, normed, active, slope, *scratch
):
    net = Net(*scratch[16:])
    rows = x.shape[0]
    parts = chunks_of(rows, 2)
    net.barrier([net.core, net.far])
    out_bias, gain, shift, down_bias = vec[2:3], vec[3:4], vec[4:5], vec[5:6]

    def mixed(slots, chunk):
        return dot(flat(mixture[slots, chunk, :]), out_weight[...], NT)

    def up(slots, chunk):
        hidden = dot(flat(normed[slots, chunk, :]), up_weight[...]) + up_bias[...]
        square = hidden * hidden
        bend = jnp.tanh(GELU * hidden * (1.0 + CUBE * square))
        half = 0.5 * (1.0 + bend)
        value = hidden * half
        rise = half + 0.5 * hidden * (1.0 - bend * bend) * GELU * (1.0 + 3.0 * CUBE * square)
        shape = (2, hidden.shape[0] // 2, hidden.shape[1])
        active[slots, chunk, :] = value.astype(BF).reshape(shape)
        slope[slots, chunk, :] = rise.astype(BF).reshape(shape)

    def down(slots, chunk):
        return dot(flat(active[slots, chunk, :]), down_weight[...], NT)

    near, far, whole = pl.ds(0, 2), pl.ds(2, 2), pl.ds(0, rows)
    first = Scatter(net, scratch[0:8])
    for key, chunk in enumerate(parts):
        first.far_part(key, chunk, mixed(far, chunk))
    for key, chunk in enumerate(parts):
        first.far_send(key, chunk)
    first.near_part(mixed(near, whole))
    first.near_done()
    sent = []
    for key, chunk in enumerate(parts):
        residual = first.result(key, chunk) + x[chunk, :] + out_bias
        after[chunk, :] = residual
        normed[0, chunk, :] = (norm_parts(residual)[0] * gain + shift).astype(BF)
        sent.append(gather_send(net, normed, chunk))
    for one, _ in sent:
        one.wait_recv()
    up(near, whole)
    second = Scatter(net, scratch[8:16])
    for key, chunk in enumerate(parts):
        passed = gather_pass(net, normed, chunk, sent[key][1])
        passed.wait_recv()
        up(far, chunk)
        second.far_part(key, chunk, down(far, chunk))
        second.far_send(key, chunk)
    second.near_part(down(near, whole))
    second.near_done()
    for key, chunk in enumerate(parts):
        x_next[chunk, :] = second.result(key, chunk) + after[chunk, :] + down_bias
    net.finish()


def mlp(mixture, x, vec, out_weight, up_weight, up_bias, down_weight):
    rows, width = x.shape
    hidden = up_weight.shape[1]
    space = pl.BlockSpec(memory_space=pltpu.VMEM)
    return pl.pallas_call(
        mlp_kernel,
        name="mlp",
        cost_estimate=micros(51),
        out_shape=[
            jax.ShapeDtypeStruct((rows, width), F32),
            jax.ShapeDtypeStruct((rows, width), F32),
            jax.ShapeDtypeStruct((4, rows, width), BF),
            jax.ShapeDtypeStruct((4, rows, hidden), BF),
            jax.ShapeDtypeStruct((4, rows, hidden), BF),
        ],
        in_specs=[space] * 7,
        out_specs=[space] * 5,
        scratch_shapes=scatter_scratch(rows, width, 2) * 2
        + [pltpu.SemaphoreType.DMA((16,)), pltpu.SemaphoreType.DMA((16,))],
        compiler_params=pltpu.CompilerParams(
            collective_id=1, has_side_effects=True, vmem_limit_bytes=VMEM_LIMIT
        ),
    )(mixture, x, vec, out_weight, up_weight, up_bias, down_weight)


def mlp_back_kernel(
    gradient, after, vec, out_weight, up_weight, down_weight, mixture, normed, active, slope,
    grad_after, grad_mixture, grad_down, grad_up, grad_out, sums, hidden_sums, *scratch
):
    net = Net(*scratch[11:])
    grad_rows, grad_hidden, grad_mid = scratch[8:11]
    rows, width = gradient.shape
    parts = chunks_of(rows, 2)
    net.barrier([net.core, net.far])
    gain = vec[3:4]
    near, far, whole = pl.ds(0, 2), pl.ds(2, 2), pl.ds(0, rows)
    rounded = gradient[...].astype(BF)
    grad_rows[0] = rounded
    sent = [gather_send(net, grad_rows, chunk) for chunk in parts]
    sums[...] = jnp.zeros_like(sums)
    sums[5:6] = jnp.sum(rounded.astype(F32), axis=0, keepdims=True)

    def hidden_grad(slots, chunk):
        value = dot(flat(grad_rows[slots, chunk, :]), down_weight[...])
        value = value * flat(slope[slots, chunk, :]).astype(F32)
        shape = (2, value.shape[0] // 2, value.shape[1])
        grad_hidden[slots, chunk, :] = value.astype(BF).reshape(shape)

    def up_back(slots, chunk):
        return dot(flat(grad_hidden[slots, chunk, :]), up_weight[...], NT)

    for one, _ in sent:
        one.wait_recv()
    hidden_grad(near, whole)
    scatter = Scatter(net, scratch[0:8])
    for key, chunk in enumerate(parts):
        passed = gather_pass(net, grad_rows, chunk, sent[key][1])
        passed.wait_recv()
        hidden_grad(far, chunk)
        scatter.far_part(key, chunk, up_back(far, chunk))
        scatter.far_send(key, chunk)
    scatter.near_part(up_back(near, whole))
    weight_grad(grad_rows, active, grad_down)
    scatter.near_done()
    sent = []
    for key, chunk in enumerate(parts):
        back, gain_sum, shift_sum = norm_back(after[chunk, :], gain, scatter.result(key, chunk))
        total = gradient[chunk, :] + back
        grad_after[chunk, :] = total
        rounded = total.astype(BF)
        grad_mid[0, chunk, :] = rounded
        sent.append(gather_send(net, grad_mid, chunk))
        sums[3:4] += gain_sum
        sums[4:5] += shift_sum
        sums[2:3] += jnp.sum(rounded.astype(F32), axis=0, keepdims=True)
    weight_grad(normed, grad_hidden, grad_up)
    column = jnp.zeros((1, hidden_sums.shape[1]), F32)
    for slot in range(4):
        column += jnp.sum(grad_hidden[slot].astype(F32), axis=0, keepdims=True)
    hidden_sums[...] = column

    def mix_back(slots, chunk):
        value = dot(flat(grad_mid[slots, chunk, :]), out_weight[...])
        shape = (2, value.shape[0] // 2, value.shape[1])
        grad_mixture[slots, chunk, :] = value.astype(BF).reshape(shape)

    for one, _ in sent:
        one.wait_recv()
    mix_back(near, whole)
    for key, chunk in enumerate(parts):
        gather_pass(net, grad_mid, chunk, sent[key][1]).wait_recv()
    mix_back(far, whole)
    weight_grad(grad_mid, mixture, grad_out)
    net.finish()


def mlp_back(
    gradient, after, vec, out_weight, up_weight, down_weight, mixture, normed, active, slope
):
    rows, width = gradient.shape
    hidden = up_weight.shape[1]
    head_cols = out_weight.shape[1]
    space = pl.BlockSpec(memory_space=pltpu.VMEM)
    return pl.pallas_call(
        mlp_back_kernel,
        name="mlp_back",
        cost_estimate=micros(54),
        out_shape=[
            jax.ShapeDtypeStruct((rows, width), F32),
            jax.ShapeDtypeStruct((4, rows, head_cols), BF),
            jax.ShapeDtypeStruct((width, hidden), BF),
            jax.ShapeDtypeStruct((width, hidden), BF),
            jax.ShapeDtypeStruct((width, head_cols), BF),
            jax.ShapeDtypeStruct((8, width), F32),
            jax.ShapeDtypeStruct((1, hidden), F32),
        ],
        in_specs=[space] * 10,
        out_specs=[space] * 7,
        scratch_shapes=scatter_scratch(rows, width, 2)
        + [
            pltpu.VMEM((4, rows, width), BF),
            pltpu.VMEM((4, rows, hidden), BF),
            pltpu.VMEM((4, rows, width), BF),
            pltpu.SemaphoreType.DMA((20,)),
            pltpu.SemaphoreType.DMA((20,)),
        ],
        compiler_params=pltpu.CompilerParams(
            collective_id=2, has_side_effects=True, vmem_limit_bytes=VMEM_LIMIT
        ),
    )(gradient, after, vec, out_weight, up_weight, down_weight, mixture, normed, active, slope)


def project_back_kernel(
    grad_after, x, vec, weight, normed, grad_queries, grad_own, grad_far,
    gradient, grad_weight, sums, column_sums, *scratch
):
    net = Net(*scratch[10:])
    landed, together = scratch[8:10]
    rows, width = x.shape
    pair_cols = grad_own.shape[2]
    all_cols = together.shape[2]
    parts = chunks_of(rows, 2)
    near, far, whole = pl.ds(0, 2), pl.ds(2, 2), pl.ds(0, rows)
    net.barrier([net.core, net.far, net.half])
    arriving = {
        slot: net.copy(grad_far.at[slot], landed.at[slot], net.half) for slot in (3, 2, 1, 0)
    }
    together[:, :, pair_cols:] = grad_queries[...]

    def join(slot):
        arriving[slot].wait_recv()
        pair = grad_own[slot].astype(F32) + landed[slot].astype(F32)
        together[slot, :, :pair_cols] = pair.astype(BF)

    def back(slots, chunk):
        return dot(flat(together[slots, chunk, :]), weight[:, :all_cols], NT)

    scatter = Scatter(net, scratch[0:8])
    join(3)
    join(2)
    for key, chunk in enumerate(parts):
        scatter.far_part(key, chunk, back(far, chunk))
    for key, chunk in enumerate(parts):
        scatter.far_send(key, chunk)
    join(1)
    join(0)
    scatter.near_part(back(near, whole))
    weight_grad(normed, together, grad_weight)
    column = jnp.zeros((1, all_cols), F32)
    for slot in range(4):
        column += jnp.sum(together[slot].astype(F32), axis=0, keepdims=True)
    column_sums[...] = column
    scatter.near_done()
    sums[...] = jnp.zeros_like(sums)
    for key, chunk in enumerate(parts):
        grad, gain_sum, shift_sum = norm_back(x[chunk, :], vec[0:1], scatter.result(key, chunk))
        gradient[chunk, :] = grad_after[chunk, :] + grad
        sums[0:1] += gain_sum
        sums[1:2] += shift_sum
    net.finish()


def project_back(grad_after, x, vec, weight, normed, grad_queries, grad_own, grad_far):
    rows, width = x.shape
    all_cols = grad_queries.shape[2] + grad_own.shape[2]
    space = pl.BlockSpec(memory_space=pltpu.VMEM)
    return pl.pallas_call(
        project_back_kernel,
        name="project_back",
        cost_estimate=micros(44),
        out_shape=[
            jax.ShapeDtypeStruct((rows, width), F32),
            jax.ShapeDtypeStruct((width, all_cols), BF),
            jax.ShapeDtypeStruct((8, width), F32),
            jax.ShapeDtypeStruct((1, all_cols), F32),
        ],
        in_specs=[space] * 8,
        out_specs=[space] * 4,
        scratch_shapes=scatter_scratch(rows, width, 2)
        + [
            pltpu.VMEM(grad_far.shape, BF),
            pltpu.VMEM((4, rows, all_cols), BF),
            pltpu.SemaphoreType.DMA((12,)),
            pltpu.SemaphoreType.DMA((12,)),
        ],
        compiler_params=pltpu.CompilerParams(
            collective_id=3, has_side_effects=True, vmem_limit_bytes=VMEM_LIMIT
        ),
    )(grad_after, x, vec, weight, normed, grad_queries, grad_own, grad_far)


def entry_kernel(
    tokens, cotangent, vectors, shard, tokens_out, cotangent_out, vectors_out, weights,
    send_sems, recv_sems, local_sem,
):
    net = Net(send_sems, recv_sems)
    count = weights.shape[0] // 2
    others = [net.core, net.far, net.far_core]
    net.barrier(others + [net.half] + net.rows(count))
    mine = net.tok
    local = pltpu.make_async_copy(shard, weights.at[mine], local_sem)
    local.start()
    along = [net.copy(shard, weights.at[mine], device) for device in net.rows(count)]
    across = [net.copy(shard, weights.at[mine], net.half)]
    moved = []
    for source, target in ((tokens, tokens_out), (cotangent, cotangent_out)):
        for device in reversed(others):
            moved.append(net.copy(source.at[device[1]], target.at[net.hid], device))
        target[net.hid] = source[net.hid]
    for device in others:
        moved.append(net.copy(vectors, vectors_out.at[net.hid], device))
    vectors_out[net.hid] = vectors[...]
    for step, one in enumerate(along):
        one.wait_recv()
        place = lax.rem(net.high + count - step - 1, count) * 2 + net.low
        across.append(net.copy(weights.at[place], weights.at[place], net.half))
    for one in across + moved:
        one.wait_recv()
    local.wait()
    net.finish()


def entry(tokens, cotangent, vectors, shard, count):
    space = pl.BlockSpec(memory_space=pltpu.VMEM)
    whole = pl.BlockSpec(memory_space=pl.ANY)
    copies = 9 + count
    return pl.pallas_call(
        entry_kernel,
        name="entry",
        cost_estimate=micros(40),
        out_shape=[
            jax.ShapeDtypeStruct(tokens.shape, BF),
            jax.ShapeDtypeStruct(cotangent.shape, BF),
            jax.ShapeDtypeStruct((4,) + vectors.shape, F32),
            jax.ShapeDtypeStruct((count,) + shard.shape, BF),
        ],
        in_specs=[space] * 3 + [whole],
        out_specs=[space] * 3 + [whole],
        scratch_shapes=[
            pltpu.SemaphoreType.DMA((copies,)),
            pltpu.SemaphoreType.DMA((copies,)),
            pltpu.SemaphoreType.DMA(()),
        ],
        compiler_params=pltpu.CompilerParams(
            collective_id=4, has_side_effects=True, vmem_limit_bytes=VMEM_LIMIT
        ),
    )(tokens, cotangent, vectors, shard)


def finish_kernel(
    final, gradient, wide, narrow, grads, final_out, gradient_out, sums, total,
    wide_land, across_land, along_land, landed, passing, arrived, send_sems, recv_sems,
):
    net = Net(send_sems, recv_sems)
    count = grads.shape[0] // 2
    others = [net.core, net.far, net.far_core]
    net.barrier(others + [net.half] + net.rows(count))
    steps = list(range(1, count)) + [0]
    place = {step: lax.rem(net.high + step, count) for step in steps}
    summed = [net.copy(wide.at[device[1]], wide_land.at[net.hid], device) for device in others]
    across = {}
    for step in steps:
        source = grads.at[place[step] * 2 + 1 - net.low]
        across[step] = net.copy(source, landed.at[place[step]], net.half)
    moved = []
    for source, target in ((final, final_out), (gradient, gradient_out)):
        for device in reversed(others):
            moved.append(net.copy(source.at[device[1]], target.at[net.hid], device))
        target[net.hid] = source[net.hid]
    wide_land[net.hid] = wide[net.hid]
    for one in summed:
        one.wait_recv()
    top = wide.shape[1]
    sums[:top] = wide_land[0] + wide_land[1] + wide_land[2] + wide_land[3]
    sums[top:] = narrow[...]
    swap = net.copy(sums, across_land, net.half)
    swap.wait()
    sums[...] += across_land[...]
    spread = [
        net.copy(sums, along_land.at[step], device)
        for step, device in enumerate(net.rows(count))
    ]
    along = []
    for step in steps[:-1]:
        across[step].wait_recv()
        mine = grads[place[step] * 2 + net.low].astype(F32)
        passing[step] = (mine + landed[place[step]].astype(F32)).astype(BF)
        along.append(net.copy(passing.at[step], arrived.at[step], net.row(place[step])))
    across[0].wait_recv()
    total[...] = grads[net.tok].astype(F32) + landed[net.high].astype(F32)
    for step, one in enumerate(spread):
        one.wait()
    reduced = sums[...]
    for step in range(count - 1):
        reduced += along_land[step]
    sums[...] = reduced
    for step, one in zip(steps, along):
        one.wait_recv()
        total[...] += arrived[step].astype(F32)
    for one in moved:
        one.wait_recv()
    net.finish([swap] + spread)


def finish(final, gradient, wide, narrow, grads):
    count, shard, width = grads.shape
    count = count // 2
    space = pl.BlockSpec(memory_space=pltpu.VMEM)
    sum_rows = wide.shape[1] + narrow.shape[0]
    copies = 10 + 3 * count
    return pl.pallas_call(
        finish_kernel,
        name="finish",
        cost_estimate=micros(40),
        out_shape=[
            jax.ShapeDtypeStruct(final.shape, BF),
            jax.ShapeDtypeStruct(gradient.shape, BF),
            jax.ShapeDtypeStruct((sum_rows, wide.shape[2]), F32),
            jax.ShapeDtypeStruct((shard, width), F32),
        ],
        in_specs=[space] * 5,
        out_specs=[space] * 4,
        scratch_shapes=[
            pltpu.VMEM(wide.shape, F32),
            pltpu.VMEM((sum_rows, wide.shape[2]), F32),
            pltpu.VMEM((count, sum_rows, wide.shape[2]), F32),
            pltpu.VMEM((count, shard, width), BF),
            pltpu.VMEM((count, shard, width), BF),
            pltpu.VMEM((count, shard, width), BF),
            pltpu.SemaphoreType.DMA((copies,)),
            pltpu.SemaphoreType.DMA((copies,)),
        ],
        compiler_params=pltpu.CompilerParams(
            collective_id=5, has_side_effects=True, vmem_limit_bytes=VMEM_LIMIT
        ),
    )(final, gradient, wide, narrow, grads)


def key_ranges(own_ids, row_ids, rows):
    position = jnp.arange(row_ids.shape[0], dtype=jnp.int32)
    bounds = []
    for block in range(own_ids.shape[0] // rows):
        first = own_ids[block * rows]
        last = own_ids[(block + 1) * rows - 1]
        low = jnp.min(jnp.where(row_ids == first, position, row_ids.shape[0]))
        high = jnp.max(jnp.where(row_ids == last, position, -1)) + 1
        bounds += [low // KEYS, (high + KEYS - 1) // KEYS]
    return bounds


def body(
    tokens, picture, cotangent, first_gain, first_shift, query_weight, query_bias, key_weight,
    value_weight, value_bias, output_weight, output_bias, second_gain, second_shift, up_weight,
    up_bias, down_weight, down_bias,
):
    token_count = tokens.shape[0]
    rows = token_count // 4
    layers = query_weight.shape[0]
    head_cols = query_bias.shape[1]
    feed = up_bias.shape[1]
    feed_pad = -feed % LANES
    hid = lax.axis_index("hid")
    tok = lax.axis_index("tok")

    own_ids = lax.dynamic_slice_in_dim(picture, tok * token_count, token_count)
    row_ids = lax.dynamic_slice_in_dim(picture, (tok // 2) * 2 * token_count, 2 * token_count)
    meta = jnp.stack([hid, tok % 2] + key_ranges(own_ids, row_ids, rows)).astype(jnp.int32)

    def side_by_side(*parts):
        return jnp.concatenate(parts, axis=1)

    def padded(part):
        return jnp.pad(part, ((0, 0), (0, feed_pad)))

    def by_tokens(array):
        return array.transpose(1, 0, 2).reshape(rows, 4 * array.shape[2]).astype(F32)

    def by_features(array):
        return array.reshape(rows, 4, head_cols).transpose(1, 0, 2)

    count = lax.axis_size("tok")
    shard = query_weight.shape[1]
    shard_pad = -shard % 16
    layer_parts = []
    for layer in range(layers):
        mixed = side_by_side(
            key_weight[layer], value_weight[layer], query_weight[layer], output_weight[layer].T
        )
        layer_parts.append((mixed, padded(up_weight[layer]), padded(down_weight[layer].T)))
    vectors = jnp.stack(
        [first_gain, first_shift, output_bias, second_gain, second_shift, down_bias], axis=1
    )
    vectors = jnp.pad(vectors, ((0, 0), (0, 2), (0, 0))).reshape(layers * 8, head_cols)
    x, gradient, vectors, first_mixed = entry(
        tokens.reshape(4, rows, head_cols),
        cotangent.reshape(4, rows, head_cols),
        vectors,
        jnp.pad(layer_parts[0][0], ((0, shard_pad), (0, 0))),
        count,
    )
    x, gradient = by_tokens(x), by_tokens(gradient)
    vectors = vectors.transpose(1, 0, 2).reshape(layers, 8, 4 * head_cols)

    def gather(part):
        return lax.all_gather(part, "tok", axis=0, tiled=True)

    weights = []
    for layer in range(layers):
        mixed, up, down = layer_parts[layer]
        if layer == 0:
            mixed = first_mixed[:, :shard].reshape(count * shard, mixed.shape[1])
        else:
            mixed, _ = lax.optimization_barrier((mixed, both))
            mixed = gather(mixed)
            up, _ = lax.optimization_barrier((up, mixed))
        both = gather(side_by_side(up, down))
        up, down = jnp.split(both, 2, axis=1)
        weights.append((mixed, mixed[:, 3 * head_cols :], up, down))

    saved = []
    for layer in range(layers):
        mixed, out, up, down = weights[layer]
        bias = jnp.concatenate(
            [jnp.zeros_like(value_bias[layer]), value_bias[layer], query_bias[layer]]
        )[None]
        normed, queries, own_pairs, far_pairs = project(x, vectors[layer], mixed, bias, head_cols)
        mixture, logsum = attend(
            meta, queries, own_pairs, far_pairs, own_ids[:, None], row_ids[None, :]
        )
        hidden_bias = jnp.pad(up_bias[layer], (0, feed_pad))[None]
        x_next, after, normed_two, active, slope = mlp(
            mixture, x, vectors[layer], out, up, hidden_bias, down
        )
        saved.append(
            (x, normed, queries, own_pairs, far_pairs, mixture, logsum, after, normed_two, active, slope)
        )
        x = x_next
    final = x

    def scatter(part):
        mine = lax.psum_scatter(part, "tok", scatter_dimension=0, tiled=True)
        return lax.optimization_barrier(mine).astype(F32)

    grads = [None] * layers
    wide, narrow, broad = [None] * layers, [None] * layers, [None] * layers
    for layer in reversed(range(layers)):
        x, normed, queries, own_pairs, far_pairs, mixture, logsum, after, normed_two, active, slope = saved[layer]
        mixed, out, up, down = weights[layer]
        grad_after, grad_mixture, grad_down, grad_up, grad_out, sums_two, hidden_sums = mlp_back(
            gradient, after, vectors[layer], out, up, down, mixture, normed_two, active, slope
        )
        grad_queries, grad_own, grad_far = attend_back(
            meta, queries, own_pairs, far_pairs, own_ids[None, :], row_ids[:, None],
            grad_mixture, logsum,
        )
        if layer == 0:
            grad_after, grads[1][1] = lax.optimization_barrier((grad_after, grads[1][1]))
        gradient, grad_mixed, sums_one, column_sums = project_back(
            grad_after, x, vectors[layer], mixed, normed, grad_queries, grad_own, grad_far
        )
        grad_both = side_by_side(grad_up, grad_down)
        grad_mixed = side_by_side(grad_mixed, grad_out)
        grads[layer] = [grad_mixed, scatter(grad_both)]
        if layer > 0:
            grads[layer][0] = scatter(grad_mixed)
        wide[layer] = sums_one + sums_two
        narrow[layer] = column_sums[0]
        broad[layer] = hidden_sums[0]
    wide = jnp.concatenate(wide, axis=0)
    wide = wide.reshape(layers * 8, 4, head_cols).transpose(1, 0, 2)
    narrow = jnp.concatenate(narrow + broad)
    narrow_rows = -(-narrow.shape[0] // head_cols)
    narrow_rows += -narrow_rows % 8
    narrow = jnp.pad(narrow, (0, narrow_rows * head_cols - narrow.shape[0]))
    grad_mixed = grads[0][0].reshape(count, shard, 4 * head_cols)
    final, gradient, sums, first_grad = finish(
        by_features(final.astype(BF)),
        by_features(gradient.astype(BF)),
        wide,
        narrow.reshape(narrow_rows, head_cols),
        jnp.pad(grad_mixed, ((0, 0), (0, shard_pad), (0, 0))),
    )
    grads[0][0] = first_grad[:shard]
    wide = sums[: layers * 8].reshape(layers, 8, head_cols)
    narrow = sums[layers * 8 :].reshape(-1)
    cut = layers * 3 * head_cols
    broad = narrow[cut : cut + layers * (feed + feed_pad)].reshape(layers, feed + feed_pad)[:, :feed]
    narrow = narrow[:cut].reshape(layers, 3 * head_cols)

    def stacked(pick):
        return jnp.stack([pick(mixed, both) for mixed, both in grads])

    return (
        final.reshape(4 * rows, head_cols).astype(F32),
        gradient.reshape(4 * rows, head_cols).astype(F32),
        wide[:, 0],
        wide[:, 1],
        stacked(lambda mixed, both: mixed[:, 2 * head_cols : 3 * head_cols]),
        narrow[:, 2 * head_cols :],
        stacked(lambda mixed, both: mixed[:, :head_cols]),
        stacked(lambda mixed, both: mixed[:, head_cols : 2 * head_cols]),
        narrow[:, head_cols : 2 * head_cols],
        stacked(lambda mixed, both: mixed[:, 3 * head_cols :].T),
        wide[:, 2],
        wide[:, 3],
        wide[:, 4],
        stacked(lambda mixed, both: both[:, :feed]),
        broad,
        stacked(lambda mixed, both: both[:, feed + feed_pad : feed + feed_pad + feed].T),
        wide[:, 5],
    )


def solution(mesh):
    rows = P("tok", "hid")
    vector = P(None, "hid")
    inward = P(None, "tok", "hid")
    outward = P(None, "hid", "tok")
    in_specs = (
        rows, P(), rows, vector, vector, inward, vector, inward, inward, vector, outward, vector,
        vector, vector, inward, vector, outward, vector,
    )
    out_specs = (
        rows, rows, vector, vector, inward, vector, inward, inward, vector, outward, vector,
        vector, vector, inward, vector, outward, vector,
    )
    return jax.shard_map(body, mesh=mesh, in_specs=in_specs, out_specs=out_specs, check_vma=False)
```

time: 1940 us -> 931 us (0.48)
  waiting for transfers between devices: 823 us -> 113 us
  Pallas kernels: 0 us -> 679 us
  blocking collectives: 372 us -> 0 us
  matrix products: 366 us -> 0 us
  loops' own time: 105 us -> 0 us
  local copies, waits for them, and re-layouts: 141 us -> 56.3 us
  other arithmetic: 95.3 us -> 44.4 us
    pallas_call x0 -> x14, Pallas kernels: none -> 679 us  [the longest x2 108 us: mlp_back(): pl.pallas_call(mlp_back_kernel, name='mlp_back', cost_estimate=micros(54)...]
    dot_general x148 -> x0, matrix products: 366 us -> none  [the longest x32 67 us: one_tile(): lax.dot_general(query_tile, key_tile, across, preferred_element_type=jnp....]
    reduce_scatter x12 -> x3, waiting for transfers between devices: 398 us -> 70.7 us  [scatter(): mine = lax.psum_scatter(part, 'tok', scatter_dimension=0, tiled=True)]
    all_gather x8 -> x0, blocking collectives: 293 us -> none  [the longest x2 99.2 us: fetch_layer(): lax.all_gather(output_part[layer_index], 'tok', axis=1, tiled=True)]
    all_gather x12 -> x3, waiting for transfers between devices: 325 us -> 42.3 us  [gather(): return lax.all_gather(part, 'tok', axis=0, tiled=True)]
    another operation x4 -> x0, loops' own time: 105 us -> none  [the longest x2 62.9 us: attend_backward(): lax.map(one_tile, jnp.arange(head_count * block_count, dtype=jnp.int32))]
    psum x5 -> x0, blocking collectives: 64.7 us -> none  [the longest x1 40.9 us: body(): lax.psum((jnp.stack(narrow_grads), jnp.stack(broad_grads)), 'tok')]
    reduce_sum x41 -> x0, other arithmetic: 52.2 us -> none  [the longest x16 11.3 us: one_tile(): totals = jnp.sum(powers, axis=1, keepdims=True)]
  transfers between devices with their start and end apart: 30 -> 6, of which waited for: 23 -> 2; matrix products, arithmetic and copies ran while one was open for 13% -> 8% of each run, Pallas kernels for 0% -> 53%
where the time goes in v1:
time: 931 us; the launch traced here: 922 us
  Pallas kernels  679 us (73%)
  waiting for transfers between devices  113 us (12%)
  local copies, waits for them, and re-layouts  56.3 us (6%)
  other arithmetic  44.4 us (5%)
  between operations  27.9 us (3%)
    pallas_call x2, Pallas kernels, mlp_back(): pl.pallas_call(mlp_back_kernel, name='mlp_back', cost_estimate=micros(54)...  108 us
    pallas_call x2, Pallas kernels, mlp(): pl.pallas_call(mlp_kernel, name='mlp', cost_estimate=micros(51), out_shap...  103 us
    pallas_call x2, Pallas kernels, project_back(): pl.pallas_call(project_back_kernel, name='project_back', cost_estimate=mi...  102 us
    pallas_call x2, Pallas kernels, project(): pl.pallas_call(functools.partial(project_kernel, factor=HEAD_DIM ** (-0.5...  97.6 us
    pallas_call x1, Pallas kernels, finish(): pl.pallas_call(finish_kernel, name='finish', cost_estimate=micros(40), ou...  82.5 us
    pallas_call x2, Pallas kernels, attend_back(): pl.pallas_call(functools.partial(attend_back_kernel, heads=heads), name='...  75.9 us
    reduce_scatter x3, waiting for transfers between devices, scatter(): mine = lax.psum_scatter(part, 'tok', scatter_dimension=0, tiled=True)  70.7 us
    pallas_call x1, Pallas kernels, entry(): pl.pallas_call(entry_kernel, name='entry', cost_estimate=micros(40), out_...  61.4 us
  transfers between devices with their start and end apart: 6, of which 2 were waited for; matrix products, arithmetic and copies ran while one was open for 8% of the time, Pallas kernels for 53%

profile of v1, /device:TPU:0, one launch (start us, length us, event | category | flops | bytes accessed | tf_op | source)
XLA Modules:
  0.0 921.6 jit_solution(16322339364337376301)
XLA Ops:
  7.2 1.2 slice_bitcast_fusion.4
  8.4 1.2 slice_bitcast_fusion.5
  9.7 0.9 fusion.3
  10.7 1.2 copy.50
  11.9 1.2 copy.51
  13.9 0.7 slice_bitcast_fusion.17
  14.6 0.9 concatenate.36.shard
  16.1 61.4 %entry.1 = (bf16[4,256,288]{2,1,0:T(8,128)(2,1)}, bf16[4,256,288]{2,1,0:T(8,128)(2,1)}, f32[4,16,288]{2,1,0:T(8,128)}, bf16[8,144,1152]{2,1,0:T(8,128)(2,1)}) custom-call(bf16[4,256,288]{2,1,0:T(8,128)(2,1)} %bitcast.151, bf16[4,256,288]{2,1,0:T(8,128)(2,1)} %bitcast.152, f32[16,288]{1,0:T(8,128)} %pad_bitcast_fusion.vectors, ...), custom_call_target="tpu_custom_call" | custom-call | flops 40000000000 | tf_op jit(solution)/shard_map/entry/pallas_call | solution.py:770
  77.5 1.3 convert_bitcast_fusion.1
  79.3 1.4 copy.55.x
  82.2 1.0 concatenate.39
  83.1 42.3 %all-gather.4.cloned.1.call-done = bf16[1152,2304]{1,0:T(8,128)(2,1)} async-done(((bf16[144,2304]{1,0:T(8,128)(2,1)}), bf16[1152,2304]{1,0:T(8,128)(2,1)}) %all-gather.4.cloned.1.call-update) | async-done | bytes 5308432 | tf_op jit(solution)/shard_map/all_gather | solution.py:948
  125.7 40.6 %project.2 = (bf16[4,256,1152]{2,1,0:T(8,128)(2,1)}, bf16[4,256,288]{2,1,0:T(8,128)(2,1)}, bf16[4,256,576]{2,1,0:T(8,128)(2,1)}, bf16[4,256,576]{2,1,0:T(8,128)(2,1)}) custom-call(f32[256,1152]{1,0:T(8,128)} %copy.55.x, f32[8,1152]{1,0:T(8,128)} %squeeze.132.vec, bf16[1152,1152]{1,0:T(8,128)(2,1)} %bitcast.154, f32[1,864]{1,0:T(1,128)} %broadcast_in_dim.43.bias), custom_call_target="tpu_custom_call" | custom-call | flops 44000002048 | tf_op jit(solution)/shard_map/project/pallas_call | solution.py:214
  166.4 0.8 dynamic_slice.7
  167.7 6.7 select_reduce_fusion
  187.3 2.5 slice.230.out_weight
  189.8 1.1 copy.56.query_ids
  191.5 0.7 squeeze.138.vec
  194.0 1.4 copy.63.gradient
  195.4 1.3 copy.64.key_ids
  197.4 24.3 %attend.2 = (bf16[4,256,288]{2,1,0:T(8,128)(2,1)}, f32[8,1024]{1,0:T(8,128)}) custom-call(s32[10]{0:T(128)} %stack.118.meta, bf16[4,256,288]{2,1,0:T(8,128)(2,1)} %get-tuple-element.82.queries, bf16[4,256,576]{2,1,0:T(8,128)(2,1)} %get-tuple-element.83.own_pairs, bf16[4,256,576]{2,1,0:T(8,128)(2,1)} %get-tuple-element.84.far_pairs, ...), custom_call_target="tpu_custom_call" | custom-call | flops 22000001024 | tf_op jit(solution)/shard_map/attend/pallas_call | solution.py:333
  221.7 5.3 fusion.8
  226.9 0.9 fusion.4
  228.1 51.7 %mlp.2 = (f32[256,1152]{1,0:T(8,128)}, f32[256,1152]{1,0:T(8,128)}, bf16[4,256,1152]{2,1,0:T(8,128)(2,1)}, bf16[4,256,1152]{2,1,0:T(8,128)(2,1)}, bf16[4,256,1152]{2,1,0:T(8,128)(2,1)}) custom-call(bf16[4,256,288]{2,1,0:T(8,128)(2,1)} %get-tuple-element.85.mixture, f32[256,1152]{1,0:T(8,128)} %copy.55.x, f32[8,1152]{1,0:T(8,128)} %squeeze.132.vec, ...), custom_call_target="tpu_custom_call" | custom-call | flops 51000000512 | tf_op jit(solution)/shard_map/mlp/pallas_call | solution.py:528
  279.8 2.5 slice.232.out_weight
  282.3 57.1 %project.3 = (bf16[4,256,1152]{2,1,0:T(8,128)(2,1)}, bf16[4,256,288]{2,1,0:T(8,128)(2,1)}, bf16[4,256,576]{2,1,0:T(8,128)(2,1)}, bf16[4,256,576]{2,1,0:T(8,128)(2,1)}) custom-call(f32[256,1152]{1,0:T(8,128)} %get-tuple-element.86.x, f32[8,1152]{1,0:T(8,128)} %squeeze.138.vec, bf16[1152,1152]{1,0:T(8,128)(2,1)} %all-gather.6.cloned.1.call-done.weight, ...), custom_call_target="tpu_custom_call" | custom-call | flops 44000002048 | tf_op jit(solution)/shard_map/project/pallas_call | solution.py:214
  339.4 24.5 %attend.3 = (bf16[4,256,288]{2,1,0:T(8,128)(2,1)}, f32[8,1024]{1,0:T(8,128)}) custom-call(s32[10]{0:T(128)} %stack.118.meta, bf16[4,256,288]{2,1,0:T(8,128)(2,1)} %get-tuple-element.88.queries, bf16[4,256,576]{2,1,0:T(8,128)(2,1)} %get-tuple-element.89.own_pairs, bf16[4,256,576]{2,1,0:T(8,128)(2,1)} %get-tuple-element.90.far_pairs, ...), custom_call_target="tpu_custom_call" | custom-call | flops 22000001024 | tf_op jit(solution)/shard_map/attend/pallas_call | solution.py:333
  363.8 5.4 fusion.7
  369.2 51.6 %mlp.3 = (f32[256,1152]{1,0:T(8,128)}, f32[256,1152]{1,0:T(8,128)}, bf16[4,256,1152]{2,1,0:T(8,128)(2,1)}, bf16[4,256,1152]{2,1,0:T(8,128)(2,1)}, bf16[4,256,1152]{2,1,0:T(8,128)(2,1)}) custom-call(bf16[4,256,288]{2,1,0:T(8,128)(2,1)} %get-tuple-element.91.mixture, f32[256,1152]{1,0:T(8,128)} %get-tuple-element.86.x, f32[8,1152]{1,0:T(8,128)} %squeeze.138.vec, ...), custom_call_target="tpu_custom_call" | custom-call | flops 51000000512 | tf_op jit(solution)/shard_map/mlp/pallas_call | solution.py:528
  420.8 53.4 %mlp_back.2 = (f32[256,1152]{1,0:T(8,128)}, bf16[4,256,288]{2,1,0:T(8,128)(2,1)}, bf16[1152,1152]{1,0:T(8,128)(2,1)}, bf16[1152,1152]{1,0:T(8,128)(2,1)}, bf16[1...) custom-call(f32[256,1152]{1,0:T(8,128)} %copy.63.gradient, f32[256,1152]{1,0:T(8,128)} %get-tuple-element.95.after, ...), custom_call_target="tpu_custom_call" | custom-call | flops 54000001024 | tf_op jit(solution)/shard_map/mlp_back/pallas_call | solution.py:627
  474.2 37.9 %attend_back.2 = (bf16[4,256,288]{2,1,0:T(8,128)(2,1)}, bf16[4,256,576]{2,1,0:T(8,128)(2,1)}, bf16[4,256,576]{2,1,0:T(8,128)(2,1)}) custom-call(s32[10]{0:T(128)} %stack.118.meta, bf16[4,256,288]{2,1,0:T(8,128)(2,1)} %get-tuple-element.88.queries, bf16[4,256,576]{2,1,0:T(8,128)(2,1)} %get-tuple-element.89.own_pairs, ...), custom_call_target="tpu_custom_call" | custom-call | flops 36999999488 | tf_op jit(solution)/shard_map/attend_back/pallas_call | solution.py:439
  512.1 43.6 %project_back.2 = (f32[256,1152]{1,0:T(8,128)}, bf16[1152,864]{1,0:T(8,128)(2,1)}, f32[8,1152]{1,0:T(8,128)}, f32[1,864]{1,0:T(1,128)}) custom-call(f32[256,1152]{1,0:T(8,128)} %get-tuple-element.99.grad_after, f32[256,1152]{1,0:T(8,128)} %get-tuple-element.86.x, f32[8,1152]{1,0:T(8,128)} %squeeze.138.vec, ...), custom_call_target="tpu_custom_call" | custom-call | flops 44000002048 | tf_op jit(solution)/shard_map/project_back/pallas_call | solution.py:710
  555.8 3.6 pad_maximum_fusion.3
  559.5 1.7 copy-done
  561.2 4.5 pad_maximum_fusion
  566.0 1.0 copy-done.1
  567.3 1.2 copy.61
  568.5 54.7 %mlp_back.3 = (f32[256,1152]{1,0:T(8,128)}, bf16[4,256,288]{2,1,0:T(8,128)(2,1)}, bf16[1152,1152]{1,0:T(8,128)(2,1)}, bf16[1152,1152]{1,0:T(8,128)(2,1)}, bf16[1...) custom-call(f32[256,1152]{1,0:T(8,128)} %get-tuple-element.106.gradient, ...), custom_call_target="tpu_custom_call" | custom-call | flops 54000001024 | tf_op jit(solution)/shard_map/mlp_back/pallas_call | solution.py:627
  623.2 0.7 reduce.8
  624.0 5.3 pad_maximum_fusion.1
  629.2 37.9 %attend_back.3 = (bf16[4,256,288]{2,1,0:T(8,128)(2,1)}, bf16[4,256,576]{2,1,0:T(8,128)(2,1)}, bf16[4,256,576]{2,1,0:T(8,128)(2,1)}) custom-call(s32[10]{0:T(128)} %stack.118.meta, bf16[4,256,288]{2,1,0:T(8,128)(2,1)} %get-tuple-element.82.queries, bf16[4,256,576]{2,1,0:T(8,128)(2,1)} %get-tuple-element.83.own_pairs, ...), custom_call_target="tpu_custom_call" | custom-call | flops 36999999488 | tf_op jit(solution)/shard_map/attend_back/pallas_call | solution.py:439
  667.2 1.0 convert_element_type.66
  668.3 0.9 slice_bitcast_fusion.8
  669.2 70.7 %reduce-scatter.4.cloned.1.call-done = bf16[144,2304]{1,0:T(8,128)(2,1)} async-done(((bf16[1152,2304]{1,0:T(8,128)(2,1)}), bf16[144,2304]{1,0:T(8,128)(2,1)}) %reduce-scatter.4.cloned.1.call-update) | async-done | bytes 663568 | tf_op jit(solution)/shard_map/reduce_scatter | solution.py:984
  739.9 1.2 convert_element_type.60
  741.1 58.0 %project_back.3 = (f32[256,1152]{1,0:T(8,128)}, bf16[1152,864]{1,0:T(8,128)(2,1)}, f32[8,1152]{1,0:T(8,128)}, f32[1,864]{1,0:T(1,128)}) custom-call(f32[256,1152]{1,0:T(8,128)} %get-tuple-element.114.grad_after, f32[256,1152]{1,0:T(8,128)} %copy.55.x, f32[8,1152]{1,0:T(8,128)} %squeeze.132.vec, bf16[1152,1152]{1,0:T(8,128)(2,1)} %bitcast.156, ...), custom_call_target="tpu_custom_call" | custom-call | flops 44000002048 | tf_op jit(solution)/shard_map/project_back/pallas_call | solution.py:710
  799.1 1.4 convert_element_type.61
  800.7 1.2 copy.68
  803.5 3.6 pad_maximum_fusion.2
  807.1 82.5 %finish.1 = (bf16[4,256,288]{2,1,0:T(8,128)(2,1)}, bf16[4,256,288]{2,1,0:T(8,128)(2,1)}, f32[32,288]{1,0:T(8,128)}, f32[144,1152]{1,0:T(8,128)}) custom-call(bf16[4,256,288]{2,1,0:T(8,128)(2,1)} %bitcast.150, bf16[4,256,288]{2,1,0:T(8,128)(2,1)} %bitcast.153, f32[4,16,288]{2,1,0:T(8,128)} %bitcast.157, f32[16,288]{1,0:T(8,128)} %reshape.99.narrow, ...), custom_call_target="tpu_custom_call" | custom-call | flops 40000000000 | tf_op jit(solution)/shard_map/finish/pallas_call | solution.py:854
  889.6 0.7 slice.210
  890.3 0.7 slice.224
  891.0 1.2 bitcast_convert_fusion.1
  892.3 1.5 copy.76
  893.7 1.2 bitcast_convert_fusion
  895.0 1.5 copy.77
  900.1 2.4 slice_bitcast_fusion.12
  902.6 1.2 convert_element_type.67
  905.2 1.8 pad_maximum_fusion.6
  907.1 1.7 pad_maximum_fusion.7
  908.8 1.7 pad_maximum_fusion.8
  910.5 1.7 pad_maximum_fusion.9
  912.2 1.1 pad_maximum_fusion.4
  913.4 1.1 pad_maximum_fusion.5
  (141 shorter events, 15.3 us)
Async XLA Ops:
  7.2 3.5 copy-start.6
  7.2 118.3 %all-gather.4.cloned.1.call-start = ((), (), s32[]{:S(2)}) async-start(), calls=%async_computation.3 | async-start | bytes 5971968 | tf_op jit(solution)/shard_map/all_gather | solution.py:948
  8.4 3.4 copy-start.7
  9.6 3.4 copy-start.29
  9.6 3.4 copy-start.30
  9.7 3.4 copy-start.31
  9.7 3.4 copy-start.32
  9.7 3.4 copy-start.33
  9.7 3.4 copy-start.34
  9.7 3.4 copy-start.13
  9.7 3.5 copy-start.14
  10.6 3.2 copy-start.11
  10.6 3.2 copy-start.12
  10.6 216.3 %all-gather.6.cloned.1.call-start = ((), (), s32[]{:S(2)}) async-start(), calls=%async_computation.4 | async-start | bytes 2985984 | tf_op jit(solution)/shard_map/all_gather | solution.py:948
  78.8 2.6 copy-start.27
  78.8 2.6 copy-start.28
  79.3 1.4 copy-start.15
  79.3 2.9 copy-start.8
  79.3 2.9 copy-start.9
  79.3 2.9 copy-start.10
  125.5 238.3 %all-gather.8.cloned.1.call-start = ((), (), s32[]{:S(2)}) async-start(), calls=%async_computation.5 | async-start | bytes 5971968 | tf_op jit(solution)/shard_map/all_gather | solution.py:948
  166.3 24.6 %copy-start.23 = (f32[2,1076]{1,0:T(2,128)S(1)}, f32[2,1076]{1,0:T(2,128)}, u32[]{:S(2)}) copy-start(f32[2,1076]{1,0:T(2,128)} %param.33) | copy-start | bytes 25828
  166.3 27.1 %copy-start.5 = (bf16[4,256,288]{2,1,0:T(8,128)(2,1)S(1)}, bf16[4,256,288]{2,1,0:T(8,128)(2,1)}, u32[]{:S(2)}) copy-start(bf16[4,256,288]{2,1,0:T(8,128)(2,1)} %get-tuple-element.94) | copy-start | bytes 1769476
  167.1 24.4 %copy-start.17 = (s32[1024]{0:T(1024)}, s32[1024]{0:T(1024)S(1)}, u32[]{:S(2)}) copy-start(s32[1024]{0:T(1024)S(1)} %dynamic_slice.7) | copy-start | bytes 12292
  174.4 21.0 %copy-start.22 = (s32[2048]{0:T(1024)}, s32[2048]{0:T(1024)S(1)}, u32[]{:S(2)}) copy-start(s32[2048]{0:T(1024)S(1)} %get-tuple-element.189) | copy-start | bytes 24580
  227.9 439.3 %reduce-scatter.6.cloned.1.call-start = ((), (), s32[]{:S(2)}) async-start(), calls=%async_computation.7 | async-start | bytes 2985984 | tf_op jit(solution)/shard_map/reduce_scatter | solution.py:984
  512.1 43.6 %copy-start.4 = (bf16[1152,288]{1,0:T(8,128)(2,1)S(1)}, bf16[1152,288]{1,0:T(8,128)(2,1)}, u32[]{:S(2)}) copy-start(bf16[1152,288]{1,0:T(8,128)(2,1)} %get-tuple-element.137) | copy-start | bytes 1990660
  559.4 1.7 copy-start
  559.4 180.4 %reduce-scatter.4.cloned.1.call-start = ((), (), s32[]{:S(2)}) async-start(), calls=%async_computation.6 | async-start | bytes 5971968 | tf_op jit(solution)/shard_map/reduce_scatter | solution.py:984
  565.7 1.3 copy-start.1
  565.7 2.7 copy-start.25
  565.7 336.9 %reduce-scatter.8.cloned.1.call-start = ((), (), s32[]{:S(2)}) async-start(), calls=%async_computation.8 | async-start | bytes 5971968 | tf_op jit(solution)/shard_map/reduce_scatter | solution.py:984
  568.4 55.5 %copy-start.24 = (f32[1,1152]{1,0:T(1,128)S(1)}, f32[1,1152]{1,0:T(1,128)}, u32[]{:S(2)}) copy-start(f32[1,1152]{1,0:T(1,128)} %get-tuple-element.129) | copy-start | bytes 13828
  568.4 55.5 %copy-start.18 = (f32[8,1152]{1,0:T(8,128)S(1)}, f32[8,1152]{1,0:T(8,128)}, u32[]{:S(2)}) copy-start(f32[8,1152]{1,0:T(8,128)} %get-tuple-element.125) | copy-start | bytes 110596
  568.4 55.5 %copy-start.20 = (f32[8,1152]{1,0:T(8,128)S(1)}, f32[8,1152]{1,0:T(8,128)}, u32[]{:S(2)}) copy-start(f32[8,1152]{1,0:T(8,128)} %get-tuple-element.124) | copy-start | bytes 110596
  799.1 2.8 copy-start.19
  799.1 2.8 copy-start.21
  799.1 3.6 copy-start.26
  800.7 2.8 copy-start.3
  893.7 2.7 copy-start.16
  902.6 4.5 copy-start.2
Sparse Core Ops, SparseCore 0:
  10.8 114.6 all-gather.3
  128.2 68.6 all-gather.5
  228.0 114.8 all-gather.7
  559.5 73.4 reduce-scatter.5
  636.9 102.8 reduce-scatter.3
  743.3 139.5 reduce-scatter.7

commit v2 on v1

v2 whole, which is shorter than its diff:
```python
import functools

import jax
import jax.numpy as jnp
from jax import lax
from jax.experimental import pallas as pl
from jax.experimental.pallas import tpu as pltpu
from jax.sharding import PartitionSpec as P

HEAD_DIM = 72
LANES = 128
KEYS = 512
EPS = 1e-06
GELU = 0.7978845608028654
CUBE = 0.044715
MASKED = -1e30
LOG2E = 1.4426950408889634
LN2 = 0.6931471805599453
NN = (((1,), (0,)), ((), ()))
NT = (((1,), (1,)), ((), ()))
TN = (((0,), (0,)), ((), ()))
MESH = pl.DeviceIdType.MESH
BF = jnp.bfloat16
F32 = jnp.float32
VMEM_LIMIT = 60 * 1024 * 1024


def dot(left, right, dims=NN):
    return lax.dot_general(left, right, dims, preferred_element_type=F32)


def micros(duration):
    return pl.CostEstimate(flops=duration * 10**9, bytes_accessed=0, transcendentals=0)


def flat(value):
    return value.reshape(value.shape[0] * value.shape[1], value.shape[2])


class Net:
    def __init__(self, send_sems, recv_sems):
        tok, hid = lax.axis_index("tok"), lax.axis_index("hid")
        near = hid + 1 - 2 * lax.rem(hid, 2)
        self.tok, self.hid = tok, hid
        self.core = (tok, near)
        self.far = (tok, lax.rem(hid + 2, 4))
        self.far_core = (tok, lax.rem(near + 2, 4))
        self.half = (tok + 1 - 2 * lax.rem(tok, 2), hid)
        self.low, self.high = lax.rem(tok, 2), lax.div(tok, 2)
        self.send_sems, self.recv_sems = send_sems, recv_sems
        self.copies, self.count = [], 0

    def row(self, high):
        return (high * 2 + self.low, self.hid)

    def line(self, count):
        self.before, self.has_before = self.row(lax.max(self.high - 1, 0)), self.high > 0
        self.after = self.row(lax.min(self.high + 1, count - 1))
        self.has_after, self.last = self.high + 1 < count, count - 1

    def barrier(self, devices, line=False):
        sem = pltpu.get_barrier_semaphore()

        def signal(device):
            pl.semaphore_signal(sem, inc=1, device_id=device, device_id_type=MESH)

        for device in devices:
            signal(device)
        peers = len(devices)
        if line:
            pl.when(self.has_before)(lambda: signal(self.before))
            pl.when(self.has_after)(lambda: signal(self.after))
            peers = peers + lax.min(self.high, 1) + lax.min(self.last - self.high, 1)
        pl.semaphore_wait(sem, peers)

    def take(self, count):
        first = self.count
        self.count += count
        return first

    def make(self, index, source, target, device):
        return pltpu.make_async_remote_copy(
            src_ref=source,
            dst_ref=target,
            send_sem=self.send_sems.at[index],
            recv_sem=self.recv_sems.at[index],
            device_id=device,
            device_id_type=MESH,
        )

    def copy(self, source, target, device):
        made = self.make(self.take(1), source, target, device)
        self.copies.append(made)
        made.start()
        return made

    def finish(self, waited=()):
        done = [id(made) for made in waited]
        for made in self.copies:
            if id(made) not in done:
                made.wait_send()


class Moves:
    def __init__(self, sems):
        self.sems, self.count, self.stores = sems, 0, []

    def take(self, count):
        first = self.count
        self.count += count
        return first

    def make(self, index, source, target):
        return pltpu.make_async_copy(source, target, self.sems.at[index])

    def load(self, source, target):
        made = self.make(self.take(1), source, target)
        made.start()
        return made

    def store(self, source, target):
        self.stores.append(self.load(source, target))

    def finish(self):
        for made in self.stores:
            made.wait()


class Several:
    def __init__(self, copies):
        self.copies = copies

    def wait(self):
        for one in self.copies:
            one.wait()


def weight_loads(parts):
    return 1 if len(parts) == 1 else 2 * parts[0].shape[0]


def load_weight(net, moves, parts, columns, target):
    if len(parts) == 1:
        return moves.load(parts[0].at[:, columns], target)
    copies = []
    for part, low in zip(parts, (net.low, 1 - net.low)):
        shard = part.shape[1]
        for high in range(part.shape[0]):
            start = pl.multiple_of((high * 2 + low) * shard, 16)
            copies.append(moves.load(part.at[high, :, columns], target.at[pl.ds(start, shard)]))
    return Several(copies)


def spaced(arrays):
    return [(array, False) for array in arrays]


def job_copies(count):
    return 2 * count + 1


class GatherJob:
    def __init__(self, net, moves, shard, weights):
        self.net, self.weights = net, weights
        self.count = weights.shape[0] // 2
        self.across = net.take(2 * self.count - 1)
        self.up, self.down = net.take(self.count), net.take(self.count)
        own = weights.at[net.tok]
        moves.store(shard, own)
        first = self.swap(0, shard, own)
        pl.when(net.has_after)(lambda: net.make(self.up, shard, own, net.after).start())
        pl.when(net.has_before)(lambda: net.make(self.down, shard, own, net.before).start())
        first.start()

    def swap(self, index, source, target):
        return self.net.make(self.across + index, source, target, self.net.half)

    def arrive(self, step, above):
        net = self.net
        place = net.high + step if above else net.high - step
        block = self.weights.at[place * 2 + net.low]
        base, onward = (self.down, net.before) if above else (self.up, net.after)
        net.make(base + step - 1, block, block, onward).wait_recv()
        if step + 1 < self.count:
            go_on = net.has_before if above else net.has_after
            pl.when(go_on)(lambda: net.make(base + step, block, block, onward).start())
        self.swap(2 * step - int(above), block, block).start()

    def forward(self, point, points):
        net = self.net
        for step in range(1, self.count):
            if (step - 1) * points // (self.count - 1) == point:
                pl.when(net.high - step >= 0)(functools.partial(self.arrive, step, False))
                pl.when(net.high + step < self.count)(functools.partial(self.arrive, step, True))

    def finish(self):
        net = self.net
        own = self.weights.at[net.tok]
        self.swap(0, own, own).wait()
        for step in range(1, self.count):
            below, above = net.high - step >= 0, net.high + step < self.count
            pl.when(below)(lambda step=step: self.swap(2 * step, own, own).wait())
            pl.when(above)(lambda step=step: self.swap(2 * step - 1, own, own).wait())
        for step in range(self.count - 1):
            for base, device, has, there in (
                (self.up, net.after, net.has_after, net.high - step >= 0),
                (self.down, net.before, net.has_before, net.high + step < self.count),
            ):
                sent = net.make(base + step, own, own, device)
                pl.when(jnp.logical_and(has, there))(sent.wait_send)


class Line:
    def __init__(self, net, count, value, passing, arrived):
        self.net, self.count, self.value = net, count, value
        self.passing, self.arrived = passing, arrived
        self.up, self.down = net.take(count), net.take(count)

    def upward(self, place):
        source, target = self.passing.at[place], self.arrived.at[place + 1]
        return self.net.make(self.up + place, source, target, self.net.after)

    def downward(self, place):
        source, target = self.passing.at[place], self.arrived.at[place]
        return self.net.make(self.down + place, source, target, self.net.before)

    def send(self, place, above):
        net = self.net
        value = self.value(place)
        self.passing[place] = value.astype(BF)
        move = self.upward(place) if above else self.downward(place)

        def add():
            move.wait_recv()
            landed = self.arrived[place + 1 if above else place]
            self.passing[place] = (value + landed.astype(F32)).astype(BF)

        pl.when(net.has_before if above else net.has_after)(add)
        move.start()

    def forward(self, point, points):
        high, last = self.net.high, self.count - 1
        for slot in range(last):
            if slot * points // last == point:
                pl.when(high <= slot)(functools.partial(self.send, last - slot + high, True))
                pl.when(last - high <= slot)(functools.partial(self.send, slot - last + high, False))

    def finish(self, total):
        net = self.net
        total[...] = self.value(net.high)

        def add(move, place):
            move.wait_recv()
            total[...] += self.arrived[place].astype(F32)

        pl.when(net.has_before)(lambda: add(self.upward(net.high), net.high + 1))
        pl.when(net.has_after)(lambda: add(self.downward(net.high), net.high))

    def drain(self):
        for place in range(self.count):
            pl.when(self.net.high < place)(self.upward(place).wait_send)
            pl.when(self.net.high > place)(self.downward(place).wait_send)


def part_scratch(count, shard, width):
    half = count // 2
    return [pltpu.VMEM((half, shard, width), BF)] * 3 + [pltpu.VMEM((half + 1, shard, width), BF)]


class ScatterParts:
    def __init__(self, net, moves, grads, scratch):
        self.net, self.moves = net, moves
        self.own, self.landed, passing, arrived = scratch
        self.count = count = grads.shape[0] // 2
        ends = [[count - 1 - step, step] for step in range((count + 1) // 2)]
        order = list(dict.fromkeys(sum(ends, [])))
        self.across, self.loads = net.take(count), moves.take(count)
        for place in order:
            self.swap(place, grads.at[place * 2 + 1 - net.low]).start()
        for place in order:
            source = grads.at[place * 2 + net.low]
            moves.make(self.loads + place, source, self.own.at[place]).start()
        self.line = Line(net, count, self.pair, passing, arrived)
        self.forward = self.line.forward

    def swap(self, place, source=None):
        target = self.landed.at[place]
        source = target if source is None else source
        return self.net.make(self.across + place, source, target, self.net.half)

    def pair(self, place):
        own = self.own.at[place]
        self.moves.make(self.loads + place, own, own).wait()
        self.swap(place).wait_recv()
        return self.own[place].astype(F32) + self.landed[place].astype(F32)

    def finish(self, total):
        self.line.finish(total)
        self.line.drain()
        for place in range(self.count):
            self.swap(place).wait_send()


def run(kernel, name, duration, inputs, outputs, scratch, identity, copies, moves):
    def space(near):
        return pl.BlockSpec(memory_space=pltpu.VMEM if near else pl.ANY)

    return pl.pallas_call(
        kernel,
        name=name,
        cost_estimate=micros(duration),
        out_shape=[jax.ShapeDtypeStruct(shape, dtype) for shape, dtype, _ in outputs],
        in_specs=[space(near) for _, near in inputs],
        out_specs=[space(near) for _, _, near in outputs],
        scratch_shapes=list(scratch)
        + [
            pltpu.SemaphoreType.DMA((copies,)),
            pltpu.SemaphoreType.DMA((copies,)),
            pltpu.SemaphoreType.DMA((moves,)),
        ],
        compiler_params=pltpu.CompilerParams(
            collective_id=identity, has_side_effects=True, vmem_limit_bytes=VMEM_LIMIT
        ),
    )(*[array for array, _ in inputs])


def split_refs(refs, inputs, outputs):
    return refs[:inputs], refs[inputs : inputs + outputs], refs[inputs + outputs :]


def norm_parts(rows):
    centred = rows - jnp.mean(rows, axis=1, keepdims=True)
    inverse = lax.rsqrt(jnp.mean(centred * centred, axis=1, keepdims=True) + EPS)
    return centred * inverse, inverse


def norm_back(rows, gain, grad):
    scaled, inverse = norm_parts(rows)
    inner = grad * gain
    first = jnp.mean(inner, axis=1, keepdims=True)
    second = jnp.mean(inner * scaled, axis=1, keepdims=True)
    return (
        inverse * (inner - first - scaled * second),
        jnp.sum(grad * scaled, axis=0, keepdims=True),
        jnp.sum(grad, axis=0, keepdims=True),
    )


def gather_send(net, full, chunk):
    near = net.copy(full.at[0, chunk], full.at[1, chunk], net.core)
    far = net.copy(full.at[0, chunk], full.at[2, chunk], net.far)
    return near, far


def gather_pass(net, full, chunk, far):
    far.wait_recv()
    return net.copy(full.at[2, chunk], full.at[3, chunk], net.core)


def scatter_scratch(rows, width):
    return [
        pltpu.VMEM((rows, width), F32),
        pltpu.VMEM((rows, width), F32),
    ] + [pltpu.VMEM((rows, width), BF)] * 6


class Scatter:
    def __init__(self, net, scratch):
        self.net = net
        self.hold, self.total, self.cs0, self.cr0, self.ys, self.yr, self.cs1, self.cr1 = scratch
        self.first, self.second = {}, {}

    def far_part(self, key, chunk, partial):
        rows = partial.shape[0] // 2
        self.hold[chunk] = partial[:rows]
        self.cs0[chunk] = partial[rows:].astype(BF)
        self.first[key] = self.net.copy(self.cs0.at[chunk], self.cr0.at[chunk], self.net.core)

    def far_send(self, key, chunk):
        self.first[key].wait_recv()
        self.ys[chunk] = (self.hold[chunk] + self.cr0[chunk].astype(F32)).astype(BF)
        self.second[key] = self.net.copy(self.ys.at[chunk], self.yr.at[chunk], self.net.far)

    def near_part(self, partial):
        rows = partial.shape[0] // 2
        self.total[...] = partial[:rows]
        self.cs1[...] = partial[rows:].astype(BF)
        self.near = self.net.copy(self.cs1, self.cr1, self.net.core)

    def near_done(self):
        self.near.wait_recv()
        self.total[...] += self.cr1[...].astype(F32)

    def result(self, key, chunk):
        self.second[key].wait_recv()
        return self.total[chunk] + self.yr[chunk].astype(F32)


def blocked(value):
    return value.astype(BF).reshape(2, value.shape[0] // 2, value.shape[1])


def chunks_of(rows, count):
    step = rows // count
    return [pl.ds(index * step, step) for index in range(count)]


def weight_grad(left, right, out, extra=None):
    width = left.shape[2]
    tile = 384

    def one(index, carry):
        columns = pl.ds(pl.multiple_of(index * tile, tile), tile)
        result = dot(flat(left[:, :, columns]), flat(right[...]), TN)
        if extra is None:
            out[columns, :] = result.astype(out.dtype)
        else:
            start = out.shape[1] - extra.shape[1]
            join = result.shape[1] - start
            added = extra[columns, :]
            out[columns, :start] = result[:, :start].astype(out.dtype)
            both = result[:, start:] + added[:, :join].astype(F32)
            out[columns, start : start + join] = both.astype(out.dtype)
            out[columns, start + join :] = added[:, join:]
        return carry

    lax.fori_loop(0, width // tile, one, 0)


def project_kernel(*refs, layer, head_cols, factor, parts):
    (x_hbm, vec, bias, *mixed_hbm), outs, scratch = split_refs(refs, 3 + parts, 4)
    normed_out, queries_out, pairs_out, far_out = outs
    x, weight, normed, queries, pairs, far_pairs, send_sems, recv_sems, move_sems = scratch
    net, moves = Net(send_sems, recv_sems), Moves(move_sems)
    rows = x.shape[0]
    pair_cols = 2 * head_cols
    chunks = chunks_of(rows, 2)
    x_load = moves.load(x_hbm, x)
    columns = pl.ds(0, weight.shape[1])
    weight_load = load_weight(net, moves, mixed_hbm, columns, weight)
    net.barrier([net.core, net.far, net.half])
    x_load.wait()
    sent = []
    for chunk in chunks:
        scaled, _ = norm_parts(x[chunk, :])
        normed[0, chunk, :] = (scaled * vec[layer, 0:1] + vec[layer, 1:2]).astype(BF)
        sent.append(gather_send(net, normed, chunk))
    arrived = []
    weight_load.wait()

    def project(slots, chunk):
        result = dot(flat(normed[slots, chunk, :]), weight[...]) + bias[layer : layer + 1]
        shape = (slots.size, chunk.size, -1)
        pairs[slots, chunk, :] = result[:, :pair_cols].astype(BF).reshape(shape)
        own = result[:, pair_cols : pair_cols + head_cols] * factor
        queries[slots, chunk, :] = own.astype(BF).reshape(shape)
        source, target = pairs.at[slots, chunk], far_pairs.at[slots, chunk]
        arrived.append(net.copy(source, target, net.half))

    whole = pl.ds(0, rows)
    project(pl.ds(0, 1), whole)
    for near, _ in sent:
        near.wait_recv()
    project(pl.ds(1, 1), whole)
    for chunk, (_, far) in zip(chunks, sent):
        gather_pass(net, normed, chunk, far).wait_recv()
        project(pl.ds(2, 2), chunk)
    moves.store(normed, normed_out)
    moves.store(queries, queries_out)
    moves.store(pairs, pairs_out)
    for one in arrived:
        one.wait_recv()
    moves.store(far_pairs, far_out)
    net.finish()
    moves.finish()


def project(layer, x, vec, bias, mixed, head_cols):
    rows, width = x.shape
    used = bias.shape[1]
    outputs = [
        ((4, rows, width), BF, False),
        ((4, rows, head_cols), BF, False),
        ((4, rows, 2 * head_cols), BF, False),
        ((4, rows, 2 * head_cols), BF, False),
    ]
    scratch = [pltpu.VMEM((rows, width), F32), pltpu.VMEM((width, used), BF)]
    scratch += [pltpu.VMEM(shape, dtype) for shape, dtype, _ in outputs]
    kernel = functools.partial(
        project_kernel,
        layer=layer,
        head_cols=head_cols,
        factor=HEAD_DIM ** (-0.5) * LOG2E,
        parts=len(mixed),
    )
    inputs = [(x, False), (vec, True), (bias, True)] + spaced(mixed)
    return run(kernel, "project", 40, inputs, outputs, scratch, 8 * layer, 12, 6 + weight_loads(mixed))


def pair_windows(width, lead=0):
    windows = []
    for first in range(lead, width - HEAD_DIM, 2 * HEAD_DIM):
        start = first // LANES * LANES
        size = min(2 * LANES, width - start)
        row = lax.broadcasted_iota(jnp.int32, (size, 2 * LANES), 0) + (start - first)
        lane = lax.broadcasted_iota(jnp.int32, (size, 2 * LANES), 1)
        second = lane >= LANES
        lane = jnp.where(second, lane - LANES, lane)
        match = row == jnp.where(second, lane + HEAD_DIM, lane)
        windows.append((start, size, jnp.logical_and(match, lane < HEAD_DIM).astype(BF)))
    return windows


def spread_heads(value, windows):
    heads = []
    for start, size, pick in windows:
        both = dot(value[:, start : start + size], pick).astype(BF)
        heads += [both[:, :LANES], both[:, LANES:]]
    return heads


def join_heads(heads, windows, width):
    tiles = [None] * (-(-width // LANES))
    for index, (start, size, pick) in enumerate(windows):
        both = jnp.concatenate(heads[2 * index : 2 * index + 2], axis=1)
        part = dot(both, pick, NT)
        for lane in range(0, size, LANES):
            tile, piece = (start + lane) // LANES, part[:, lane : lane + LANES]
            tiles[tile] = piece if tiles[tile] is None else tiles[tile] + piece
    return jnp.concatenate(tiles, axis=1)


def as_rows(columns):
    rows = columns[0].shape[0]
    lane = lax.broadcasted_iota(jnp.int32, (rows, LANES), 1)
    together = jnp.zeros((rows, LANES), F32)
    for head, column in enumerate(columns):
        together = jnp.where(lane == head, column, together)
    return together.T[:8]


def load_pairs(meta, own_pairs, far_pairs, key_scratch, value_scratch, heads):
    rows = own_pairs.shape[1]
    hid, half = meta[0], meta[1]
    windows = pair_windows(own_pairs.shape[2])
    for which, source in ((0, own_pairs), (1, far_pairs)):
        for slot in range(4):
            place = jnp.bitwise_xor(half, which) * 4 + jnp.bitwise_xor(hid, slot)
            start = pl.ds(pl.multiple_of(place * rows, rows), rows)
            spread = spread_heads(source[slot], windows)
            for head in range(heads):
                key_scratch[head, start, :] = spread[head]
                value_scratch[head, start, :] = spread[heads + head]


def attend_kernel(
    meta, queries, own_pairs, far_pairs, query_ids, key_ids, mixture, logsum,
    key_scratch, value_scratch, score_scratch, high_scratch, total_scratch, sum_scratch, query_scratch,
    *, heads
):
    rows = queries.shape[1]
    head_cols = heads * HEAD_DIM
    load_pairs(meta, own_pairs, far_pairs, key_scratch, value_scratch, heads)
    query_windows = pair_windows(head_cols)
    mixed_windows = pair_windows(mixture.shape[2], mixture.shape[2] - head_cols)

    def one_block(block, carry):
        slot = jnp.bitwise_xor(meta[0], block)
        first, last = meta[2 + 2 * block], meta[3 + 2 * block]
        own = pl.ds(pl.multiple_of(block * rows, rows), rows)
        ids = query_ids[own, :]
        for head, query in enumerate(spread_heads(queries[slot], query_windows)):
            query_scratch[head] = query
        high_scratch[...] = jnp.full_like(high_scratch, -3e38)
        sum_scratch[...] = jnp.zeros_like(sum_scratch)
        total_scratch[...] = jnp.zeros_like(total_scratch)

        def scores_of(key_block, inner):
            keys = pl.ds(pl.multiple_of(key_block * KEYS, KEYS), KEYS)
            same = ids == key_ids[:, keys]
            for head in range(heads):
                scores = dot(query_scratch[head], key_scratch[head, keys, :], NT)
                scores = jnp.where(same, scores, MASKED)
                score_scratch[head, :, keys] = scores
                high = high_scratch[head]
                for lane in range(0, KEYS, LANES):
                    high = jnp.maximum(high, scores[:, lane : lane + LANES])
                high_scratch[head] = high
            return inner

        lax.fori_loop(first, last, scores_of, 0)
        for head in range(heads):
            high_scratch[head] = jnp.broadcast_to(
                jnp.max(high_scratch[head], axis=1, keepdims=True), (rows, LANES)
            )

        def sums_of(key_block, inner):
            keys = pl.ds(pl.multiple_of(key_block * KEYS, KEYS), KEYS)
            for head in range(heads):
                high = high_scratch[head]
                high = jnp.concatenate([high] * (KEYS // LANES), axis=1)
                powers = jnp.exp2(score_scratch[head, :, keys] - high)
                total = total_scratch[head]
                for lane in range(0, KEYS, LANES):
                    total += powers[:, lane : lane + LANES]
                total_scratch[head] = total
                sum_scratch[head] += dot(powers.astype(BF), value_scratch[head, keys, :])
            return inner

        lax.fori_loop(first, last, sums_of, 0)
        mixed, columns = [], []
        for head in range(heads):
            total = jnp.sum(total_scratch[head], axis=1, keepdims=True)
            columns.append(high_scratch[head][:, :1] + jnp.log2(total))
            mixed.append((sum_scratch[head] / total).astype(BF))
        mixture[slot] = join_heads(mixed, mixed_windows, mixture.shape[2]).astype(BF)
        logsum[:, own] = as_rows(columns)
        return carry

    lax.fori_loop(0, 4, one_block, 0)


def attend(meta, queries, own_pairs, far_pairs, query_ids, key_ids, lead):
    _, rows, head_cols = queries.shape
    heads = head_cols // HEAD_DIM
    own, count = 4 * rows, 8 * rows
    space = pl.BlockSpec(memory_space=pltpu.VMEM)
    return pl.pallas_call(
        functools.partial(attend_kernel, heads=heads),
        name="attend",
        cost_estimate=micros(22),
        out_shape=[
            jax.ShapeDtypeStruct((4, rows, lead + head_cols), BF),
            jax.ShapeDtypeStruct((8, own), F32),
        ],
        in_specs=[pl.BlockSpec(memory_space=pltpu.SMEM)] + [space] * 5,
        out_specs=[space] * 2,
        scratch_shapes=[
            pltpu.VMEM((heads, count, LANES), BF),
            pltpu.VMEM((heads, count, LANES), BF),
            pltpu.VMEM((heads, rows, count), F32),
            pltpu.VMEM((heads, rows, LANES), F32),
            pltpu.VMEM((heads, rows, LANES), F32),
            pltpu.VMEM((heads, rows, LANES), F32),
            pltpu.VMEM((heads, rows, LANES), BF),
        ],
        compiler_params=pltpu.CompilerParams(vmem_limit_bytes=VMEM_LIMIT),
    )(meta, queries, own_pairs, far_pairs, query_ids, key_ids)


def attend_back_kernel(
    meta, queries, own_pairs, far_pairs, query_ids, key_ids, grad_mixture, logsum,
    grad_queries, grad_own, grad_far,
    key_scratch, value_scratch, grad_key, grad_value, grad_query, query_scratch, grad_scratch,
    prob_scratch, grad_prob_scratch, delta_scratch,
    *, heads
):
    rows = queries.shape[1]
    head_cols = heads * HEAD_DIM
    load_pairs(meta, own_pairs, far_pairs, key_scratch, value_scratch, heads)
    query_windows = pair_windows(head_cols)
    mixed_windows = pair_windows(grad_mixture.shape[2], grad_mixture.shape[2] - head_cols)
    grad_key[...] = jnp.zeros_like(grad_key)
    grad_value[...] = jnp.zeros_like(grad_value)

    def one_block(block, carry):
        slot = jnp.bitwise_xor(meta[0], block)
        first, last = meta[2 + 2 * block], meta[3 + 2 * block]
        own = pl.ds(pl.multiple_of(block * rows, rows), rows)
        ids = query_ids[:, own]
        for head, query in enumerate(spread_heads(queries[slot], query_windows)):
            query_scratch[head] = query
        for head, grad in enumerate(spread_heads(grad_mixture[slot], mixed_windows)):
            grad_scratch[head] = grad
        logs = logsum[:, own]
        grad_query[...] = jnp.zeros_like(grad_query)
        delta_scratch[...] = jnp.zeros_like(delta_scratch)

        def probs_of(key_block, inner):
            keys = pl.ds(pl.multiple_of(key_block * KEYS, KEYS), KEYS)
            same = key_ids[keys, :] == ids
            for head in range(heads):
                grad = grad_scratch[head]
                scores = dot(key_scratch[head, keys, :], query_scratch[head], NT)
                probs = jnp.where(same, jnp.exp2(scores - logs[head : head + 1]), 0.0)
                grad_probs = dot(value_scratch[head, keys, :], grad, NT)
                prob_scratch[head, keys, :] = probs
                grad_prob_scratch[head, keys, :] = grad_probs
                delta_scratch[head] += jnp.sum((probs * grad_probs).reshape(KEYS // 8, 8, rows), axis=0)
                grad_value[head, keys, :] += dot(probs.astype(BF), grad)
            return inner

        lax.fori_loop(first, last, probs_of, 0)
        for head in range(heads):
            delta_scratch[head, 0:1] = jnp.sum(delta_scratch[head], axis=0, keepdims=True)

        def one_key(key_block, inner):
            keys = pl.ds(pl.multiple_of(key_block * KEYS, KEYS), KEYS)
            for head in range(heads):
                delta = delta_scratch[head, 0:1]
                grad_scores = prob_scratch[head, keys, :] * (grad_prob_scratch[head, keys, :] - delta)
                grad_scores = grad_scores.astype(BF)
                grad_key[head, keys, :] += dot(grad_scores, query_scratch[head])
                grad_query[head] += dot(grad_scores, key_scratch[head, keys, :], TN)
            return inner

        lax.fori_loop(first, last, one_key, 0)
        scaled = [(grad_query[head] * HEAD_DIM ** (-0.5)).astype(BF) for head in range(heads)]
        grad_queries[slot] = join_heads(scaled, query_windows, head_cols).astype(BF)
        return carry

    lax.fori_loop(0, 4, one_block, 0)
    hid, half = meta[0], meta[1]
    for which, target in ((0, grad_own), (1, grad_far)):
        for slot in range(4):
            place = jnp.bitwise_xor(half, which) * 4 + jnp.bitwise_xor(hid, slot)
            start = pl.ds(pl.multiple_of(place * rows, rows), rows)
            parts = [(grad_key[head, start, :] * LN2).astype(BF) for head in range(heads)]
            parts += [grad_value[head, start, :].astype(BF) for head in range(heads)]
            target[slot] = join_heads(parts, pair_windows(2 * head_cols), 2 * head_cols).astype(BF)


def attend_back(meta, queries, own_pairs, far_pairs, query_ids, key_ids, grad_mixture, logsum):
    _, rows, head_cols = queries.shape
    heads = head_cols // HEAD_DIM
    count = 8 * rows
    space = pl.BlockSpec(memory_space=pltpu.VMEM)
    return pl.pallas_call(
        functools.partial(attend_back_kernel, heads=heads),
        name="attend_back",
        cost_estimate=micros(37),
        out_shape=[
            jax.ShapeDtypeStruct((4, rows, head_cols), BF),
            jax.ShapeDtypeStruct((4, rows, 2 * head_cols), BF),
            jax.ShapeDtypeStruct((4, rows, 2 * head_cols), BF),
        ],
        in_specs=[pl.BlockSpec(memory_space=pltpu.SMEM)] + [space] * 7,
        out_specs=[space] * 3,
        scratch_shapes=[
            pltpu.VMEM((heads, count, LANES), BF),
            pltpu.VMEM((heads, count, LANES), BF),
            pltpu.VMEM((heads, count, LANES), F32),
            pltpu.VMEM((heads, count, LANES), F32),
            pltpu.VMEM((heads, rows, LANES), F32),
            pltpu.VMEM((heads, rows, LANES), BF),
            pltpu.VMEM((heads, rows, LANES), BF),
            pltpu.VMEM((heads, count, rows), F32),
            pltpu.VMEM((heads, count, rows), F32),
            pltpu.VMEM((heads, 8, rows), F32),
        ],
        compiler_params=pltpu.CompilerParams(vmem_limit_bytes=VMEM_LIMIT),
    )(meta, queries, own_pairs, far_pairs, query_ids, key_ids, grad_mixture, logsum)


def mlp_kernel(*refs, layer, parts):
    ins, outs, scratch = split_refs(refs, 4 + sum(parts), 5)
    mixture_hbm, x_hbm, vec, up_bias = ins[:4]
    mixed_hbm, up_hbm, down_hbm = split_refs(ins[4:], parts[0], parts[1])
    x_out, after_out, normed_out, active_out, slope_out = outs
    mixture, x, out_weight, up_weight, down_weight, x_next, after, normed, active, slope = scratch[:10]
    first_scratch, second_scratch = scratch[10:18], scratch[18:26]
    send_sems, recv_sems, move_sems = scratch[26:]
    net, moves = Net(send_sems, recv_sems), Moves(move_sems)
    rows = x.shape[0]
    hidden_cols = up_weight.shape[1]
    out_cols = out_weight.shape[1]
    chunks = chunks_of(rows, 2)
    out_part = pl.ds(x.shape[1] - out_cols, out_cols)
    loads = [
        moves.load(mixture_hbm, mixture), load_weight(net, moves, mixed_hbm, out_part, out_weight),
    ]
    x_load = moves.load(x_hbm, x)
    up_load = load_weight(net, moves, up_hbm, pl.ds(0, hidden_cols), up_weight)
    down_load = load_weight(net, moves, down_hbm, pl.ds(0, hidden_cols), down_weight)
    net.barrier([net.core, net.far])
    out_bias, gain = vec[layer, 2:3], vec[layer, 3:4]
    shift, down_bias = vec[layer, 4:5], vec[layer, 5:6]

    def mixed(slots, chunk):
        return dot(flat(mixture[slots, chunk, :]), out_weight[...], NT)

    def up(slots, chunk):
        hidden = dot(flat(normed[slots, chunk, :]), up_weight[...]) + up_bias[layer : layer + 1]
        square = hidden * hidden
        bend = jnp.tanh(GELU * hidden * (1.0 + CUBE * square))
        half = 0.5 * (1.0 + bend)
        value = hidden * half
        rise = half + 0.5 * hidden * (1.0 - bend * bend) * GELU * (1.0 + 3.0 * CUBE * square)
        active[slots, chunk, :] = blocked(value)
        slope[slots, chunk, :] = blocked(rise)

    def down(slots, chunk):
        return dot(flat(active[slots, chunk, :]), down_weight[...], NT)

    near, far, whole = pl.ds(0, 2), pl.ds(2, 2), pl.ds(0, rows)
    for load in loads:
        load.wait()
    first = Scatter(net, first_scratch)
    for key, chunk in enumerate(chunks):
        first.far_part(key, chunk, mixed(far, chunk))
    for key, chunk in enumerate(chunks):
        first.far_send(key, chunk)
    first.near_part(mixed(near, whole))
    first.near_done()
    x_load.wait()
    sent = []
    for key, chunk in enumerate(chunks):
        residual = first.result(key, chunk) + x[chunk, :] + out_bias
        after[chunk, :] = residual
        normed[0, chunk, :] = (norm_parts(residual)[0] * gain + shift).astype(BF)
        sent.append(gather_send(net, normed, chunk))
    moves.store(after, after_out)
    for one, _ in sent:
        one.wait_recv()
    up_load.wait()
    up(near, whole)
    down_load.wait()
    second = Scatter(net, second_scratch)
    for key, chunk in enumerate(chunks):
        passed = gather_pass(net, normed, chunk, sent[key][1])
        passed.wait_recv()
        up(far, chunk)
        second.far_part(key, chunk, down(far, chunk))
        second.far_send(key, chunk)
    moves.store(normed, normed_out)
    moves.store(active, active_out)
    moves.store(slope, slope_out)
    second.near_part(down(near, whole))
    second.near_done()
    for key, chunk in enumerate(chunks):
        x_next[chunk, :] = second.result(key, chunk) + after[chunk, :] + down_bias
    moves.store(x_next, x_out)
    net.finish()
    moves.finish()


def mlp(layer, mixture, x, vec, up_bias, mixed, up, down):
    rows, width = x.shape
    hidden = up_bias.shape[1]
    outputs = [
        ((rows, width), F32, False),
        ((rows, width), F32, False),
        ((4, rows, width), BF, False),
        ((4, rows, hidden), BF, False),
        ((4, rows, hidden), BF, False),
    ]
    scratch = [
        pltpu.VMEM(mixture.shape, BF),
        pltpu.VMEM((rows, width), F32),
        pltpu.VMEM((width, mixture.shape[2]), BF),
        pltpu.VMEM((width, hidden), BF),
        pltpu.VMEM((width, hidden), BF),
    ]
    scratch += [pltpu.VMEM(shape, dtype) for shape, dtype, _ in outputs]
    scratch += scatter_scratch(rows, width) * 2
    inputs = [(mixture, False), (x, False), (vec, True), (up_bias, True)]
    inputs += spaced(mixed + up + down)
    parts = (len(mixed), len(up), len(down))
    kernel = functools.partial(mlp_kernel, layer=layer, parts=parts)
    moves = 8 + weight_loads(mixed) + weight_loads(up) + weight_loads(down)
    return run(kernel, "mlp", 48, inputs, outputs, scratch, 8 * layer + 1, 18, moves)


def mlp_back_kernel(*refs, layer, parts):
    ins, outs, scratch = split_refs(refs, 7 + sum(parts), 7)
    gradient_hbm, after_hbm, vec, mixture_hbm, normed_hbm, active_hbm, slope_hbm = ins[:7]
    mixed_hbm, up_hbm, down_hbm = split_refs(ins[7:], parts[0], parts[1])
    after_out, mixture_out, up_out, down_out, out_out, sums, hidden_sums = outs
    gradient, after, out_weight, up_weight, down_weight, mixture, normed, active, slope = scratch[:9]
    grad_after, grad_mixture, grad_down, grad_up, grad_out = scratch[9:14]
    grad_rows, grad_hidden, grad_mid = scratch[14:17]
    scatter_refs = scratch[17:25]
    send_sems, recv_sems, move_sems = scratch[25:]
    net, moves = Net(send_sems, recv_sems), Moves(move_sems)
    rows, width = gradient.shape
    hidden_cols = up_weight.shape[1]
    out_cols = out_weight.shape[1]
    chunks = chunks_of(rows, 2)
    out_part = pl.ds(width - out_cols, out_cols)
    load_gradient = moves.load(gradient_hbm, gradient)
    load_down = load_weight(net, moves, down_hbm, pl.ds(0, hidden_cols), down_weight)
    load_slope = moves.load(slope_hbm, slope)
    load_up = load_weight(net, moves, up_hbm, pl.ds(0, hidden_cols), up_weight)
    load_active = moves.load(active_hbm, active)
    load_after = moves.load(after_hbm, after)
    load_normed = moves.load(normed_hbm, normed)
    load_out = load_weight(net, moves, mixed_hbm, out_part, out_weight)
    load_mixture = moves.load(mixture_hbm, mixture)
    net.barrier([net.core, net.far])
    gain = vec[layer, 3:4]
    near, far, whole = pl.ds(0, 2), pl.ds(2, 2), pl.ds(0, rows)
    load_gradient.wait()
    rounded = gradient[...].astype(BF)
    grad_rows[0] = rounded
    sent = [gather_send(net, grad_rows, chunk) for chunk in chunks]
    sums[...] = jnp.zeros_like(sums)
    sums[5:6] = jnp.sum(rounded.astype(F32), axis=0, keepdims=True)

    def hidden_grad(slots, chunk):
        value = dot(flat(grad_rows[slots, chunk, :]), down_weight[...])
        value = value * flat(slope[slots, chunk, :]).astype(F32)
        grad_hidden[slots, chunk, :] = blocked(value)

    def up_back(slots, chunk):
        return dot(flat(grad_hidden[slots, chunk, :]), up_weight[...], NT)

    for one, _ in sent:
        one.wait_recv()
    load_down.wait()
    load_slope.wait()
    hidden_grad(near, whole)
    load_up.wait()
    scatter = Scatter(net, scatter_refs)
    for key, chunk in enumerate(chunks):
        passed = gather_pass(net, grad_rows, chunk, sent[key][1])
        passed.wait_recv()
        hidden_grad(far, chunk)
        scatter.far_part(key, chunk, up_back(far, chunk))
        scatter.far_send(key, chunk)
    scatter.near_part(up_back(near, whole))
    load_active.wait()
    weight_grad(grad_rows, active, grad_down)
    moves.store(grad_down, down_out)
    scatter.near_done()
    load_after.wait()
    sent = []
    for key, chunk in enumerate(chunks):
        back, gain_sum, shift_sum = norm_back(after[chunk, :], gain, scatter.result(key, chunk))
        total = gradient[chunk, :] + back
        grad_after[chunk, :] = total
        rounded = total.astype(BF)
        grad_mid[0, chunk, :] = rounded
        sent.append(gather_send(net, grad_mid, chunk))
        sums[3:4] += gain_sum
        sums[4:5] += shift_sum
        sums[2:3] += jnp.sum(rounded.astype(F32), axis=0, keepdims=True)
    moves.store(grad_after, after_out)
    load_normed.wait()
    weight_grad(normed, grad_hidden, grad_up)
    moves.store(grad_up, up_out)
    column = jnp.zeros((1, hidden_cols), F32)
    for slot in range(4):
        column += jnp.sum(grad_hidden[slot].astype(F32), axis=0, keepdims=True)
    hidden_sums[...] = column

    def mix_back(slots, chunk):
        value = dot(flat(grad_mid[slots, chunk, :]), out_weight[...])
        grad_mixture[slots, chunk, :] = blocked(value)

    for one, _ in sent:
        one.wait_recv()
    load_out.wait()
    mix_back(near, whole)
    for key, chunk in enumerate(chunks):
        gather_pass(net, grad_mid, chunk, sent[key][1]).wait_recv()
    mix_back(far, whole)
    moves.store(grad_mixture, mixture_out)
    load_mixture.wait()
    weight_grad(grad_mid, mixture, grad_out)
    moves.store(grad_out, out_out)
    net.finish()
    moves.finish()


def mlp_back(layer, gradient, after, vec, mixed, up, down, mixture, normed, active, slope):
    rows, width = gradient.shape
    hidden = active.shape[2]
    out_cols = mixture.shape[2]
    outputs = [
        ((rows, width), F32, False),
        ((4, rows, out_cols), BF, False),
        ((width, hidden), BF, False),
        ((width, hidden), BF, False),
        ((width, out_cols), BF, False),
        ((8, width), F32, True),
        ((1, hidden), F32, True),
    ]
    shapes = [
        ((rows, width), F32),
        ((rows, width), F32),
        ((width, out_cols), BF),
        ((width, hidden), BF),
        ((width, hidden), BF),
        ((4, rows, out_cols), BF),
        ((4, rows, width), BF),
        ((4, rows, hidden), BF),
        ((4, rows, hidden), BF),
        ((rows, width), F32),
        ((4, rows, out_cols), BF),
        ((width, hidden), BF),
        ((width, hidden), BF),
        ((width, out_cols), BF),
        ((4, rows, width), BF),
        ((4, rows, hidden), BF),
        ((4, rows, width), BF),
    ]
    scratch = [pltpu.VMEM(shape, dtype) for shape, dtype in shapes] + scatter_scratch(rows, width)
    inputs = [
        (gradient, False), (after, False), (vec, True), (mixture, False), (normed, False),
        (active, False), (slope, False),
    ] + spaced(mixed + up + down)
    parts = (len(mixed), len(up), len(down))
    kernel = functools.partial(mlp_back_kernel, layer=layer, parts=parts)
    moves = 12 + weight_loads(mixed) + weight_loads(up) + weight_loads(down)
    return run(kernel, "mlp_back", 48, inputs, outputs, scratch, 8 * layer + 2, 20, moves)


def project_back_kernel(*refs, layer, parts):
    ins, outs, scratch = split_refs(refs, 8 + parts, 4)
    after_hbm, x_hbm, vec, normed_hbm, queries_hbm, own_hbm, far_hbm, out_hbm = ins[:8]
    mixed_hbm = ins[8:]
    gradient_out, weight_out, sums, column_sums = outs
    grad_after, x, weight, normed, grad_queries, grad_own, grad_out = scratch[:7]
    landed, together, gradient, grad_weight = scratch[7:11]
    scatter_refs = scratch[11:19]
    send_sems, recv_sems, move_sems = scratch[19:]
    net, moves = Net(send_sems, recv_sems), Moves(move_sems)
    rows, width = x.shape
    pair_cols = grad_own.shape[2]
    used_cols = pair_cols + grad_queries.shape[2]
    all_cols = together.shape[2]
    chunks = chunks_of(rows, 2)
    near, far, whole = pl.ds(0, 2), pl.ds(2, 2), pl.ds(0, rows)
    load_own = moves.load(own_hbm, grad_own)
    load_queries = moves.load(queries_hbm, grad_queries)
    loading = load_weight(net, moves, mixed_hbm, pl.ds(0, all_cols), weight)
    load_normed = moves.load(normed_hbm, normed)
    load_out = moves.load(out_hbm, grad_out)
    load_x = moves.load(x_hbm, x)
    load_after = moves.load(after_hbm, grad_after)
    net.barrier([net.core, net.far, net.half])
    arriving = {
        slot: net.copy(far_hbm.at[slot], landed.at[slot], net.half) for slot in (3, 2, 1, 0)
    }
    load_queries.wait()
    together[:, :, pair_cols:used_cols] = grad_queries[...]
    together[:, :, used_cols:] = jnp.zeros((4, rows, all_cols - used_cols), BF)
    load_own.wait()
    loading.wait()

    def join(slot):
        arriving[slot].wait_recv()
        pair = grad_own[slot].astype(F32) + landed[slot].astype(F32)
        together[slot, :, :pair_cols] = pair.astype(BF)

    def back(slots, chunk):
        return dot(flat(together[slots, chunk, :]), weight[...], NT)

    scatter = Scatter(net, scatter_refs)
    join(3)
    join(2)
    for key, chunk in enumerate(chunks):
        scatter.far_part(key, chunk, back(far, chunk))
    for key, chunk in enumerate(chunks):
        scatter.far_send(key, chunk)
    join(1)
    join(0)
    scatter.near_part(back(near, whole))
    load_normed.wait()
    load_out.wait()
    weight_grad(normed, together, grad_weight, grad_out)
    moves.store(grad_weight, weight_out)
    column = jnp.zeros((1, all_cols), F32)
    for slot in range(4):
        column += jnp.sum(together[slot].astype(F32), axis=0, keepdims=True)
    column_sums[...] = column
    scatter.near_done()
    sums[...] = jnp.zeros_like(sums)
    load_x.wait()
    load_after.wait()
    for key, chunk in enumerate(chunks):
        grad, gain_sum, shift_sum = norm_back(
            x[chunk, :], vec[layer, 0:1], scatter.result(key, chunk)
        )
        gradient[chunk, :] = grad_after[chunk, :] + grad
        sums[0:1] += gain_sum
        sums[1:2] += shift_sum
    moves.store(gradient, gradient_out)
    net.finish()
    moves.finish()


def project_back(
    layer, grad_after, x, vec, mixed, normed, grad_queries, grad_own, grad_far, grad_out, all_cols
):
    rows, width = x.shape
    outputs = [
        ((rows, width), F32, False),
        ((width, width), BF, False),
        ((8, width), F32, True),
        ((1, all_cols), F32, True),
    ]
    shapes = [
        ((rows, width), F32),
        ((rows, width), F32),
        ((width, all_cols), BF),
        (normed.shape, BF),
        (grad_queries.shape, BF),
        (grad_own.shape, BF),
        (grad_out.shape, BF),
        (grad_far.shape, BF),
        ((4, rows, all_cols), BF),
        ((rows, width), F32),
        ((width, width), BF),
    ]
    scratch = [pltpu.VMEM(shape, dtype) for shape, dtype in shapes] + scatter_scratch(rows, width)
    inputs = [
        (grad_after, False), (x, False), (vec, True), (normed, False), (grad_queries, False),
        (grad_own, False), (grad_far, False), (grad_out, False),
    ] + spaced(mixed)
    kernel = functools.partial(project_back_kernel, layer=layer, parts=len(mixed))
    return run(kernel, "project_back", 42, inputs, outputs, scratch, 8 * layer + 3, 12, 9 + weight_loads(mixed))


def entry_kernel(*refs):
    (tokens, cotangent, vectors, shard), outs, scratch = split_refs(refs, 4, 4)
    tokens_out, cotangent_out, vectors_out, weights = outs
    send_sems, recv_sems, move_sems = scratch
    net, moves = Net(send_sems, recv_sems), Moves(move_sems)
    others = [net.core, net.far, net.far_core]
    net.line(weights.shape[0] // 2)
    net.barrier(others + [net.half], True)
    gathering = GatherJob(net, moves, shard, weights)
    moved = []
    for source, target in ((tokens, tokens_out), (cotangent, cotangent_out)):
        for device in reversed(others):
            moved.append(net.copy(source.at[device[1]], target.at[net.hid], device))
        target[net.hid] = source[net.hid]
    for device in others:
        moved.append(net.copy(vectors, vectors_out.at[net.hid], device))
    vectors_out[net.hid] = vectors[...]
    gathering.forward(0, 1)
    gathering.finish()
    for one in moved:
        one.wait_recv()
    net.finish()
    moves.finish()


def entry(tokens, cotangent, vectors, shard, count):
    inputs = [(tokens, True), (cotangent, True), (vectors, True), (shard, False)]
    outputs = [
        (tokens.shape, BF, True),
        (cotangent.shape, BF, True),
        ((4,) + vectors.shape, F32, True),
        ((count,) + shard.shape, BF, False),
    ]
    return run(entry_kernel, "entry", 40, inputs, outputs, [], 4, 9 + job_copies(count), 1)


def finish_kernel(*refs):
    (final, gradient, wide, narrow, broad, grads), outs, scratch = split_refs(refs, 6, 5)
    final_out, gradient_out, sums, hidden_sums, total = outs
    final_land, gradient_land, wide_land, across_land, along_land = scratch[:5]
    across_hidden, along_hidden = scratch[5:7]
    job_refs = scratch[7:11]
    send_sems, recv_sems, move_sems = scratch[11:]
    net, moves = Net(send_sems, recv_sems), Moves(move_sems)
    count = grads.shape[0] // 2
    others = [net.core, net.far, net.far_core]
    net.line(count)
    net.barrier(others + [net.half], True)
    summed = [net.copy(wide.at[device[1]], wide_land.at[net.hid], device) for device in others]
    scattering = ScatterParts(net, moves, grads, job_refs)
    moved = []
    for source, target in ((final, final_land), (gradient, gradient_land)):
        for device in reversed(others):
            moved.append(net.copy(source.at[device[1]], target.at[net.hid], device))
        target[net.hid] = source[net.hid]
    wide_land[net.hid] = wide[net.hid]
    last = count - 1
    pairs = ((sums, across_land, along_land), (hidden_sums, across_hidden, along_hidden))
    bases = [(net.take(count), net.take(count)) for _ in pairs]

    def send_sums():
        for one in summed:
            one.wait_recv()
        top = wide.shape[1]
        sums[:top] = wide_land[0] + wide_land[1] + wide_land[2] + wide_land[3]
        sums[top:] = narrow[...]
        hidden_sums[...] = broad[...]
        return [net.copy(value, across, net.half) for value, across, _ in pairs]

    def spread_sums(swaps):
        for one in swaps:
            one.wait()
        for (value, across, along), base in zip(pairs, bases):
            value[...] += across[...]
            own = along.at[net.high]
            along[net.high] = value[...]
            pl.when(net.has_after)(net.make(base[0], own, own, net.after).start)
            pl.when(net.has_before)(net.make(base[1], own, own, net.before).start)

    def pass_sums(step):
        for (_, _, along), base in zip(pairs, bases):
            below, above = along.at[net.high - step], along.at[net.high + step]

            def pass_on(index, block, device, has):
                net.make(index, block, block, device).wait_recv()
                if step < last:
                    pl.when(has)(net.make(index + 1, block, block, device).start)

            pl.when(net.high >= step)(
                functools.partial(pass_on, base[0] + step - 1, below, net.after, net.has_after)
            )
            pl.when(net.high + step < count)(
                functools.partial(pass_on, base[1] + step - 1, above, net.before, net.has_before)
            )

    swaps = send_sums()
    scattering.forward(0, 3)
    scattering.forward(1, 3)
    spread_sums(swaps)
    scattering.forward(2, 3)
    for step in range(1, count):
        pass_sums(step)
    for (value, _, along), base in zip(pairs, bases):
        total_value = along[0]
        for place in range(1, count):
            total_value += along[place]
        value[...] = total_value
        own = along.at[net.high]
        for step in range(count - 1):
            up = jnp.logical_and(net.has_after, net.high >= step)
            down = jnp.logical_and(net.has_before, net.high + step < count)
            pl.when(up)(net.make(base[0] + step, own, own, net.after).wait_send)
            pl.when(down)(net.make(base[1] + step, own, own, net.before).wait_send)
    for one in moved:
        one.wait_recv()
    for source, target in ((final_land, final_out), (gradient_land, gradient_out)):
        target[...] = flat(source[...]).astype(F32)
    scattering.finish(total)
    net.finish(swaps)


def finish(final, gradient, wide, narrow, broad, grads):
    count = grads.shape[0] // 2
    sums = (wide.shape[1] + narrow.shape[0], wide.shape[2])
    rows = (final.shape[0] * final.shape[1], final.shape[2])
    outputs = [
        (rows, F32, True),
        (rows, F32, True),
        (sums, F32, True),
        (broad.shape, F32, True),
        (grads.shape[1:], F32, True),
    ]
    scratch = [
        pltpu.VMEM(final.shape, BF),
        pltpu.VMEM(final.shape, BF),
        pltpu.VMEM(wide.shape, F32),
        pltpu.VMEM(sums, F32),
        pltpu.VMEM((count,) + sums, F32),
        pltpu.VMEM(broad.shape, F32),
        pltpu.VMEM((count,) + broad.shape, F32),
    ] + part_scratch(*grads.shape)
    inputs = [
        (final, True), (gradient, True), (wide, True), (narrow, True), (broad, True), (grads, False),
    ]
    return run(
        finish_kernel, "finish", 40, inputs, outputs, scratch, 5, 12 + 7 * count, 1 + count
    )


def key_ranges(own_ids, row_ids, rows):
    blocks = own_ids.reshape(-1, rows)
    position = jnp.arange(row_ids.shape[0], dtype=jnp.int32)
    low = jnp.min(jnp.where(row_ids == blocks[:, :1], position, row_ids.shape[0]), axis=1)
    high = jnp.max(jnp.where(row_ids == blocks[:, -1:], position, -1), axis=1)
    return jnp.stack([low // KEYS, high // KEYS + 1], axis=1).reshape(-1)


def body(
    tokens, picture, cotangent, first_gain, first_shift, query_weight, query_bias, key_weight,
    value_weight, value_bias, output_weight, output_bias, second_gain, second_shift, up_weight,
    up_bias, down_weight, down_bias,
):
    token_count = tokens.shape[0]
    rows = token_count // 4
    layers = query_weight.shape[0]
    head_cols = query_bias.shape[1]
    feed = up_bias.shape[1]
    feed_pad = -feed % LANES
    feed_cols = feed + feed_pad
    hid = lax.axis_index("hid")
    tok = lax.axis_index("tok")
    count = lax.axis_size("tok")
    shard = query_weight.shape[1]
    shard_pad = -shard % 16
    width = count * shard
    lead = 3 * head_cols % LANES
    used_cols = 3 * head_cols + -3 * head_cols % LANES

    own_ids = lax.dynamic_slice_in_dim(picture, tok * token_count, token_count)
    row_ids = lax.dynamic_slice_in_dim(picture, (tok // 2) * 2 * token_count, 2 * token_count)
    place = jnp.stack([hid, tok % 2]).astype(jnp.int32)
    meta = jnp.concatenate([place, key_ranges(own_ids, row_ids, rows)])

    def side_by_side(*parts):
        return jnp.concatenate(parts, axis=1)

    def padded(part):
        return jnp.pad(part, ((0, 0), (0, feed_pad)))

    def shards(part):
        return jnp.pad(part, ((0, shard_pad), (0, 0)))

    def by_tokens(array):
        return array.transpose(1, 0, 2).reshape(rows, 4 * array.shape[2]).astype(F32)

    def by_features(array):
        return array.reshape(rows, 4, head_cols).transpose(1, 0, 2)

    def joined(gathered):
        return gathered[:, :shard].reshape(width, gathered.shape[2])

    def separate(grads):
        grads = grads.reshape(count, shard, grads.shape[1])
        return jnp.pad(grads, ((0, 0), (0, shard_pad), (0, 0)))

    mixed_parts = [
        shards(
            side_by_side(
                key_weight[layer], value_weight[layer], query_weight[layer], output_weight[layer].T
            )
        )
        for layer in range(layers)
    ]
    vectors = jnp.stack(
        [first_gain, first_shift, output_bias, second_gain, second_shift, down_bias], axis=1
    )
    vectors = jnp.pad(vectors, ((0, 0), (0, 2), (0, 0))).reshape(layers * 8, head_cols)
    x, gradient, vectors, mixed = entry(
        tokens.reshape(4, rows, head_cols),
        cotangent.reshape(4, rows, head_cols),
        vectors,
        mixed_parts[0],
        count,
    )
    x, gradient = by_tokens(x), by_tokens(gradient)
    vectors = vectors.transpose(1, 0, 2).reshape(layers, 8, width)
    bias = side_by_side(jnp.zeros_like(value_bias), value_bias, query_bias)
    bias = jnp.pad(bias, ((0, 0), (0, used_cols - 3 * head_cols)))
    up_bias = padded(up_bias)

    halves = [(place, place ^ 1) for place in range(count)]
    lines = [[place * 2 + low for place in range(count // 2)] for low in range(2)]

    def swap(part):
        return lax.ppermute(part, "tok", halves)

    def both_halves(own, other):
        first = tok % 2 == 0
        return jnp.stack([jnp.where(first, own, other), jnp.where(first, other, own)])

    def along(part):
        return lax.all_gather(part, "tok", axis=0, tiled=True, axis_index_groups=lines)

    def along_first(part):
        own = along(part)
        other = swap(own)
        parts = [rows_of.reshape(count // 2, shard, part.shape[1]) for rows_of in (own, other)]
        if shard % 16 == 0:
            return parts
        return [both_halves(*parts).transpose(1, 0, 2, 3).reshape(width, part.shape[1])]

    def across_first(part):
        pair = both_halves(part, swap(part)).reshape(2 * shard, part.shape[1])
        return along(pair)

    def up_part(layer):
        return padded(up_weight[layer])

    def down_part(layer):
        return padded(down_weight[layer].T)

    weights = [[[joined(mixed)], along_first(up_part(0)), [across_first(down_part(0))]]]
    for layer in range(1, layers):
        mixed = along_first(mixed_parts[layer][:shard])
        weights.append([mixed, [across_first(up_part(layer))], [across_first(down_part(layer))]])
    saved = []
    for layer in range(layers):
        mixed, up, down = weights[layer]
        normed, queries, own_pairs, far_pairs = project(layer, x, vectors, bias, mixed, head_cols)
        mixture, logsum = attend(
            meta, queries, own_pairs, far_pairs, own_ids[:, None], row_ids[None, :], lead
        )
        x_next, after, normed_two, active, slope = mlp(
            layer, mixture, x, vectors, up_bias, mixed, up, down
        )
        saved.append(
            (x, normed, queries, own_pairs, far_pairs, mixture, logsum, after, normed_two, active, slope)
        )
        x = x_next
    final = x

    def by_halves(part):
        own = lax.dynamic_index_in_dim(part, tok % 2, 1, keepdims=False)
        other = lax.dynamic_index_in_dim(part, 1 - tok % 2, 1, keepdims=False)
        return own, other

    def sum_along(part):
        return lax.psum_scatter(
            part, "tok", scatter_dimension=0, tiled=True, axis_index_groups=lines
        )

    def hold(*values):
        return lax.optimization_barrier(values)

    def halves_of(part):
        part = part.reshape(-1, 2, shard, part.shape[1])
        own, other = by_halves(part)
        return own, swap(other)

    def added(own, other):
        return (own.astype(F32) + other.astype(F32)).astype(BF)

    def in_rows(part):
        return part.reshape(-1, part.shape[-1])

    mixed_grads, up_grads, down_grads = [None] * layers, [None] * layers, [None] * layers
    wide, narrow, broad = [None] * layers, [None] * layers, [None] * layers
    grads = None
    for layer in reversed(range(layers)):
        x, normed, queries, own_pairs, far_pairs, mixture, logsum, after, normed_two, active, slope = saved[layer]
        mixed, up, down = weights[layer]
        last = layer + 1
        if last < layers:
            gradient, down_grad, up_grad = hold(gradient, down_grads[last], up_grads[last])
            up_grads[last] = sum_along(in_rows(up_grad))
            mixed_own, mixed_other = halves_of(grads)
            down_own, down_other = halves_of(down_grad)
        grad_after, grad_mixture, grad_up, grad_down, grad_out, sums_two, hidden_sums = mlp_back(
            layer, gradient, after, vectors, mixed, up, down, mixture, normed_two, active, slope
        )
        if last < layers:
            mixed_other, down_other, grad_mixture = hold(mixed_other, down_other, grad_mixture)
            down_grads[last] = added(down_own, down_other)[0]
            mixed_grad = added(mixed_own, mixed_other)
            grad_mixture, up_grads[last], mixed_grad = hold(grad_mixture, up_grads[last], mixed_grad)
            down_rows = grad_down.reshape(count // 2, 2 * shard, feed_cols)
            together = jnp.concatenate([mixed_grad, down_rows], axis=1)
            together = sum_along(in_rows(together))
        else:
            down_grads[layer] = sum_along(grad_down)
        up_own, up_other = halves_of(grad_up)
        grad_queries, grad_own, grad_far = attend_back(
            meta, queries, own_pairs, far_pairs, own_ids[None, :], row_ids[:, None],
            grad_mixture, logsum,
        )
        up_other, grad_far = hold(up_other, grad_far)
        up_grads[layer] = added(up_own, up_other)
        gradient, grads, sums_one, column_sums = project_back(
            layer, grad_after, x, vectors, mixed, normed, grad_queries, grad_own, grad_far,
            grad_out, used_cols,
        )
        if last < layers:
            grads, together = hold(grads, together)
            mixed_grads[last], down_grads[layer] = together[:shard], together[shard:]
        wide[layer] = sums_one + sums_two
        narrow[layer] = column_sums[0, : 3 * head_cols].reshape(3, head_cols)
        broad[layer] = hidden_sums
    up_grad, down_grads[0] = hold(up_grads[0], down_grads[0])
    up_grads[0] = sum_along(in_rows(up_grad))
    down_own, down_other = halves_of(down_grads[0])
    grads = separate(grads)
    wide = jnp.concatenate(wide, axis=0)
    wide = wide.reshape(layers * 8, 4, head_cols).transpose(1, 0, 2)

    def tall(parts):
        rows_of = jnp.concatenate(parts, axis=0)
        return jnp.pad(rows_of, ((0, -rows_of.shape[0] % 8), (0, 0)))

    final, gradient, sums, broad, first_grad = finish(
        by_features(final.astype(BF)),
        by_features(gradient.astype(BF)),
        wide,
        tall(narrow),
        tall(broad),
        grads,
    )
    mixed_grads[0] = first_grad[:shard]
    down_other, up_grads[0], final, gradient, sums, broad, mixed_grads[0] = hold(
        down_other, up_grads[0], final, gradient, sums, broad, mixed_grads[0]
    )
    down_grads[0] = added(down_own, down_other)[0]
    wide = sums[: layers * 8].reshape(layers, 8, head_cols)
    narrow = sums[layers * 8 : layers * 11].reshape(layers, 3, head_cols)

    def mixed_columns(start):
        columns = slice(start * head_cols, (start + 1) * head_cols)
        return jnp.stack([part[:, columns].astype(F32) for part in mixed_grads])

    def hidden_columns(parts):
        return jnp.stack([part[:, :feed].astype(F32) for part in parts])

    return (
        final,
        gradient,
        wide[:, 0],
        wide[:, 1],
        mixed_columns(2),
        narrow[:, 2],
        mixed_columns(0),
        mixed_columns(1),
        narrow[:, 1],
        mixed_columns(3).transpose(0, 2, 1),
        wide[:, 2],
        wide[:, 3],
        wide[:, 4],
        hidden_columns(up_grads),
        broad[:layers, :feed],
        hidden_columns(down_grads).transpose(0, 2, 1),
        wide[:, 5],
    )


def solution(mesh):
    rows = P("tok", "hid")
    vector = P(None, "hid")
    inward = P(None, "tok", "hid")
    outward = P(None, "hid", "tok")
    in_specs = (
        rows, P(), rows, vector, vector, inward, vector, inward, inward, vector, outward, vector,
        vector, vector, inward, vector, outward, vector,
    )
    out_specs = (
        rows, rows, vector, vector, inward, vector, inward, inward, vector, outward, vector,
        vector, vector, inward, vector, outward, vector,
    )
    return jax.shard_map(body, mesh=mesh, in_specs=in_specs, out_specs=out_specs, check_vma=False)
```

time: 931 us -> 682 us (0.73)
  Pallas kernels: 679 us -> 554 us
  waiting for transfers between devices: 113 us -> 12.3 us
  between operations: 27.9 us -> 14.8 us
  starting transfers between devices: 0.84 us -> 12.4 us
  other arithmetic: 44.4 us -> 33.4 us
    pallas_call x10, Pallas kernels: 554 us -> 472 us  [run(): pl.pallas_call(kernel, name=name, cost_estimate=micros(duration), out_sha...]
    reduce_scatter x3 -> x4, waiting for transfers between devices: 70.7 us -> 0.04 us  [sum_along(): lax.psum_scatter(part, 'tok', scatter_dimension=0, tiled=True, axis_index...]
    all_gather x3 -> x5, waiting for transfers between devices: 42.3 us -> 0.02 us  [along(): lax.all_gather(part, 'tok', axis=0, tiled=True, axis_index_groups=lines)]
    pallas_call x2, Pallas kernels: 75.9 us -> 50 us  [attend_back(): pl.pallas_call(functools.partial(attend_back_kernel, heads=heads), name='...]
    concatenate x6 -> x1, other arithmetic: 18.9 us -> 0.08 us  [side_by_side(): return jnp.concatenate(parts, axis=1)]
    pallas_call x2, Pallas kernels: 48.7 us -> 31.8 us  [attend(): pl.pallas_call(functools.partial(attend_kernel, heads=heads), name='atten...]
    ppermute x0 -> x10, waiting for transfers between devices: none -> 12.1 us  [swap(): return lax.ppermute(part, 'tok', halves)]
    ppermute x0 -> x10, starting transfers between devices: none -> 11.6 us  [swap(): return lax.ppermute(part, 'tok', halves)]
  transfers between devices with their start and end apart: 6 -> 19, of which waited for: 2 -> 2; matrix products, arithmetic and copies ran while one was open for 8% -> 9% of each run, Pallas kernels for 53% -> 68%
where the time goes in v2:
time: 682 us; the launch traced here: 675 us
  Pallas kernels  554 us (81%)
  local copies, waits for them, and re-layouts  47.9 us (7%)
  other arithmetic  33.4 us (5%)
  between operations  14.8 us (2%)
  starting transfers between devices  12.4 us (2%)
  waiting for transfers between devices  12.3 us (2%)
    pallas_call x10, Pallas kernels, run(): pl.pallas_call(kernel, name=name, cost_estimate=micros(duration), out_sha...  472 us
    pallas_call x2, Pallas kernels, attend_back(): pl.pallas_call(functools.partial(attend_back_kernel, heads=heads), name='...  50 us
    pallas_call x2, Pallas kernels, attend(): pl.pallas_call(functools.partial(attend_kernel, heads=heads), name='atten...  31.8 us
  transfers between devices with their start and end apart: 19, of which 2 were waited for; matrix products, arithmetic and copies ran while one was open for 9% of the time, Pallas kernels for 68%

profile of v2, /device:TPU:0, one launch (start us, length us, event | category | flops | bytes accessed | tf_op | source)
XLA Modules:
  0.0 674.5 jit_solution(1805156990730425618)
XLA Ops:
  7.2 1.2 slice_bitcast_fusion.5
  9.4 3.0 collective-permute-start.1
  14.0 2.0 collective-permute-start.4
  16.1 0.9 concatenate.27
  17.3 1.2 copy.111
  18.4 1.2 copy.112
  19.7 1.0 concatenate.24.refs_3_
  21.3 1.1 select_bitcast_fusion.5
  22.4 0.9 pad_maximum_fusion.1
  23.3 64.4 %entry.1 = (bf16[4,256,288]{2,1,0:T(8,128)(2,1)}, bf16[4,256,288]{2,1,0:T(8,128)(2,1)}, f32[4,16,288]{2,1,0:T(8,128)}, bf16[8,144,1152]{2,1,0:T(8,128)(2,1)}) custom-call(bf16[4,256,288]{2,1,0:T(8,128)(2,1)} %bitcast.225, bf16[4,256,288]{2,1,0:T(8,128)(2,1)} %bitcast.226, f32[16,288]{1,0:T(8,128)} %pad_bitcast_fusion.refs_2_, ...), custom_call_target="tpu_custom_call" | custom-call | flops 40000000000 | tf_op jit(solution)/shard_map/entry/pallas_call | solution.py:308
  87.7 1.3 convert_bitcast_fusion
  90.3 1.4 copy.118.refs_0_.refs_1_
  92.4 1.1 select_bitcast_fusion.3
  93.5 0.9 pad_maximum_fusion.2
  94.5 35.7 %project.2 = (bf16[4,256,1152]{2,1,0:T(8,128)(2,1)}, bf16[4,256,288]{2,1,0:T(8,128)(2,1)}, bf16[4,256,576]{2,1,0:T(8,128)(2,1)}, bf16[4,256,576]{2,1,0:T(8,128)(2,1)}) custom-call(f32[256,1152]{1,0:T(8,128)} %copy.118.refs_0_.refs_1_, f32[2,8,1152]{2,1,0:T(8,128)} %reshape.268.refs_1_.refs_2_, f32[2,896]{1,0:T(2,128)} %pad.34.refs_2_, ...), custom_call_target="tpu_custom_call" | custom-call | flops 40000000000 | tf_op jit(solution)/shard_map/project/pallas_call | solution.py:308
  132.2 1.0 copy.119.query_ids
  133.9 15.9 %attend.2 = (bf16[4,256,384]{2,1,0:T(8,128)(2,1)}, f32[8,1024]{1,0:T(8,128)}) custom-call(s32[10]{0:T(128)} %pad_add_fusion.1.meta, bf16[4,256,288]{2,1,0:T(8,128)(2,1)} %get-tuple-element.104.queries, bf16[4,256,576]{2,1,0:T(8,128)(2,1)} %get-tuple-element.105.own_pairs, bf16[4,256,576]{2,1,0:T(8,128)(2,1)} %get-tuple-element.106.far_pairs, ...), custom_call_target="tpu_custom_call" | custom-call | flops 22000001024 | tf_op jit(solution)/shard_map/attend/pallas_call | solution.py:628
  151.0 1.4 copy.122.refs_0_
  152.4 1.3 copy.123.key_ids
  153.7 1.1 select_bitcast_fusion.1
  154.9 0.9 pad_maximum_fusion.3
  156.1 1.2 collective-permute-start.2
  157.3 9.0 %collective-permute-done = bf16[576,1152]{1,0:T(8,128)(2,1)} collective-permute-done((bf16[576,1152]{1,0:T(8,128)(2,1)}, bf16[576,1152]{1,0:T(8,128)(2,1)}, u32[]{:S(2)}, u32[]{:S(2)}) %collective-permute-start) | collective-permute-done | bytes 1327136 | tf_op jit(solution)/shard_map/ppermute | solution.py:1349
  166.2 46.6 %mlp.2 = (f32[256,1152]{1,0:T(8,128)}, f32[256,1152]{1,0:T(8,128)}, bf16[4,256,1152]{2,1,0:T(8,128)(2,1)}, bf16[4,256,1152]{2,1,0:T(8,128)(2,1)}, bf16[4,256,1152]{2,1,0:T(8,128)(2,1)}) custom-call(bf16[4,256,384]{2,1,0:T(8,128)(2,1)} %get-tuple-element.107.refs_0_.refs_3_, f32[256,1152]{1,0:T(8,128)} %copy.118.refs_0_.refs_1_, ...), custom_call_target="tpu_custom_call" | custom-call | flops 48000000000 | tf_op jit(solution)/shard_map/mlp/pallas_call | solution.py:308
  212.9 1.1 copy-done.44
  213.9 34.5 %project.3 = (bf16[4,256,1152]{2,1,0:T(8,128)(2,1)}, bf16[4,256,288]{2,1,0:T(8,128)(2,1)}, bf16[4,256,576]{2,1,0:T(8,128)(2,1)}, bf16[4,256,576]{2,1,0:T(8,128)(2,1)}) custom-call(f32[256,1152]{1,0:T(8,128)} %get-tuple-element.108.refs_0_.refs_1_, f32[2,8,1152]{2,1,0:T(8,128)} %reshape.268.refs_1_.refs_2_, f32[2,896]{1,0:T(2,128)} %pad.34.refs_2_, ...), custom_call_target="tpu_custom_call" | custom-call | flops 40000000000 | tf_op jit(solution)/shard_map/project/pallas_call | solution.py:308
  248.4 15.8 %attend.3 = (bf16[4,256,384]{2,1,0:T(8,128)(2,1)}, f32[8,1024]{1,0:T(8,128)}) custom-call(s32[10]{0:T(128)} %pad_add_fusion.1.meta, bf16[4,256,288]{2,1,0:T(8,128)(2,1)} %get-tuple-element.109.queries, bf16[4,256,576]{2,1,0:T(8,128)(2,1)} %get-tuple-element.110.own_pairs, bf16[4,256,576]{2,1,0:T(8,128)(2,1)} %get-tuple-element.111.far_pairs, ...), custom_call_target="tpu_custom_call" | custom-call | flops 22000001024 | tf_op jit(solution)/shard_map/attend/pallas_call | solution.py:628
  264.2 46.5 %mlp.3 = (f32[256,1152]{1,0:T(8,128)}, f32[256,1152]{1,0:T(8,128)}, bf16[4,256,1152]{2,1,0:T(8,128)(2,1)}, bf16[4,256,1152]{2,1,0:T(8,128)(2,1)}, bf16[4,256,1152]{2,1,0:T(8,128)(2,1)}) custom-call(bf16[4,256,384]{2,1,0:T(8,128)(2,1)} %get-tuple-element.112.refs_0_.refs_3_, f32[256,1152]{1,0:T(8,128)} %get-tuple-element.108.refs_0_.refs_1_, ...), custom_call_target="tpu_custom_call" | custom-call | flops 48000000000 | tf_op jit(solution)/shard_map/mlp/pallas_call | solution.py:308
  310.8 46.9 %mlp_back.2 = (f32[256,1152]{1,0:T(8,128)}, bf16[4,256,384]{2,1,0:T(8,128)(2,1)}, bf16[1152,1152]{1,0:T(8,128)(2,1)}, bf16[1152,1152]{1,0:T(8,128)(2,1)}, bf16[1...) custom-call(f32[256,1152]{1,0:T(8,128)} %copy.122.refs_0_, f32[256,1152]{1,0:T(8,128)} %get-tuple-element.113.refs_1_, ...), custom_call_target="tpu_custom_call" | custom-call | flops 48000000000 | tf_op jit(solution)/shard_map/mlp_back/pallas_call | solution.py:308
  357.7 1.4 dynamic-slice_bitcast_fusion.2
  359.9 25.0 %attend_back.2 = (bf16[4,256,288]{2,1,0:T(8,128)(2,1)}, bf16[4,256,576]{2,1,0:T(8,128)(2,1)}, bf16[4,256,576]{2,1,0:T(8,128)(2,1)}) custom-call(s32[10]{0:T(128)} %pad_add_fusion.1.meta, bf16[4,256,288]{2,1,0:T(8,128)(2,1)} %get-tuple-element.109.queries, bf16[4,256,576]{2,1,0:T(8,128)(2,1)} %get-tuple-element.110.own_pairs, ...), custom_call_target="tpu_custom_call" | custom-call | flops 36999999488 | tf_op jit(solution)/shard_map/attend_back/pallas_call | solution.py:728
  384.9 1.3 convert_element_type.137
  386.5 1.2 copy.128
  387.6 3.1 collective-permute-done.5
  390.7 40.6 %project_back.2 = (f32[256,1152]{1,0:T(8,128)}, bf16[1152,1152]{1,0:T(8,128)(2,1)}, f32[8,1152]{1,0:T(8,128)}, f32[1,896]{1,0:T(1,128)}) custom-call(f32[256,1152]{1,0:T(8,128)} %get-tuple-element.117.refs_0_, f32[256,1152]{1,0:T(8,128)} %get-tuple-element.108.refs_0_.refs_1_, f32[2,8,1152]{2,1,0:T(8,128)} %reshape.268.refs_1_.refs_2_, ...), custom_call_target="tpu_custom_call" | custom-call | flops 41999998976 | tf_op jit(solution)/shard_map/project_back/pallas_call | solution.py:308
  431.4 2.6 dynamic-slice_bitcast_fusion
  434.0 1.3 collective-permute-start.7
  436.9 2.7 fusion.2
  439.6 1.0 dynamic-slice_bitcast_fusion.4
  440.6 0.8 collective-permute-start.8
  441.7 47.0 %mlp_back.3 = (f32[256,1152]{1,0:T(8,128)}, bf16[4,256,384]{2,1,0:T(8,128)(2,1)}, bf16[1152,1152]{1,0:T(8,128)(2,1)}, bf16[1152,1152]{1,0:T(8,128)(2,1)}, bf16[1...) custom-call(f32[256,1152]{1,0:T(8,128)} %get-tuple-element.130.refs_0_, ...), custom_call_target="tpu_custom_call" | custom-call | flops 48000000000 | tf_op jit(solution)/shard_map/mlp_back/pallas_call | solution.py:308
  488.7 1.6 dynamic-slice_bitcast_fusion.1
  490.3 1.3 collective-permute-start.6
  491.6 1.3 select_maximum_fusion.refs_4_
  493.8 1.6 fusion
  495.4 4.0 pad_maximum_fusion
  499.5 25.0 %attend_back.3 = (bf16[4,256,288]{2,1,0:T(8,128)(2,1)}, bf16[4,256,576]{2,1,0:T(8,128)(2,1)}, bf16[4,256,576]{2,1,0:T(8,128)(2,1)}) custom-call(s32[10]{0:T(128)} %pad_add_fusion.1.meta, bf16[4,256,288]{2,1,0:T(8,128)(2,1)} %get-tuple-element.104.queries, bf16[4,256,576]{2,1,0:T(8,128)(2,1)} %get-tuple-element.105.own_pairs, ...), custom_call_target="tpu_custom_call" | custom-call | flops 36999999488 | tf_op jit(solution)/shard_map/attend_back/pallas_call | solution.py:728
  524.5 40.6 %project_back.3 = (f32[256,1152]{1,0:T(8,128)}, bf16[1152,1152]{1,0:T(8,128)(2,1)}, f32[8,1152]{1,0:T(8,128)}, f32[1,896]{1,0:T(1,128)}) custom-call(f32[256,1152]{1,0:T(8,128)} %get-tuple-element.146.refs_0_, f32[256,1152]{1,0:T(8,128)} %copy.118.refs_0_.refs_1_, f32[2,8,1152]{2,1,0:T(8,128)} %reshape.268.refs_1_.refs_2_, ...), custom_call_target="tpu_custom_call" | custom-call | flops 41999998976 | tf_op jit(solution)/shard_map/project_back/pallas_call | solution.py:308
  567.5 1.3 convert_element_type.138
  568.8 1.1 copy.129
  569.9 2.2 copy.130
  572.7 1.0 slice_bitcast_fusion.2
  573.7 2.7 fusion.1
  576.5 1.1 slice.139
  577.6 1.3 collective-permute-start.9
  579.0 69.1 %finish.1 = (f32[1024,288]{1,0:T(8,128)}, f32[1024,288]{1,0:T(8,128)}, f32[24,288]{1,0:T(8,128)}, f32[8,1152]{1,0:T(8,128)}, f32[144,1152]{1,0:T(8,128)}) custom-call(bf16[4,256,288]{2,1,0:T(8,128)(2,1)} %bitcast.224, bf16[4,256,288]{2,1,0:T(8,128)(2,1)} %bitcast.227, f32[4,16,288]{2,1,0:T(8,128)} %bitcast.230, f32[8,288]{1,0:T(8,128)} %select_maximum_fusion.1.refs_3_, ...), custom_call_target="tpu_custom_call" | custom-call | flops 40000000000 | tf_op jit(solution)/shard_map/finish/pallas_call | solution.py:308
  648.1 2.2 bitcast_convert_fusion
  652.1 1.2 slice_bitcast_fusion.8
  653.2 1.5 copy.138
  654.7 1.5 copy.139
  660.8 1.4 slice.161
  662.2 1.2 convert_bitcast_fusion.2
  663.4 1.2 maximum_convert_fusion
  665.4 0.8 pad_maximum_fusion.6
  (196 shorter events, 25.2 us)
Async XLA Ops:
  7.2 2.1 copy-start.19
  7.2 126.7 %all-gather.6.cloned.1.call-start = ((), (), s32[]{:S(2)}) async-start(), calls=%async_computation.4 | async-start | bytes 1658880 | tf_op jit(solution)/shard_map/all_gather | solution.py:1356
  9.2 146.9 %all-gather.10.cloned.1.call-start = ((), (), s32[]{:S(2)}) async-start(), calls=%async_computation.6 | async-start | bytes 1658880 | tf_op jit(solution)/shard_map/all_gather | solution.py:1356
  9.3 6.6 copy-start.25
  9.3 6.6 copy-start.26
  9.4 6.7 copy-start.23
  9.4 6.7 copy-start.24
  9.4 11.8 %collective-permute-start.1 = (bf16[144,1152]{1,0:T(8,128)(2,1)S(1)}, bf16[144,1152]{1,0:T(8,128)(2,1)}, u32[]{:S(2)}, u32[]{:S(2)}) collective-permute-start(bf16[144,1152]{1,0:T(8,128)(2,1)S(1)} %pad.37), channel_id=1, source_target_pairs={{0,4},{4,0},{8,12},{12,8},{16,20},{20,16},{24,28},{28,24},{1,5},{5... | collective-permute-start | bytes 995336 | tf_op jit(solution)/shard_map/ppermute | solution.py:1349
  13.2 79.2 %collective-permute-start.3 = (bf16[144,1152]{1,0:T(8,128)(2,1)}, bf16[144,1152]{1,0:T(8,128)(2,1)}, u32[]{:S(2)}, u32[]{:S(2)}) collective-permute-start(bf16[144,1152]{1,0:T(8,128)(2,1)} %pad.38), channel_id=1, source_target_pairs={{0,4},{4,0},{8,12},{12,8},{16,20},{20,16},{24,28},{28,24},{1,5},{5... | collective-permute-start | bytes 995336 | tf_op jit(solution)/shard_map/ppermute | solution.py:1349
  14.0 139.8 %collective-permute-start.4 = (bf16[144,1152]{1,0:T(8,128)(2,1)}, bf16[144,1152]{1,0:T(8,128)(2,1)}, u32[]{:S(2)}, u32[]{:S(2)}) collective-permute-start(bf16[144,1152]{1,0:T(8,128)(2,1)} %pad.39), channel_id=1, source_target_pairs={{0,4},{4,0},{8,12},{12,8},{16,20},{20,16},{24,28},{28,24},{1,5},{5... | collective-permute-start | bytes 995336 | tf_op jit(solution)/shard_map/ppermute | solution.py:1349
  16.0 1.2 copy-start.36
  16.0 1.2 copy-start.20
  16.1 2.3 copy-start.21
  17.1 149.1 %all-gather.8.cloned.1.call-start = ((), (), s32[]{:S(2)}) async-start(), calls=%async_computation.5 | async-start | bytes 3317760 | tf_op jit(solution)/shard_map/all_gather | solution.py:1356
  17.2 2.4 copy-start.37
  17.2 2.4 copy-start.38
  17.2 2.4 copy-start.39
  17.2 2.4 copy-start.40
  17.3 2.4 copy-start.41
  23.3 240.9 %all-gather.12.cloned.1.call-start = ((), (), s32[]{:S(2)}) async-start(), calls=%async_computation.7 | async-start | bytes 3317760 | tf_op jit(solution)/shard_map/all_gather | solution.py:1356
  87.7 1.3 copy-start.27
  90.2 1.4 copy-start.42
  90.3 1.4 copy-start.43
  94.4 169.8 %all-gather.14.cloned.1.call-start = ((), (), s32[]{:S(2)}) async-start(), calls=%async_computation.8 | async-start | bytes 3317760 | tf_op jit(solution)/shard_map/all_gather | solution.py:1356
  130.9 3.0 copy-start.28
  131.6 2.3 copy-start.30
  133.8 32.4 %collective-permute-start = (bf16[576,1152]{1,0:T(8,128)(2,1)}, bf16[576,1152]{1,0:T(8,128)(2,1)}, u32[]{:S(2)}, u32[]{:S(2)}) collective-permute-start(bf16[576,1152]{1,0:T(8,128)(2,1)} %all-gather.6.cloned.1.call-done), channel_id=1, source_target_pairs={{0,4},{4,0},{8,12},{12,8},{16,20},{20,16},{24,28},{28,24},{1,5},{5... | collective-permute-start | bytes 3981320 | tf_op jit(solution)/shard_map/ppermute | solution.py:1349
  133.9 16.0 %copy-start.34 = (f32[2,1076]{1,0:T(2,128)S(1)}, f32[2,1076]{1,0:T(2,128)}, u32[]{:S(2)}) copy-start(f32[2,1076]{1,0:T(2,128)} %param.33) | copy-start | bytes 25828
  133.9 16.6 %copy-start.17 = (bf16[4,256,288]{2,1,0:T(8,128)(2,1)S(1)}, bf16[4,256,288]{2,1,0:T(8,128)(2,1)}, u32[]{:S(2)}) copy-start(bf16[4,256,288]{2,1,0:T(8,128)(2,1)} %get-tuple-element.100) | copy-start | bytes 1769476
  151.0 1.4 copy-start.29
  155.8 283.7 %reduce-scatter.5.cloned.1.call-start = ((), (), s32[]{:S(2)}) async-start(), calls=%async_computation.9 | async-start | bytes 3317760 | tf_op jit(solution)/shard_map/reduce_scatter | solution.py:1402
  156.1 56.8 %collective-permute-start.2 = (bf16[576,1152]{1,0:T(8,128)(2,1)}, bf16[576,1152]{1,0:T(8,128)(2,1)S(1)}, u32[]{:S(2)}, u32[]{:S(2)}) collective-permute-start(bf16[576,1152]{1,0:T(8,128)(2,1)} %all-gather.10.cloned.1.call-done), channel_id=1, source_target_pairs={{0,4},{4,0},{8,12},{12,8},{16,20},{20,16},{24,28},{28,24},{1,5},{5... | collective-permute-start | bytes 3981320 | tf_op jit(solution)/shard_map/ppermute | solution.py:1349
  212.9 1.1 copy-start.44
  359.1 31.6 %collective-permute-start.5 = (bf16[4,144,1152]{2,1,0:T(8,128)(2,1)S(1)}, bf16[4,144,1152]{2,1,0:T(8,128)(2,1)}, u32[]{:S(2)}, u32[]{:S(2)}) collective-permute-start(bf16[4,144,1152]{2,1,0:T(8,128)(2,1)S(1)} %dynamic-slice_bitcast_fusion.2), channel_id=1, source_target_pairs={{0,4},{4,0},{8,12},{12,8},{16,20},{20,16},{24,28},{28,24},{1,5},{5... | collective-permute-start | bytes 3981320 | tf_op jit(solution)/shard_map/ppermute | solution.py:1349
  359.8 135.6 %reduce-scatter.7.cloned.1.call-start = ((), (), s32[]{:S(2)}) async-start(), calls=%async_computation.10 | async-start | bytes 1658880 | tf_op jit(solution)/shard_map/reduce_scatter | solution.py:1402
  390.7 45.4 %copy-start.32 = (f32[8,1152]{1,0:T(8,128)S(1)}, f32[8,1152]{1,0:T(8,128)}, u32[]{:S(2)}) copy-start(f32[8,1152]{1,0:T(8,128)} %get-tuple-element.163) | copy-start | bytes 110596
  431.4 5.5 copy-start.2
  434.0 58.9 %collective-permute-start.7 = (bf16[4,144,1152]{2,1,0:T(8,128)(2,1)}, bf16[4,144,1152]{2,1,0:T(8,128)(2,1)}, u32[]{:S(2)}, u32[]{:S(2)}) collective-permute-start(bf16[4,144,1152]{2,1,0:T(8,128)(2,1)} %dynamic-slice_bitcast_fusion), channel_id=1, source_target_pairs={{0,4},{4,0},{8,12},{12,8},{16,20},{20,16},{24,28},{28,24},{1,5},{5... | collective-permute-start | bytes 3981320 | tf_op jit(solution)/shard_map/ppermute | solution.py:1349
  440.6 52.4 %collective-permute-start.8 = (bf16[1,144,1152]{2,1,0:T(8,128)(2,1)S(1)}, bf16[1,144,1152]{2,1,0:T(8,128)(2,1)S(1)}, u32[]{:S(2)}, u32[]{:S(2)}) collective-permute-start(bf16[1,144,1152]{2,1,0:T(8,128)(2,1)S(1)} %dynamic-slice_bitcast_fusion.4), channel_id=1, source_target_pairs={{0,4},{4,0},{8,12},{12,8},{16,20},{20,16},{24,28},{28,24},{1,5},{5... | collective-permute-start | bytes 995336 | tf_op jit(solution)/shard_map/ppermute | solution.py:1349
  441.4 135.0 %reduce-scatter.9.cloned.1.call-start = ((), (), s32[]{:S(2)}) async-start(), calls=%async_computation.11 | async-start | bytes 4976640 | tf_op jit(solution)/shard_map/reduce_scatter | solution.py:1402
  441.7 49.9 %copy-start.35 = (f32[1,1152]{1,0:T(1,128)S(1)}, f32[1,1152]{1,0:T(1,128)}, u32[]{:S(2)}) copy-start(f32[1,1152]{1,0:T(1,128)} %get-tuple-element.167) | copy-start | bytes 13828
  441.7 51.2 %copy-start.18 = (bf16[288,1152]{1,0:T(8,128)(2,1)S(1)}, bf16[288,1152]{1,0:T(8,128)(2,1)}, u32[]{:S(2)}) copy-start(bf16[288,1152]{1,0:T(8,128)(2,1)} %reduce-scatter.5.cloned.1.call-done) | copy-start | bytes 1990660
  488.7 5.1 copy-start.1
  490.3 34.2 %collective-permute-start.6 = (bf16[4,144,1152]{2,1,0:T(8,128)(2,1)S(1)}, bf16[4,144,1152]{2,1,0:T(8,128)(2,1)}, u32[]{:S(2)}, u32[]{:S(2)}) collective-permute-start(bf16[4,144,1152]{2,1,0:T(8,128)(2,1)S(1)} %dynamic-slice_bitcast_fusion.1), channel_id=1, source_target_pairs={{0,4},{4,0},{8,12},{12,8},{16,20},{20,16},{24,28},{28,24},{1,5},{5... | collective-permute-start | bytes 3981320 | tf_op jit(solution)/shard_map/ppermute | solution.py:1349
  499.4 150.8 %reduce-scatter.11.cloned.1.call-start = ((), (), s32[]{:S(2)}) async-start(), calls=%async_computation.12 | async-start | bytes 1658880 | tf_op jit(solution)/shard_map/reduce_scatter | solution.py:1402
  524.5 41.4 %copy-start.31 = (f32[8,1152]{1,0:T(8,128)S(1)}, f32[8,1152]{1,0:T(8,128)}, u32[]{:S(2)}) copy-start(f32[8,1152]{1,0:T(8,128)} %get-tuple-element.161) | copy-start | bytes 110596
  568.8 4.9 copy-start
  577.6 72.6 %collective-permute-start.9 = (bf16[1,144,1152]{2,1,0:T(8,128)(2,1)S(1)}, bf16[1,144,1152]{2,1,0:T(8,128)(2,1)S(1)}, u32[]{:S(2)}, u32[]{:S(2)}) collective-permute-start(bf16[1,144,1152]{2,1,0:T(8,128)(2,1)S(1)} %dynamic-slice_bitcast_fusion.3), channel_id=1, source_target_pairs={{0,4},{4,0},{8,12},{12,8},{16,20},{20,16},{24,28},{28,24},{1,5},{5... | collective-permute-start | bytes 995336 | tf_op jit(solution)/shard_map/ppermute | solution.py:1349
  648.1 2.2 copy-start.33
  650.2 1.8 copy-start.8
  650.3 1.0 copy-start.22
  651.3 1.9 copy-start.4
  653.2 1.5 copy-start.3
  654.7 7.5 %copy-start.5 = (bf16[1,144,1076]{2,1,0:T(8,128)(2,1)S(1)}, bf16[1,144,1076]{2,1,0:T(8,128)(2,1)}, u32[]{:S(2)}) copy-start(bf16[1,144,1076]{2,1,0:T(8,128)(2,1)} %slice_bitcast_fusion) | copy-start | bytes 929668
  654.7 7.5 %copy-start.7 = (bf16[1,144,1076]{2,1,0:T(8,128)(2,1)S(1)}, bf16[1,144,1076]{2,1,0:T(8,128)(2,1)}, u32[]{:S(2)}) copy-start(bf16[1,144,1076]{2,1,0:T(8,128)(2,1)} %slice_bitcast_fusion.1) | copy-start | bytes 929668
  656.1 7.2 %copy-start.6 = (bf16[1,144,1076]{2,1,0:T(8,128)(2,1)S(1)}, bf16[1,144,1076]{2,1,0:T(8,128)(2,1)}, u32[]{:S(2)}) copy-start(bf16[1,144,1076]{2,1,0:T(8,128)(2,1)} %slice_bitcast_fusion.3) | copy-start | bytes 929668
  663.4 1.2 copy-start.12
  663.4 1.2 copy-start.16
  663.4 2.0 copy-start.11
  663.4 2.0 copy-start.15
  664.5 1.6 copy-start.10
  664.5 1.6 copy-start.14
  664.6 2.4 copy-start.9
  664.6 2.4 copy-start.13
Sparse Core Ops, SparseCore 0:
  10.2 42.7 all-gather.5
  55.1 34.5 all-gather.9
  91.9 54.6 all-gather.7
  148.0 54.1 all-gather.11
  203.5 54.1 all-gather.13
  359.9 52.1 reduce-scatter.4
  441.5 32.2 reduce-scatter.6
  499.6 74.5 reduce-scatter.8
  579.1 49.4 reduce-scatter.10

commit v3 on v2

--- a/solution.py
+++ b/solution.py
@@ -151,6 +151,22 @@
     return Several(copies)
 
 
+def store_halves(net, moves, grad, outs, shard):
+    if not shard:
+        moves.store(grad, outs[0])
+        return
+    for out, low in zip(outs, (net.low, 1 - net.low)):
+        for place in range(out.shape[0]):
+            start = pl.multiple_of((place * 2 + low) * shard, 16)
+            moves.store(grad.at[pl.ds(start, shard)], out.at[place])
+
+
+def half_outputs(rows, columns, shard):
+    if not shard:
+        return [((rows, columns), BF, False)]
+    return [((rows // (2 * shard), shard, columns), BF, False)] * 2
+
+
 def spaced(arrays):
     return [(array, False) for array in arrays]
 
@@ -272,12 +288,17 @@
         self.net, self.moves = net, moves
         self.own, self.landed, passing, arrived = scratch
         self.count = count = grads.shape[0] // 2
-        ends = [[count - 1 - step, step] for step in range((count + 1) // 2)]
-        order = list(dict.fromkeys(sum(ends, [])))
         self.across, self.loads = net.take(count), moves.take(count)
-        for place in order:
+        high, last = net.high, count - 1
+
+        def start(place):
             self.swap(place, grads.at[place * 2 + 1 - net.low]).start()
-        for place in order:
+
+        for slot in range(last):
+            pl.when(high <= slot)(functools.partial(start, last - slot + high))
+            pl.when(last - high <= slot)(functools.partial(start, slot - last + high))
+        start(high)
+        for place in range(count):
             source = grads.at[place * 2 + net.low]
             moves.make(self.loads + place, source, self.own.at[place]).start()
         self.line = Line(net, count, self.pair, passing, arrived)
@@ -752,12 +773,12 @@
     )(meta, queries, own_pairs, far_pairs, query_ids, key_ids, grad_mixture, logsum)
 
 
-def mlp_kernel(*refs, layer, parts):
-    ins, outs, scratch = split_refs(refs, 4 + sum(parts), 5)
+def mlp_kernel(*refs, layer, parts, last):
+    ins, outs, scratch = split_refs(refs, 4 + sum(parts), 5 - last)
     mixture_hbm, x_hbm, vec, up_bias = ins[:4]
     mixed_hbm, up_hbm, down_hbm = split_refs(ins[4:], parts[0], parts[1])
-    x_out, after_out, normed_out, active_out, slope_out = outs
-    mixture, x, out_weight, up_weight, down_weight, x_next, after, normed, active, slope = scratch[:10]
+    after_out, normed_out, active_out, slope_out = outs[:4]
+    mixture, x, out_weight, up_weight, down_weight, after, normed, active, slope, x_next = scratch[:10]
     first_scratch, second_scratch = scratch[10:18], scratch[18:26]
     send_sems, recv_sems, move_sems = scratch[26:]
     net, moves = Net(send_sems, recv_sems), Moves(move_sems)
@@ -771,7 +792,8 @@
     ]
     x_load = moves.load(x_hbm, x)
     up_load = load_weight(net, moves, up_hbm, pl.ds(0, hidden_cols), up_weight)
-    down_load = load_weight(net, moves, down_hbm, pl.ds(0, hidden_cols), down_weight)
+    if not last:
+        down_load = load_weight(net, moves, down_hbm, pl.ds(0, hidden_cols), down_weight)
     net.barrier([net.core, net.far])
     out_bias, gain = vec[layer, 2:3], vec[layer, 3:4]
     shift, down_bias = vec[layer, 4:5], vec[layer, 5:6]
@@ -814,35 +836,38 @@
         one.wait_recv()
     up_load.wait()
     up(near, whole)
-    down_load.wait()
+    if not last:
+        down_load.wait()
     second = Scatter(net, second_scratch)
     for key, chunk in enumerate(chunks):
         passed = gather_pass(net, normed, chunk, sent[key][1])
         passed.wait_recv()
         up(far, chunk)
-        second.far_part(key, chunk, down(far, chunk))
-        second.far_send(key, chunk)
+        if not last:
+            second.far_part(key, chunk, down(far, chunk))
+            second.far_send(key, chunk)
     moves.store(normed, normed_out)
     moves.store(active, active_out)
     moves.store(slope, slope_out)
-    second.near_part(down(near, whole))
-    second.near_done()
-    for key, chunk in enumerate(chunks):
-        x_next[chunk, :] = second.result(key, chunk) + after[chunk, :] + down_bias
-    moves.store(x_next, x_out)
+    if not last:
+        second.near_part(down(near, whole))
+        second.near_done()
+        for key, chunk in enumerate(chunks):
+            x_next[chunk, :] = second.result(key, chunk) + after[chunk, :] + down_bias
+        moves.store(x_next, outs[4])
     net.finish()
     moves.finish()
 
 
-def mlp(layer, mixture, x, vec, up_bias, mixed, up, down):
+def mlp(layer, mixture, x, vec, up_bias, mixed, up, down, last):
     rows, width = x.shape
     hidden = up_bias.shape[1]
     outputs = [
         ((rows, width), F32, False),
-        ((rows, width), F32, False),
         ((4, rows, width), BF, False),
         ((4, rows, hidden), BF, False),
         ((4, rows, hidden), BF, False),
+        ((rows, width), F32, False),
     ]
     scratch = [
         pltpu.VMEM(mixture.shape, BF),
@@ -853,19 +878,22 @@
     ]
     scratch += [pltpu.VMEM(shape, dtype) for shape, dtype, _ in outputs]
     scratch += scatter_scratch(rows, width) * 2
+    outputs = outputs[: 5 - last]
+    down = () if last else down
     inputs = [(mixture, False), (x, False), (vec, True), (up_bias, True)]
-    inputs += spaced(mixed + up + down)
+    inputs += spaced([*mixed, *up, *down])
     parts = (len(mixed), len(up), len(down))
-    kernel = functools.partial(mlp_kernel, layer=layer, parts=parts)
-    moves = 8 + weight_loads(mixed) + weight_loads(up) + weight_loads(down)
+    kernel = functools.partial(mlp_kernel, layer=layer, parts=parts, last=last)
+    moves = 8 + sum(weight_loads(part) for part in (mixed, up, down) if part)
     return run(kernel, "mlp", 48, inputs, outputs, scratch, 8 * layer + 1, 18, moves)
 
 
-def mlp_back_kernel(*refs, layer, parts):
-    ins, outs, scratch = split_refs(refs, 7 + sum(parts), 7)
+def mlp_back_kernel(*refs, layer, parts, given, shard):
+    ins, outs, scratch = split_refs(refs, 7 + given + sum(parts), 7 + (shard > 0))
     gradient_hbm, after_hbm, vec, mixture_hbm, normed_hbm, active_hbm, slope_hbm = ins[:7]
-    mixed_hbm, up_hbm, down_hbm = split_refs(ins[7:], parts[0], parts[1])
-    after_out, mixture_out, up_out, down_out, out_out, sums, hidden_sums = outs
+    mixed_hbm, up_hbm, down_hbm = split_refs(ins[7 + given :], parts[0], parts[1])
+    after_out, mixture_out, down_out, out_out, sums, hidden_sums = outs[:6]
+    up_outs = outs[6:]
     gradient, after, out_weight, up_weight, down_weight, mixture, normed, active, slope = scratch[:9]
     grad_after, grad_mixture, grad_down, grad_up, grad_out = scratch[9:14]
     grad_rows, grad_hidden, grad_mid = scratch[14:17]
@@ -877,7 +905,7 @@
     out_cols = out_weight.shape[1]
     chunks = chunks_of(rows, 2)
     out_part = pl.ds(width - out_cols, out_cols)
-    load_gradient = moves.load(gradient_hbm, gradient)
+    load_gradient = moves.load(ins[7] if given else gradient_hbm, grad_rows if given else gradient)
     load_down = load_weight(net, moves, down_hbm, pl.ds(0, hidden_cols), down_weight)
     load_slope = moves.load(slope_hbm, slope)
     load_up = load_weight(net, moves, up_hbm, pl.ds(0, hidden_cols), up_weight)
@@ -886,15 +914,17 @@
     load_normed = moves.load(normed_hbm, normed)
     load_out = load_weight(net, moves, mixed_hbm, out_part, out_weight)
     load_mixture = moves.load(mixture_hbm, mixture)
+    if given:
+        load_own = moves.load(gradient_hbm, gradient)
     net.barrier([net.core, net.far])
     gain = vec[layer, 3:4]
     near, far, whole = pl.ds(0, 2), pl.ds(2, 2), pl.ds(0, rows)
     load_gradient.wait()
-    rounded = gradient[...].astype(BF)
-    grad_rows[0] = rounded
-    sent = [gather_send(net, grad_rows, chunk) for chunk in chunks]
+    if not given:
+        grad_rows[0] = gradient[...].astype(BF)
+        sent = [gather_send(net, grad_rows, chunk) for chunk in chunks]
     sums[...] = jnp.zeros_like(sums)
-    sums[5:6] = jnp.sum(rounded.astype(F32), axis=0, keepdims=True)
+    sums[5:6] = jnp.sum(grad_rows[0].astype(F32), axis=0, keepdims=True)
 
     def hidden_grad(slots, chunk):
         value = dot(flat(grad_rows[slots, chunk, :]), down_weight[...])
@@ -904,25 +934,38 @@
     def up_back(slots, chunk):
         return dot(flat(grad_hidden[slots, chunk, :]), up_weight[...], NT)
 
-    for one, _ in sent:
-        one.wait_recv()
+    if not given:
+        for one, _ in sent:
+            one.wait_recv()
     load_down.wait()
     load_slope.wait()
-    hidden_grad(near, whole)
-    load_up.wait()
     scatter = Scatter(net, scatter_refs)
-    for key, chunk in enumerate(chunks):
-        passed = gather_pass(net, grad_rows, chunk, sent[key][1])
-        passed.wait_recv()
-        hidden_grad(far, chunk)
-        scatter.far_part(key, chunk, up_back(far, chunk))
-        scatter.far_send(key, chunk)
+    if given:
+        for key, chunk in enumerate(chunks):
+            hidden_grad(far, chunk)
+            if key == 0:
+                load_up.wait()
+            scatter.far_part(key, chunk, up_back(far, chunk))
+        for key, chunk in enumerate(chunks):
+            scatter.far_send(key, chunk)
+        hidden_grad(near, whole)
+    else:
+        hidden_grad(near, whole)
+        load_up.wait()
+        for key, chunk in enumerate(chunks):
+            passed = gather_pass(net, grad_rows, chunk, sent[key][1])
+            passed.wait_recv()
+            hidden_grad(far, chunk)
+            scatter.far_part(key, chunk, up_back(far, chunk))
+            scatter.far_send(key, chunk)
     scatter.near_part(up_back(near, whole))
     load_active.wait()
     weight_grad(grad_rows, active, grad_down)
     moves.store(grad_down, down_out)
     scatter.near_done()
     load_after.wait()
+    if given:
+        load_own.wait()
     sent = []
     for key, chunk in enumerate(chunks):
         back, gain_sum, shift_sum = norm_back(after[chunk, :], gain, scatter.result(key, chunk))
@@ -937,7 +980,7 @@
     moves.store(grad_after, after_out)
     load_normed.wait()
     weight_grad(normed, grad_hidden, grad_up)
-    moves.store(grad_up, up_out)
+    store_halves(net, moves, grad_up, up_outs, shard)
     column = jnp.zeros((1, hidden_cols), F32)
     for slot in range(4):
         column += jnp.sum(grad_hidden[slot].astype(F32), axis=0, keepdims=True)
@@ -962,14 +1005,16 @@
     moves.finish()
 
 
-def mlp_back(layer, gradient, after, vec, mixed, up, down, mixture, normed, active, slope):
+def mlp_back(
+    layer, gradient, after, vec, mixed, up, down, mixture, normed, active, slope, given=(),
+    shard=0,
+):
     rows, width = gradient.shape
     hidden = active.shape[2]
     out_cols = mixture.shape[2]
     outputs = [
         ((rows, width), F32, False),
         ((4, rows, out_cols), BF, False),
-        ((width, hidden), BF, False),
         ((width, hidden), BF, False),
         ((width, out_cols), BF, False),
         ((8, width), F32, True),
@@ -994,26 +1039,30 @@
         ((4, rows, hidden), BF),
         ((4, rows, width), BF),
     ]
+    outputs += half_outputs(width, hidden, shard)
     scratch = [pltpu.VMEM(shape, dtype) for shape, dtype in shapes] + scatter_scratch(rows, width)
     inputs = [
         (gradient, False), (after, False), (vec, True), (mixture, False), (normed, False),
         (active, False), (slope, False),
-    ] + spaced(mixed + up + down)
+    ] + spaced([*given, *mixed, *up, *down])
     parts = (len(mixed), len(up), len(down))
-    kernel = functools.partial(mlp_back_kernel, layer=layer, parts=parts)
-    moves = 12 + weight_loads(mixed) + weight_loads(up) + weight_loads(down)
+    kernel = functools.partial(
+        mlp_back_kernel, layer=layer, parts=parts, given=len(given), shard=shard
+    )
+    moves = 13 + (3 * width // (2 * shard) if shard else 0)
+    moves += weight_loads(mixed) + weight_loads(up) + weight_loads(down)
     return run(kernel, "mlp_back", 48, inputs, outputs, scratch, 8 * layer + 2, 20, moves)
 
 
-def project_back_kernel(*refs, layer, parts):
-    ins, outs, scratch = split_refs(refs, 8 + parts, 4)
+def project_back_kernel(*refs, layer, parts, closing):
+    ins, outs, scratch = split_refs(refs, 8 + parts + closing, 4 + (closing > 0))
     after_hbm, x_hbm, vec, normed_hbm, queries_hbm, own_hbm, far_hbm, out_hbm = ins[:8]
-    mixed_hbm = ins[8:]
-    gradient_out, weight_out, sums, column_sums = outs
+    mixed_hbm, closing_ins = ins[8 : 8 + parts], ins[8 + parts :]
+    gradient_out, sums, column_sums, weight_out = outs[:4]
     grad_after, x, weight, normed, grad_queries, grad_own, grad_out = scratch[:7]
     landed, together, gradient, grad_weight = scratch[7:11]
-    scatter_refs = scratch[11:19]
-    send_sems, recv_sems, move_sems = scratch[19:]
+    scatter_refs, closing_refs = scratch[11:19], scratch[19:-3]
+    send_sems, recv_sems, move_sems = scratch[-3:]
     net, moves = Net(send_sems, recv_sems), Moves(move_sems)
     rows, width = x.shape
     pair_cols = grad_own.shape[2]
@@ -1028,6 +1077,12 @@
     load_out = moves.load(out_hbm, grad_out)
     load_x = moves.load(x_hbm, x)
     load_after = moves.load(after_hbm, grad_after)
+    if closing:
+        active, down_weight, after, final = closing_refs[:4]
+        load_active = moves.load(closing_ins[0], active)
+        load_after_two = moves.load(closing_ins[1], after)
+        columns = pl.ds(0, down_weight.shape[1])
+        load_down = load_weight(net, moves, closing_ins[2:], columns, down_weight)
     net.barrier([net.core, net.far, net.half])
     arriving = {
         slot: net.copy(far_hbm.at[slot], landed.at[slot], net.half) for slot in (3, 2, 1, 0)
@@ -1046,6 +1101,20 @@
     def back(slots, chunk):
         return dot(flat(together[slots, chunk, :]), weight[...], NT)
 
+    if closing:
+
+        def down(slots, chunk):
+            return dot(flat(active[slots, chunk, :]), down_weight[...], NT)
+
+        load_active.wait()
+        load_down.wait()
+        last = Scatter(net, closing_refs[4:])
+        for key, chunk in enumerate(chunks):
+            last.far_part(key, chunk, down(far, chunk))
+        for key, chunk in enumerate(chunks):
+            last.far_send(key, chunk)
+        last.near_part(down(near, whole))
+        last.near_done()
     scatter = Scatter(net, scatter_refs)
     join(3)
     join(2)
@@ -1076,19 +1145,25 @@
         sums[0:1] += gain_sum
         sums[1:2] += shift_sum
     moves.store(gradient, gradient_out)
+    if closing:
+        load_after_two.wait()
+        for key, chunk in enumerate(chunks):
+            final[chunk, :] = last.result(key, chunk) + after[chunk, :] + vec[layer, 5:6]
+        moves.store(final, outs[-1])
     net.finish()
     moves.finish()
 
 
 def project_back(
-    layer, grad_after, x, vec, mixed, normed, grad_queries, grad_own, grad_far, grad_out, all_cols
+    layer, grad_after, x, vec, mixed, normed, grad_queries, grad_own, grad_far, grad_out, all_cols,
+    closing=(),
 ):
     rows, width = x.shape
     outputs = [
         ((rows, width), F32, False),
-        ((width, width), BF, False),
         ((8, width), F32, True),
         ((1, all_cols), F32, True),
+        ((width, width), BF, False),
     ]
     shapes = [
         ((rows, width), F32),
@@ -1104,64 +1179,135 @@
         ((width, width), BF),
     ]
     scratch = [pltpu.VMEM(shape, dtype) for shape, dtype in shapes] + scatter_scratch(rows, width)
+    copies, moves = 12, 9 + weight_loads(mixed)
+    if closing:
+        active, after, *down = closing
+        outputs.append(((rows, width), F32, False))
+        shapes = [
+            (active.shape, BF), ((width, active.shape[2]), BF), ((rows, width), F32), ((rows, width), F32),
+        ]
+        scratch += [pltpu.VMEM(shape, dtype) for shape, dtype in shapes] + scatter_scratch(rows, width)
+        copies, moves = 18, moves + 3 + weight_loads(down)
     inputs = [
         (grad_after, False), (x, False), (vec, True), (normed, False), (grad_queries, False),
         (grad_own, False), (grad_far, False), (grad_out, False),
-    ] + spaced(mixed)
-    kernel = functools.partial(project_back_kernel, layer=layer, parts=len(mixed))
-    return run(kernel, "project_back", 42, inputs, outputs, scratch, 8 * layer + 3, 12, 9 + weight_loads(mixed))
+    ] + spaced([*mixed, *closing])
+    kernel = functools.partial(
+        project_back_kernel, layer=layer, parts=len(mixed), closing=len(closing)
+    )
+    return run(kernel, "project_back", 42, inputs, outputs, scratch, 8 * layer + 3, copies, moves)
 
 
 def entry_kernel(*refs):
-    (tokens, cotangent, vectors, shard), outs, scratch = split_refs(refs, 4, 4)
-    tokens_out, cotangent_out, vectors_out, weights = outs
-    send_sems, recv_sems, move_sems = scratch
+    ins, outs, scratch = split_refs(refs, 12, 7)
+    tokens, cotangent, value_bias, query_bias, up_bias, shard = ins[:6]
+    x, gradient, grad_rows, vec, bias, hidden_bias, weights = outs
+    vectors, token_land, cotangent_land, vector_land, send_sems, recv_sems, move_sems = scratch
     net, moves = Net(send_sems, recv_sems), Moves(move_sems)
+    rows, cols = x.shape[0], tokens.shape[0]
+    layers = vec.shape[0]
     others = [net.core, net.far, net.far_core]
+    vectors[...] = jnp.zeros_like(vectors)
+    for index, one in enumerate(ins[6:]):
+        for layer in range(layers):
+            vectors[layer * 8 + index : layer * 8 + index + 1] = one[layer : layer + 1]
     net.line(weights.shape[0] // 2)
     net.barrier(others + [net.half], True)
     gathering = GatherJob(net, moves, shard, weights)
-    moved = []
-    for source, target in ((tokens, tokens_out), (cotangent, cotangent_out)):
-        for device in reversed(others):
-            moved.append(net.copy(source.at[device[1]], target.at[net.hid], device))
-        target[net.hid] = source[net.hid]
-    for device in others:
-        moved.append(net.copy(vectors, vectors_out.at[net.hid], device))
-    vectors_out[net.hid] = vectors[...]
-    gathering.forward(0, 1)
-    gathering.finish()
+
+    def block(hid):
+        return pl.ds(pl.multiple_of(hid * rows, rows), rows)
+
+    moved = [
+        net.copy(tokens.at[:, block(device[1])], token_land.at[net.hid], device)
+        for device in reversed(others)
+    ]
+    moved += [net.copy(vectors, vector_land.at[net.hid], device) for device in others]
+    sent = []
+    for chunk in chunks_of(4 * rows, 2):
+        source, own = cotangent.at[:, chunk], cotangent_land.at[net.hid, :, chunk]
+        moved.append(net.copy(source, own, net.core))
+        sent.append((net.copy(source, own, net.far), cotangent_land.at[net.far[1], :, chunk]))
+    token_land[net.hid] = tokens[:, block(net.hid)]
+    cotangent_land[net.hid] = cotangent[...]
+    vector_land[net.hid] = vectors[...]
+    bias[...] = jnp.zeros_like(bias)
+    bias[:, cols : 2 * cols] = value_bias[...]
+    bias[:, 2 * cols : 3 * cols] = query_bias[...]
+    hidden_bias[...] = jnp.zeros_like(hidden_bias)
+    hidden_bias[:, : up_bias.shape[1]] = up_bias[...]
+    gathering.forward(0, 3)
+    for point, (one, landed) in enumerate(sent):
+        one.wait_recv()
+        moved.append(net.copy(landed, landed, net.core))
+        gathering.forward(point + 1, 3)
     for one in moved:
         one.wait_recv()
+    for place in range(4):
+        columns = slice(place * cols, (place + 1) * cols)
+        for layer in range(layers):
+            vec[layer, :, columns] = vector_land[place, layer * 8 : layer * 8 + 8]
+    x[...] = flat(token_land[...]).astype(F32).T
+    for slot, device in enumerate([(net.tok, net.hid)] + others):
+        whole = flat(cotangent_land[:, :, block(device[1])])
+        grad_rows[slot] = whole.astype(F32).T.astype(BF)
+    gradient[...] = grad_rows[0].astype(F32)
+    gathering.finish()
     net.finish()
     moves.finish()
 
 
-def entry(tokens, cotangent, vectors, shard, count):
-    inputs = [(tokens, True), (cotangent, True), (vectors, True), (shard, False)]
+def entry(tokens, cotangent, value_bias, query_bias, up_bias, shard, vectors, count, used_cols):
+    cols, rows = tokens.shape[0], tokens.shape[1] // 4
+    layers, feed = up_bias.shape
+    inputs = [
+        (tokens, True), (cotangent, True), (value_bias, True), (query_bias, True), (up_bias, True),
+        (shard, False),
+    ] + [(one, True) for one in vectors]
     outputs = [
-        (tokens.shape, BF, True),
-        (cotangent.shape, BF, True),
-        ((4,) + vectors.shape, F32, True),
+        ((rows, 4 * cols), F32, True),
+        ((rows, 4 * cols), F32, True),
+        ((4, rows, 4 * cols), BF, True),
+        ((layers, 8, 4 * cols), F32, True),
+        ((layers, used_cols), F32, True),
+        ((layers, feed + -feed % LANES), F32, True),
         ((count,) + shard.shape, BF, False),
     ]
-    return run(entry_kernel, "entry", 40, inputs, outputs, [], 4, 9 + job_copies(count), 1)
-
-
-def finish_kernel(*refs):
-    (final, gradient, wide, narrow, broad, grads), outs, scratch = split_refs(refs, 6, 5)
-    final_out, gradient_out, sums, hidden_sums, total = outs
-    final_land, gradient_land, wide_land, across_land, along_land = scratch[:5]
-    across_hidden, along_hidden = scratch[5:7]
-    job_refs = scratch[7:11]
-    send_sems, recv_sems, move_sems = scratch[11:]
+    scratch = [
+        pltpu.VMEM((layers * 8, cols), F32),
+        pltpu.VMEM((4, cols, rows), BF),
+        pltpu.VMEM((4,) + cotangent.shape, BF),
+        pltpu.VMEM((4, layers * 8, cols), F32),
+    ]
+    return run(entry_kernel, "entry", 50, inputs, outputs, scratch, 4, 12 + job_copies(count), 1)
+
+
+def finish_kernel(*refs, layers):
+    ins, outs, scratch = split_refs(refs, 3 + 4 * layers, 12)
+    final_rows, gradient_rows, grads = ins[:3]
+    layer_sums = [ins[3 + 4 * layer : 7 + 4 * layer] for layer in range(layers)]
+    final_out, gradient_out, total = outs[:3]
+    wide_outs, query_out, value_out, hidden_out = outs[3:9], outs[9], outs[10], outs[11]
+    final, gradient, wide, sums, hidden_sums = scratch[:5]
+    final_land, gradient_land, wide_land, across_land, along_land = scratch[5:10]
+    across_hidden, along_hidden = scratch[10:12]
+    job_refs = scratch[12:16]
+    send_sems, recv_sems, move_sems = scratch[16:]
     net, moves = Net(send_sems, recv_sems), Moves(move_sems)
     count = grads.shape[0] // 2
     others = [net.core, net.far, net.far_core]
     net.line(count)
     net.barrier(others + [net.half], True)
+    scattering = ScatterParts(net, moves, grads, job_refs)
+    cols, rows = wide.shape[2], final_rows.shape[0]
+    for layer, (one, two, _, _) in enumerate(layer_sums):
+        both = one[...] + two[...]
+        for place in range(4):
+            columns = slice(place * cols, (place + 1) * cols)
+            wide[place, layer * 8 : layer * 8 + 8] = both[:, columns]
     summed = [net.copy(wide.at[device[1]], wide_land.at[net.hid], device) for device in others]
-    scattering = ScatterParts(net, moves, grads, job_refs)
+    for target, source in ((final, final_rows), (gradient, gradient_rows)):
+        target[...] = source[...].T.astype(BF).reshape(target.shape)
     moved = []
     for source, target in ((final, final_land), (gradient, gradient_land)):
         for device in reversed(others):
@@ -1177,8 +1323,13 @@
             one.wait_recv()
         top = wide.shape[1]
         sums[:top] = wide_land[0] + wide_land[1] + wide_land[2] + wide_land[3]
-        sums[top:] = narrow[...]
-        hidden_sums[...] = broad[...]
+        sums[top:] = jnp.zeros((sums.shape[0] - top, cols), F32)
+        hidden_sums[...] = jnp.zeros_like(hidden_sums)
+        for layer, (_, _, column_sums, hidden) in enumerate(layer_sums):
+            for place in range(3):
+                row = top + layer * 3 + place
+                sums[row : row + 1] = column_sums[:, place * cols : (place + 1) * cols]
+            hidden_sums[layer : layer + 1] = hidden[...]
         return [net.copy(value, across, net.half) for value, across, _ in pairs]
 
     def spread_sums(swaps):
@@ -1228,37 +1379,51 @@
     for one in moved:
         one.wait_recv()
     for source, target in ((final_land, final_out), (gradient_land, gradient_out)):
-        target[...] = flat(source[...]).astype(F32)
+        for place in range(4):
+            target[:, place * rows : (place + 1) * rows] = source[place].astype(F32)
+    for layer in range(layers):
+        one = slice(layer, layer + 1)
+        for index, out in enumerate(wide_outs):
+            out[one, :] = sums[layer * 8 + index : layer * 8 + index + 1]
+        row = layers * 8 + layer * 3
+        value_out[one, :] = sums[row + 1 : row + 2]
+        query_out[one, :] = sums[row + 2 : row + 3]
+        hidden_out[one, :] = hidden_sums[one, : hidden_out.shape[1]]
     scattering.finish(total)
     net.finish(swaps)
 
 
-def finish(final, gradient, wide, narrow, broad, grads):
-    count = grads.shape[0] // 2
-    sums = (wide.shape[1] + narrow.shape[0], wide.shape[2])
-    rows = (final.shape[0] * final.shape[1], final.shape[2])
+def finish(final, gradient, grads, layer_sums, head_cols, feed):
+    count, layers = grads.shape[0] // 2, len(layer_sums)
+    rows = final.shape[0]
+    sums = (layers * 11 + -layers * 11 % 8, head_cols)
+    hidden = (layers + -layers % 8, layer_sums[0][3].shape[1])
+    vector = ((layers, head_cols), F32, True)
     outputs = [
-        (rows, F32, True),
-        (rows, F32, True),
-        (sums, F32, True),
-        (broad.shape, F32, True),
+        ((head_cols, 4 * rows), F32, True),
+        ((head_cols, 4 * rows), F32, True),
         (grads.shape[1:], F32, True),
-    ]
+    ] + [vector] * 8
+    outputs.append(((layers, feed), F32, True))
+    blocks, wide = (4, head_cols, rows), (4, layers * 8, head_cols)
     scratch = [
-        pltpu.VMEM(final.shape, BF),
-        pltpu.VMEM(final.shape, BF),
-        pltpu.VMEM(wide.shape, F32),
+        pltpu.VMEM(blocks, BF),
+        pltpu.VMEM(blocks, BF),
+        pltpu.VMEM(wide, F32),
+        pltpu.VMEM(sums, F32),
+        pltpu.VMEM(hidden, F32),
+        pltpu.VMEM(blocks, BF),
+        pltpu.VMEM(blocks, BF),
+        pltpu.VMEM(wide, F32),
         pltpu.VMEM(sums, F32),
         pltpu.VMEM((count,) + sums, F32),
-        pltpu.VMEM(broad.shape, F32),
-        pltpu.VMEM((count,) + broad.shape, F32),
+        pltpu.VMEM(hidden, F32),
+        pltpu.VMEM((count,) + hidden, F32),
     ] + part_scratch(*grads.shape)
-    inputs = [
-        (final, True), (gradient, True), (wide, True), (narrow, True), (broad, True), (grads, False),
-    ]
-    return run(
-        finish_kernel, "finish", 40, inputs, outputs, scratch, 5, 12 + 7 * count, 1 + count
-    )
+    inputs = [(final, True), (gradient, True), (grads, False)]
+    inputs += [(one, True) for four in layer_sums for one in four]
+    kernel = functools.partial(finish_kernel, layers=layers)
+    return run(kernel, "finish", 40, inputs, outputs, scratch, 5, 12 + 7 * count, 1 + count)
 
 
 def key_ranges(own_ids, row_ids, rows):
@@ -1304,12 +1469,6 @@
     def shards(part):
         return jnp.pad(part, ((0, shard_pad), (0, 0)))
 
-    def by_tokens(array):
-        return array.transpose(1, 0, 2).reshape(rows, 4 * array.shape[2]).astype(F32)
-
-    def by_features(array):
-        return array.reshape(rows, 4, head_cols).transpose(1, 0, 2)
-
     def joined(gathered):
         return gathered[:, :shard].reshape(width, gathered.shape[2])
 
@@ -1325,22 +1484,10 @@
         )
         for layer in range(layers)
     ]
-    vectors = jnp.stack(
-        [first_gain, first_shift, output_bias, second_gain, second_shift, down_bias], axis=1
+    vectors = (first_gain, first_shift, output_bias, second_gain, second_shift, down_bias)
+    x, gradient, grad_rows, vectors, bias, up_bias, mixed = entry(
+        tokens.T, cotangent.T, value_bias, query_bias, up_bias, mixed_parts[0], vectors, count, used_cols
     )
-    vectors = jnp.pad(vectors, ((0, 0), (0, 2), (0, 0))).reshape(layers * 8, head_cols)
-    x, gradient, vectors, mixed = entry(
-        tokens.reshape(4, rows, head_cols),
-        cotangent.reshape(4, rows, head_cols),
-        vectors,
-        mixed_parts[0],
-        count,
-    )
-    x, gradient = by_tokens(x), by_tokens(gradient)
-    vectors = vectors.transpose(1, 0, 2).reshape(layers, 8, width)
-    bias = side_by_side(jnp.zeros_like(value_bias), value_bias, query_bias)
-    bias = jnp.pad(bias, ((0, 0), (0, used_cols - 3 * head_cols)))
-    up_bias = padded(up_bias)
 
     halves = [(place, place ^ 1) for place in range(count)]
     lines = [[place * 2 + low for place in range(count // 2)] for low in range(2)]
@@ -1363,9 +1510,11 @@
             return parts
         return [both_halves(*parts).transpose(1, 0, 2, 3).reshape(width, part.shape[1])]
 
-    def across_first(part):
-        pair = both_halves(part, swap(part)).reshape(2 * shard, part.shape[1])
-        return along(pair)
+    def hold(*values):
+        return lax.optimization_barrier(values)
+
+    def pair_rows(part, other):
+        return both_halves(part, other).reshape(2 * shard, part.shape[1])
 
     def up_part(layer):
         return padded(up_weight[layer])
@@ -1373,25 +1522,35 @@
     def down_part(layer):
         return padded(down_weight[layer].T)
 
-    weights = [[[joined(mixed)], along_first(up_part(0)), [across_first(down_part(0))]]]
+    ups, weights = [along_first(up_part(0))], [[joined(mixed)]]
+    early = down_part(0)
+    early, early_other, x = hold(early, swap(early), x)
+    downs = [[along(pair_rows(early, early_other))]]
     for layer in range(1, layers):
-        mixed = along_first(mixed_parts[layer][:shard])
-        weights.append([mixed, [across_first(up_part(layer))], [across_first(down_part(layer))]])
+        weights.append(along_first(mixed_parts[layer][:shard]))
+        coming = up_part(layer)
+        ups.append([along(pair_rows(coming, swap(coming)))])
     saved = []
     for layer in range(layers):
-        mixed, up, down = weights[layer]
+        mixed, up = weights[layer], ups[layer]
+        more = layer + 1 < layers
         normed, queries, own_pairs, far_pairs = project(layer, x, vectors, bias, mixed, head_cols)
+        if layer > 0:
+            queries, coming, coming_other = hold(queries, coming, coming_other)
+            downs.append([along(pair_rows(coming, coming_other))])
         mixture, logsum = attend(
             meta, queries, own_pairs, far_pairs, own_ids[:, None], row_ids[None, :], lead
         )
-        x_next, after, normed_two, active, slope = mlp(
-            layer, mixture, x, vectors, up_bias, mixed, up, down
+        if more:
+            coming, mixture = hold(down_part(layer + 1), mixture)
+            coming_other = swap(coming)
+        after, normed_two, active, slope, *x_next = mlp(
+            layer, mixture, x, vectors, up_bias, mixed, up, downs[layer], not more
         )
         saved.append(
             (x, normed, queries, own_pairs, far_pairs, mixture, logsum, after, normed_two, active, slope)
         )
-        x = x_next
-    final = x
+        x = x_next[0] if x_next else None
 
     def by_halves(part):
         own = lax.dynamic_index_in_dim(part, tok % 2, 1, keepdims=False)
@@ -1403,13 +1562,11 @@
             part, "tok", scatter_dimension=0, tiled=True, axis_index_groups=lines
         )
 
-    def hold(*values):
-        return lax.optimization_barrier(values)
-
-    def halves_of(part):
-        part = part.reshape(-1, 2, shard, part.shape[1])
-        own, other = by_halves(part)
-        return own, swap(other)
+    def halves_of(parts):
+        if len(parts) == 1:
+            part = parts[0].reshape(-1, 2, shard, parts[0].shape[1])
+            parts = by_halves(part)
+        return parts[0], swap(parts[1])
 
     def added(own, other):
         return (own.astype(F32) + other.astype(F32)).astype(BF)
@@ -1417,74 +1574,63 @@
     def in_rows(part):
         return part.reshape(-1, part.shape[-1])
 
+    split = shard if shard % 16 == 0 else 0
     mixed_grads, up_grads, down_grads = [None] * layers, [None] * layers, [None] * layers
-    wide, narrow, broad = [None] * layers, [None] * layers, [None] * layers
-    grads = None
+    layer_sums = [None] * layers
+    grads = final = None
     for layer in reversed(range(layers)):
         x, normed, queries, own_pairs, far_pairs, mixture, logsum, after, normed_two, active, slope = saved[layer]
-        mixed, up, down = weights[layer]
+        mixed, up, down = weights[layer], ups[layer], downs[layer]
         last = layer + 1
         if last < layers:
-            gradient, down_grad, up_grad = hold(gradient, down_grads[last], up_grads[last])
-            up_grads[last] = sum_along(in_rows(up_grad))
-            mixed_own, mixed_other = halves_of(grads)
-            down_own, down_other = halves_of(down_grad)
-        grad_after, grad_mixture, grad_up, grad_down, grad_out, sums_two, hidden_sums = mlp_back(
-            layer, gradient, after, vectors, mixed, up, down, mixture, normed_two, active, slope
+            gradient, down_grads[last] = hold(gradient, down_grads[last])
+            down_own, down_other = halves_of([down_grads[last]])
+        grad_after, grad_mixture, grad_down, grad_out, sums_two, hidden_sums, *grad_up = mlp_back(
+            layer, gradient, after, vectors, mixed, up, down, mixture, normed_two, active, slope,
+            () if last < layers else (grad_rows,), split,
         )
         if last < layers:
-            mixed_other, down_other, grad_mixture = hold(mixed_other, down_other, grad_mixture)
+            down_other, up_grads[last], grad_mixture = hold(
+                down_other, up_grads[last], grad_mixture
+            )
             down_grads[last] = added(down_own, down_other)[0]
-            mixed_grad = added(mixed_own, mixed_other)
-            grad_mixture, up_grads[last], mixed_grad = hold(grad_mixture, up_grads[last], mixed_grad)
-            down_rows = grad_down.reshape(count // 2, 2 * shard, feed_cols)
-            together = jnp.concatenate([mixed_grad, down_rows], axis=1)
-            together = sum_along(in_rows(together))
-        else:
-            down_grads[layer] = sum_along(grad_down)
+            grad_down, up_grads[last] = hold(grad_down, up_grads[last])
+        down_grads[layer] = sum_along(grad_down)
         up_own, up_other = halves_of(grad_up)
         grad_queries, grad_own, grad_far = attend_back(
             meta, queries, own_pairs, far_pairs, own_ids[None, :], row_ids[:, None],
             grad_mixture, logsum,
         )
         up_other, grad_far = hold(up_other, grad_far)
-        up_grads[layer] = added(up_own, up_other)
-        gradient, grads, sums_one, column_sums = project_back(
+        up_grad = added(up_own, up_other)
+        if last < layers:
+            grad_after, mixed_grads[last] = hold(grad_after, mixed_grads[last])
+            mixed_own, mixed_other = halves_of([mixed_grads[last]])
+        grad_after, up_grad = hold(grad_after, up_grad)
+        up_grads[layer] = sum_along(in_rows(up_grad))
+        gradient, sums_one, column_sums, grads, *closed = project_back(
             layer, grad_after, x, vectors, mixed, normed, grad_queries, grad_own, grad_far,
-            grad_out, used_cols,
+            grad_out, used_cols, () if last < layers else (active, after, *down),
         )
+        final = closed[0] if closed else final
         if last < layers:
-            grads, together = hold(grads, together)
-            mixed_grads[last], down_grads[layer] = together[:shard], together[shard:]
-        wide[layer] = sums_one + sums_two
-        narrow[layer] = column_sums[0, : 3 * head_cols].reshape(3, head_cols)
-        broad[layer] = hidden_sums
-    up_grad, down_grads[0] = hold(up_grads[0], down_grads[0])
-    up_grads[0] = sum_along(in_rows(up_grad))
-    down_own, down_other = halves_of(down_grads[0])
-    grads = separate(grads)
-    wide = jnp.concatenate(wide, axis=0)
-    wide = wide.reshape(layers * 8, 4, head_cols).transpose(1, 0, 2)
-
-    def tall(parts):
-        rows_of = jnp.concatenate(parts, axis=0)
-        return jnp.pad(rows_of, ((0, -rows_of.shape[0] % 8), (0, 0)))
-
-    final, gradient, sums, broad, first_grad = finish(
-        by_features(final.astype(BF)),
-        by_features(gradient.astype(BF)),
-        wide,
-        tall(narrow),
-        tall(broad),
-        grads,
+            mixed_other, gradient = hold(mixed_other, gradient)
+            mixed_grads[last] = added(mixed_own, mixed_other)[0]
+        if layer > 0:
+            mixed_grads[layer] = sum_along(grads)
+        layer_sums[layer] = (sums_one, sums_two, column_sums, hidden_sums)
+    gradient, down_grads[0] = hold(gradient, down_grads[0])
+    down_own, down_other = halves_of([down_grads[0]])
+    final, gradient, mixed_grad, *small = finish(
+        final, gradient, separate(grads), layer_sums, head_cols, feed
     )
-    mixed_grads[0] = first_grad[:shard]
-    down_other, up_grads[0], final, gradient, sums, broad, mixed_grads[0] = hold(
-        down_other, up_grads[0], final, gradient, sums, broad, mixed_grads[0]
+    down_other, up_grads[0], final, gradient, mixed_grad, *small = hold(
+        down_other, up_grads[0], final, gradient, mixed_grad, *small
     )
+    mixed_grads[0] = mixed_grad[:shard]
     down_grads[0] = added(down_own, down_other)[0]
-    wide = sums[: layers * 8].reshape(layers, 8, head_cols)
-    narrow = sums[layers * 8 : layers * 11].reshape(layers, 3, head_cols)
+    first_gain, first_shift, output_bias, second_gain, second_shift, down_bias = small[:6]
+    query_bias, value_bias, up_bias = small[6:]
 
     def mixed_columns(start):
         columns = slice(start * head_cols, (start + 1) * head_cols)
@@ -1494,23 +1640,23 @@
         return jnp.stack([part[:, :feed].astype(F32) for part in parts])
 
     return (
-        final,
-        gradient,
-        wide[:, 0],
-        wide[:, 1],
+        final.T,
+        gradient.T,
+        first_gain,
+        first_shift,
         mixed_columns(2),
-        narrow[:, 2],
+        query_bias,
         mixed_columns(0),
         mixed_columns(1),
-        narrow[:, 1],
+        value_bias,
         mixed_columns(3).transpose(0, 2, 1),
-        wide[:, 2],
-        wide[:, 3],
-        wide[:, 4],
+        output_bias,
+        second_gain,
+        second_shift,
         hidden_columns(up_grads),
-        broad[:layers, :feed],
+        up_bias,
         hidden_columns(down_grads).transpose(0, 2, 1),
-        wide[:, 5],
+        down_bias,
     )
 
 

time: 682 us -> 629 us (0.922)
  local copies, waits for them, and re-layouts: 47.9 us -> 22.9 us
  other arithmetic: 33.4 us -> 12.6 us
    pallas_call x10, Pallas kernels: 472 us -> 453 us  [run(): pl.pallas_call(kernel, name=name, cost_estimate=micros(duration), out_sha...]
    pallas_call x2, Pallas kernels: 50 us -> 61.7 us  [attend_back(): pl.pallas_call(functools.partial(attend_back_kernel, heads=heads), name='...]
  transfers between devices with their start and end apart: 19 -> 20, of which waited for: 2 -> 2; matrix products, arithmetic and copies ran while one was open for 9% -> 3% of each run, Pallas kernels for 68% -> 82%
where the time goes in v3:
time: 629 us; the launch traced here: 621 us
  Pallas kernels  551 us (88%)
  local copies, waits for them, and re-layouts  22.9 us (4%)
  between operations  15.2 us (2%)
  other arithmetic  12.6 us (2%)
  waiting for transfers between devices  9.81 us (2%)
  starting transfers between devices  9.61 us (2%)
    pallas_call x10, Pallas kernels, run(): pl.pallas_call(kernel, name=name, cost_estimate=micros(duration), out_sha...  453 us
    pallas_call x2, Pallas kernels, attend_back(): pl.pallas_call(functools.partial(attend_back_kernel, heads=heads), name='...  61.7 us
    pallas_call x2, Pallas kernels, attend(): pl.pallas_call(functools.partial(attend_kernel, heads=heads), name='atten...  37.1 us
  transfers between devices with their start and end apart: 20, of which 2 were waited for; matrix products, arithmetic and copies ran while one was open for 3% of the time, Pallas kernels for 82%

profile of v3, /device:TPU:0, one launch (start us, length us, event | category | flops | bytes accessed | tf_op | source)
XLA Modules:
  0.0 621.5 jit_solution(16038656798070335612)
XLA Ops:
  7.2 1.2 slice_bitcast_fusion.4
  8.4 0.8 pad.15
  9.4 3.0 collective-permute-start
  12.7 1.0 concatenate.11
  13.7 1.0 concatenate.9.refs_5_
  14.7 62.2 %entry.1 = (f32[256,1152]{1,0:T(8,128)}, f32[256,1152]{1,0:T(8,128)}, bf16[4,256,1152]{2,1,0:T(8,128)(2,1)}, f32[2,8,1152]{2,1,0:T(8,128)}, f32[2,896]{1,0:T(2,1...) custom-call(bf16[288,1024]{1,0:T(8,128)(2,1)} %bitcast.172, bf16[288,1024]{1,0:T(8,128)(2,1)} %bitcast.173, ...), custom_call_target="tpu_custom_call" | custom-call | flops 49999998976 | tf_op jit(solution)/shard_map/entry/pallas_call | solution.py:329
  76.9 0.7 dynamic_slice.25
  77.6 0.7 dynamic_slice.26
  78.3 0.2 slice_reduce_fusion.1
  78.5 0.2 select_reduce_fusion.1
  78.9 1.0 copy.47.query_ids
  80.0 0.6 pad_add_fusion.1.meta
  80.7 0.9 pad_maximum_fusion
  81.7 33.7 %project.2 = (bf16[4,256,1152]{2,1,0:T(8,128)(2,1)}, bf16[4,256,288]{2,1,0:T(8,128)(2,1)}, bf16[4,256,576]{2,1,0:T(8,128)(2,1)}, bf16[4,256,576]{2,1,0:T(8,128)(2,1)}) custom-call(f32[256,1152]{1,0:T(8,128)} %get-tuple-element.133.refs_0_.refs_1_, f32[2,8,1152]{2,1,0:T(8,128)} %get-tuple-element.134.refs_1_.refs_2_, f32[2,896]{1,0:T(2,128)} %get-tuple-element.135.refs_2_, ...), custom_call_target="tpu_custom_call" | custom-call | flops 40000000000 | tf_op jit(solution)/shard_map/project/pallas_call | solution.py:329
  115.4 1.6 collective-permute-start.1
  116.9 18.5 %attend.2 = (bf16[4,256,384]{2,1,0:T(8,128)(2,1)}, f32[8,1024]{1,0:T(8,128)}) custom-call(s32[10]{0:T(128)} %pad_add_fusion.1.meta, bf16[4,256,288]{2,1,0:T(8,128)(2,1)} %get-tuple-element.137.queries, bf16[4,256,576]{2,1,0:T(8,128)(2,1)} %get-tuple-element.138.own_pairs, bf16[4,256,576]{2,1,0:T(8,128)(2,1)} %get-tuple-element.139.far_pairs, ...), custom_call_target="tpu_custom_call" | custom-call | flops 22000001024 | tf_op jit(solution)/shard_map/attend/pallas_call | solution.py:649
  135.6 0.9 pad_maximum_fusion.1
  136.5 0.3 all-gather.14.cloned.1.call-start
  136.9 2.1 collective-permute-start.2
  139.0 8.8 %collective-permute-done.1 = bf16[576,1152]{1,0:T(8,128)(2,1)} collective-permute-done((bf16[576,1152]{1,0:T(8,128)(2,1)}, bf16[576,1152]{1,0:T(8,128)(2,1)}, u32[]{:S(2)}, u32[]{:S(2)}) %collective-permute-start.1) | collective-permute-done | bytes 1327136 | tf_op jit(solution)/shard_map/ppermute | solution.py:1496
  147.8 46.6 %mlp.2 = (f32[256,1152]{1,0:T(8,128)}, bf16[4,256,1152]{2,1,0:T(8,128)(2,1)}, bf16[4,256,1152]{2,1,0:T(8,128)(2,1)}, bf16[4,256,1152]{2,1,0:T(8,128)(2,1)}, f32[256,1152]{1,0:T(8,128)}) custom-call(bf16[4,256,384]{2,1,0:T(8,128)(2,1)} %get-tuple-element.141.refs_0_.refs_3_, f32[256,1152]{1,0:T(8,128)} %get-tuple-element.133.refs_0_.refs_1_, ...), custom_call_target="tpu_custom_call" | custom-call | flops 48000000000 | tf_op jit(solution)/shard_map/mlp/pallas_call | solution.py:329
  194.4 42.2 %project.3 = (bf16[4,256,1152]{2,1,0:T(8,128)(2,1)}, bf16[4,256,288]{2,1,0:T(8,128)(2,1)}, bf16[4,256,576]{2,1,0:T(8,128)(2,1)}, bf16[4,256,576]{2,1,0:T(8,128)(2,1)}) custom-call(f32[256,1152]{1,0:T(8,128)} %get-tuple-element.145.refs_0_.refs_1_, f32[2,8,1152]{2,1,0:T(8,128)} %get-tuple-element.134.refs_1_.refs_2_, f32[2,896]{1,0:T(2,128)} %get-tuple-element.135.refs_2_, ...), custom_call_target="tpu_custom_call" | custom-call | flops 40000000000 | tf_op jit(solution)/shard_map/project/pallas_call | solution.py:329
  236.7 0.9 pad_maximum_fusion.2
  237.7 18.5 %attend.3 = (bf16[4,256,384]{2,1,0:T(8,128)(2,1)}, f32[8,1024]{1,0:T(8,128)}) custom-call(s32[10]{0:T(128)} %pad_add_fusion.1.meta, bf16[4,256,288]{2,1,0:T(8,128)(2,1)} %get-tuple-element.148.queries, bf16[4,256,576]{2,1,0:T(8,128)(2,1)} %get-tuple-element.149.own_pairs, bf16[4,256,576]{2,1,0:T(8,128)(2,1)} %get-tuple-element.150.far_pairs, ...), custom_call_target="tpu_custom_call" | custom-call | flops 22000001024 | tf_op jit(solution)/shard_map/attend/pallas_call | solution.py:649
  256.2 36.7 %mlp.3 = (f32[256,1152]{1,0:T(8,128)}, bf16[4,256,1152]{2,1,0:T(8,128)(2,1)}, bf16[4,256,1152]{2,1,0:T(8,128)(2,1)}, bf16[4,256,1152]{2,1,0:T(8,128)(2,1)}) custom-call(bf16[4,256,384]{2,1,0:T(8,128)(2,1)} %get-tuple-element.151.refs_0_.refs_3_, f32[256,1152]{1,0:T(8,128)} %get-tuple-element.145.refs_0_.refs_1_, ...), custom_call_target="tpu_custom_call" | custom-call | flops 48000000000 | tf_op jit(solution)/shard_map/mlp/pallas_call | solution.py:329
  293.0 41.5 %mlp_back.2 = (f32[256,1152]{1,0:T(8,128)}, bf16[4,256,384]{2,1,0:T(8,128)(2,1)}, bf16[1152,1152]{1,0:T(8,128)(2,1)}, bf16[1152,384]{1,0:T(8,128)(2,1)}, f32[8,1...) custom-call(f32[256,1152]{1,0:T(8,128)} %get-tuple-element.131.refs_0_, ...), custom_call_target="tpu_custom_call" | custom-call | flops 48000000000 | tf_op jit(solution)/shard_map/mlp_back/pallas_call | solution.py:329
  334.6 0.6 copy-done.19
  335.2 1.3 copy.49.key_ids
  336.5 31.2 %attend_back.2 = (bf16[4,256,288]{2,1,0:T(8,128)(2,1)}, bf16[4,256,576]{2,1,0:T(8,128)(2,1)}, bf16[4,256,576]{2,1,0:T(8,128)(2,1)}) custom-call(s32[10]{0:T(128)} %pad_add_fusion.1.meta, bf16[4,256,288]{2,1,0:T(8,128)(2,1)} %get-tuple-element.148.queries, bf16[4,256,576]{2,1,0:T(8,128)(2,1)} %get-tuple-element.149.own_pairs, ...), custom_call_target="tpu_custom_call" | custom-call | flops 36999999488 | tf_op jit(solution)/shard_map/attend_back/pallas_call | solution.py:749
  367.7 0.6 collective-permute-done.5
  368.3 1.4 add_convert_fusion.1
  369.8 40.9 %project_back.2 = (f32[256,1152]{1,0:T(8,128)}, f32[8,1152]{1,0:T(8,128)}, f32[1,896]{1,0:T(1,128)}, bf16[1152,1152]{1,0:T(8,128)(2,1)}, f32[256,1152]{1,0:T(8,128)}) custom-call(f32[256,1152]{1,0:T(8,128)} %get-tuple-element.166.refs_0_, f32[256,1152]{1,0:T(8,128)} %get-tuple-element.145.refs_0_.refs_1_, f32[2,8,1152]{2,1,0:T(8,128)} %get-tuple-element.134.refs_1_.refs_2_, ...), custom_call_target="tpu_custom_call" | custom-call | flops 41999998976 | tf_op jit(solution)/shard_map/project_back/pallas_call | solution.py:329
  410.8 1.0 dynamic-slice_bitcast_fusion.1
  411.9 0.9 collective-permute-start.8
  412.8 47.3 %mlp_back.3 = (f32[256,1152]{1,0:T(8,128)}, bf16[4,256,384]{2,1,0:T(8,128)(2,1)}, bf16[1152,1152]{1,0:T(8,128)(2,1)}, bf16[1152,384]{1,0:T(8,128)(2,1)}, f32[8,1...) custom-call(f32[256,1152]{1,0:T(8,128)} %get-tuple-element.174.refs_0_, ...), custom_call_target="tpu_custom_call" | custom-call | flops 48000000000 | tf_op jit(solution)/shard_map/mlp_back/pallas_call | solution.py:329
  460.1 1.2 collective-permute-start.7
  461.3 0.7 copy-done.10
  462.0 30.5 %attend_back.3 = (bf16[4,256,288]{2,1,0:T(8,128)(2,1)}, bf16[4,256,576]{2,1,0:T(8,128)(2,1)}, bf16[4,256,576]{2,1,0:T(8,128)(2,1)}) custom-call(s32[10]{0:T(128)} %pad_add_fusion.1.meta, bf16[4,256,288]{2,1,0:T(8,128)(2,1)} %get-tuple-element.137.queries, bf16[4,256,576]{2,1,0:T(8,128)(2,1)} %get-tuple-element.138.own_pairs, ...), custom_call_target="tpu_custom_call" | custom-call | flops 36999999488 | tf_op jit(solution)/shard_map/attend_back/pallas_call | solution.py:749
  492.7 0.8 copy-done.12
  493.6 0.4 copy-done
  494.0 1.4 add_convert_fusion
  495.5 46.7 %project_back.3 = (f32[256,1152]{1,0:T(8,128)}, f32[8,1152]{1,0:T(8,128)}, f32[1,896]{1,0:T(1,128)}, bf16[1152,1152]{1,0:T(8,128)(2,1)}) custom-call(f32[256,1152]{1,0:T(8,128)} %get-tuple-element.192.refs_0_, f32[256,1152]{1,0:T(8,128)} %get-tuple-element.133.refs_0_.refs_1_, f32[2,8,1152]{2,1,0:T(8,128)} %get-tuple-element.134.refs_1_.refs_2_, ...), custom_call_target="tpu_custom_call" | custom-call | flops 41999998976 | tf_op jit(solution)/shard_map/project_back/pallas_call | solution.py:329
  542.5 1.7 dynamic-slice_bitcast_fusion
  544.3 55.0 %finish.1 = (f32[288,1024]{1,0:T(8,128)}, f32[288,1024]{1,0:T(8,128)}, f32[144,1152]{1,0:T(8,128)}, f32[2,288]{1,0:T(2,128)}, f32[2,288]{1,0:T(2,128)}, /*index=...) custom-call(f32[256,1152]{1,0:T(8,128)} %get-tuple-element.205.refs_, ...), custom_call_target="tpu_custom_call" | custom-call | flops 40000000000 | tf_op jit(solution)/shard_map/finish/pallas_call | solution.py:329
  599.5 0.9 copy-done.13
  600.5 0.2 slice_bitcast_fusion.8
  600.7 1.2 convert_bitcast_fusion
  601.9 1.2 maximum_convert_fusion
  603.0 0.8 maximum_bitcast_fusion
  603.8 0.8 pad_maximum_fusion.5
  604.6 0.8 pad_maximum_fusion.4
  605.4 0.8 pad_maximum_fusion.3
  606.2 1.0 copy.62
  607.2 0.7 copy-done.3
  607.9 1.0 copy.63
  609.0 0.6 copy.64
  609.5 0.6 copy.65
  610.1 0.6 copy.66
  610.7 0.6 copy.67
  611.3 0.6 copy.68
  611.9 0.6 copy.69
  612.4 0.6 copy.70
  613.0 0.6 copy.71
  613.6 0.6 copy.72
  (122 shorter events, 2.4 us)
Async XLA Ops:
  7.2 2.1 copy-start.9
  7.2 108.2 %all-gather.6.cloned.1.call-start = ((), (), s32[]{:S(2)}) async-start(), calls=%async_computation.5 | async-start | bytes 1658880 | tf_op jit(solution)/shard_map/all_gather | solution.py:1503
  9.2 3.3 copy-start.16
  9.2 3.4 copy-start.17
  9.2 127.6 %all-gather.10.cloned.1.call-start = ((), (), s32[]{:S(2)}) async-start(), calls=%async_computation.7 | async-start | bytes 1658880 | tf_op jit(solution)/shard_map/all_gather | solution.py:1503
  9.4 3.3 copy-start.14
  9.4 3.3 copy-start.15
  9.4 71.2 %collective-permute-start = (bf16[144,1152]{1,0:T(8,128)(2,1)S(1)}, bf16[144,1152]{1,0:T(8,128)(2,1)S(1)}, u32[]{:S(2)}, u32[]{:S(2)}) collective-permute-start(bf16[144,1152]{1,0:T(8,128)(2,1)S(1)} %pad.14), channel_id=1, source_target_pairs={{0,4},{4,0},{8,12},{12,8},{16,20},{20,16},{24,28},{28,24},{1,5},{5... | collective-permute-start | bytes 995336 | tf_op jit(solution)/shard_map/ppermute | solution.py:1496
  12.5 123.0 %collective-permute-start.4 = (bf16[144,1152]{1,0:T(8,128)(2,1)S(1)}, bf16[144,1152]{1,0:T(8,128)(2,1)S(1)}, u32[]{:S(2)}, u32[]{:S(2)}) collective-permute-start(bf16[144,1152]{1,0:T(8,128)(2,1)S(1)} %pad.16), channel_id=1, source_target_pairs={{0,4},{4,0},{8,12},{12,8},{16,20},{20,16},{24,28},{28,24},{1,5},{5... | collective-permute-start | bytes 995336 | tf_op jit(solution)/shard_map/ppermute | solution.py:1496
  13.7 134.1 %all-gather.8.cloned.1.call-start = ((), (), s32[]{:S(2)}) async-start(), calls=%async_computation.6 | async-start | bytes 3317760 | tf_op jit(solution)/shard_map/all_gather | solution.py:1503
  77.6 4.0 copy-start.18
  78.3 3.3 copy-start.20
  81.6 174.6 %all-gather.12.cloned.1.call-start = ((), (), s32[]{:S(2)}) async-start(), calls=%async_computation.8 | async-start | bytes 3317760 | tf_op jit(solution)/shard_map/all_gather | solution.py:1503
  115.4 32.4 %collective-permute-start.1 = (bf16[576,1152]{1,0:T(8,128)(2,1)}, bf16[576,1152]{1,0:T(8,128)(2,1)}, u32[]{:S(2)}, u32[]{:S(2)}) collective-permute-start(bf16[576,1152]{1,0:T(8,128)(2,1)} %all-gather.6.cloned.1.call-done), channel_id=1, source_target_pairs={{0,4},{4,0},{8,12},{12,8},{16,20},{20,16},{24,28},{28,24},{1,5},{5... | collective-permute-start | bytes 3981320 | tf_op jit(solution)/shard_map/ppermute | solution.py:1496
  135.5 101.1 %collective-permute-start.3 = (bf16[144,1152]{1,0:T(8,128)(2,1)S(1)}, bf16[144,1152]{1,0:T(8,128)(2,1)S(1)}, u32[]{:S(2)}, u32[]{:S(2)}) collective-permute-start(bf16[144,1152]{1,0:T(8,128)(2,1)S(1)} %pad.13), channel_id=1, source_target_pairs={{0,4},{4,0},{8,12},{12,8},{16,20},{20,16},{24,28},{28,24},{1,5},{5... | collective-permute-start | bytes 995336 | tf_op jit(solution)/shard_map/ppermute | solution.py:1496
  136.5 156.4 %all-gather.14.cloned.1.call-start = ((), (), s32[]{:S(2)}) async-start(), calls=%async_computation.9 | async-start | bytes 3317760 | tf_op jit(solution)/shard_map/all_gather | solution.py:1503
  136.9 57.5 %collective-permute-start.2 = (bf16[576,1152]{1,0:T(8,128)(2,1)}, bf16[576,1152]{1,0:T(8,128)(2,1)}, u32[]{:S(2)}, u32[]{:S(2)}) collective-permute-start(bf16[576,1152]{1,0:T(8,128)(2,1)} %all-gather.10.cloned.1.call-done), channel_id=1, source_target_pairs={{0,4},{4,0},{8,12},{12,8},{16,20},{20,16},{24,28},{28,24},{1,5},{5... | collective-permute-start | bytes 3981320 | tf_op jit(solution)/shard_map/ppermute | solution.py:1496
  237.6 173.2 %reduce-scatter.6.cloned.1.call-start = ((), (), s32[]{:S(2)}) async-start(), calls=%async_computation.10 | async-start | bytes 3317760 | tf_op jit(solution)/shard_map/reduce_scatter | solution.py:1561
  334.5 0.7 copy-start.19
  334.5 2.0 copy-start.30
  334.5 126.8 %reduce-scatter.10.cloned.1.call-start = ((), (), s32[]{:S(2)}) async-start(), calls=%async_computation.12 | async-start | bytes 1658880 | tf_op jit(solution)/shard_map/reduce_scatter | solution.py:1561
  336.5 31.8 %collective-permute-start.5 = (bf16[4,144,1152]{2,1,0:T(8,128)(2,1)S(1)}, bf16[4,144,1152]{2,1,0:T(8,128)(2,1)S(1)}, u32[]{:S(2)}, u32[]{:S(2)}) collective-permute-start(bf16[4,144,1152]{2,1,0:T(8,128)(2,1)S(1)} %copy-done.30), channel_id=1, source_target_pairs={{0,4},{4,0},{8,12},{12,8},{16,20},{20,16},{24,28},{28,24},{1,5},{5... | collective-permute-start | bytes 3981320 | tf_op jit(solution)/shard_map/ppermute | solution.py:1496
  336.5 31.8 %copy-start.1 = (bf16[4,144,1152]{2,1,0:T(8,128)(2,1)S(1)}, bf16[4,144,1152]{2,1,0:T(8,128)(2,1)}, u32[]{:S(2)}) copy-start(bf16[4,144,1152]{2,1,0:T(8,128)(2,1)} %get-tuple-element.160) | copy-start | bytes 3981316
  369.7 123.8 %reduce-scatter.8.cloned.1.call-start = ((), (), s32[]{:S(2)}) async-start(), calls=%async_computation.11 | async-start | bytes 3317760 | tf_op jit(solution)/shard_map/reduce_scatter | solution.py:1561
  410.8 131.8 %reduce-scatter.12.cloned.1.call-start = ((), (), s32[]{:S(2)}) async-start(), calls=%async_computation.13 | async-start | bytes 3317760 | tf_op jit(solution)/shard_map/reduce_scatter | solution.py:1561
  411.9 49.4 %collective-permute-start.8 = (bf16[1,144,1152]{2,1,0:T(8,128)(2,1)S(1)}, bf16[1,144,1152]{2,1,0:T(8,128)(2,1)S(1)}, u32[]{:S(2)}, u32[]{:S(2)}) collective-permute-start(bf16[1,144,1152]{2,1,0:T(8,128)(2,1)S(1)} %dynamic-slice_bitcast_fusion.1), channel_id=1, source_target_pairs={{0,4},{4,0},{8,12},{12,8},{16,20},{20,16},{24,28},{28,24},{1,5},{5... | collective-permute-start | bytes 995336 | tf_op jit(solution)/shard_map/ppermute | solution.py:1496
  460.1 33.5 %collective-permute-start.7 = (bf16[4,144,1152]{2,1,0:T(8,128)(2,1)}, bf16[4,144,1152]{2,1,0:T(8,128)(2,1)S(1)}, u32[]{:S(2)}, u32[]{:S(2)}) collective-permute-start(bf16[4,144,1152]{2,1,0:T(8,128)(2,1)} %get-tuple-element.184), channel_id=1, source_target_pairs={{0,4},{4,0},{8,12},{12,8},{16,20},{20,16},{24,28},{28,24},{1,5},{5... | collective-permute-start | bytes 3981320 | tf_op jit(solution)/shard_map/ppermute | solution.py:1496
  461.3 0.7 copy-start.10
  462.0 137.3 %reduce-scatter.14.cloned.1.call-start = ((), (), s32[]{:S(2)}) async-start(), calls=%async_computation.14 | async-start | bytes 1658880 | tf_op jit(solution)/shard_map/reduce_scatter | solution.py:1561
  462.0 30.5 %copy-start.5 = (bf16[288,1152]{1,0:T(8,128)(2,1)S(1)}, bf16[288,1152]{1,0:T(8,128)(2,1)}, u32[]{:S(2)}) copy-start(bf16[288,1152]{1,0:T(8,128)(2,1)} %reduce-scatter.6.cloned.1.call-done) | copy-start | bytes 1990660
  462.0 30.5 %copy-start.11 = (bf16[1,144,1152]{2,1,0:T(8,128)(2,1)S(1)}, bf16[1,144,1152]{2,1,0:T(8,128)(2,1)}, u32[]{:S(2)}) copy-start(bf16[1,144,1152]{2,1,0:T(8,128)(2,1)} %copy-done.10) | copy-start | bytes 995332
  492.5 1.0 copy-start.12
  492.5 1.4 copy-start
  493.9 1.4 copy-start.6
  495.4 46.9 %collective-permute-start.6 = (bf16[1,144,1152]{2,1,0:T(8,128)(2,1)S(1)}, bf16[1,144,1152]{2,1,0:T(8,128)(2,1)S(1)}, u32[]{:S(2)}, u32[]{:S(2)}) collective-permute-start(bf16[1,144,1152]{2,1,0:T(8,128)(2,1)S(1)} %dynamic-slice_bitcast_fusion.2), channel_id=1, source_target_pairs={{0,4},{4,0},{8,12},{12,8},{16,20},{20,16},{24,28},{28,24},{1,5},{5... | collective-permute-start | bytes 995336 | tf_op jit(solution)/shard_map/ppermute | solution.py:1496
  495.5 46.8 %copy-start.7 = (bf16[288,1152]{1,0:T(8,128)(2,1)S(1)}, bf16[288,1152]{1,0:T(8,128)(2,1)}, u32[]{:S(2)}) copy-start(bf16[288,1152]{1,0:T(8,128)(2,1)} %reduce-scatter.8.cloned.1.call-done) | copy-start | bytes 1990660
  544.3 55.0 %collective-permute-start.9 = (bf16[1,144,1152]{2,1,0:T(8,128)(2,1)}, bf16[1,144,1152]{2,1,0:T(8,128)(2,1)S(1)}, u32[]{:S(2)}, u32[]{:S(2)}) collective-permute-start(bf16[1,144,1152]{2,1,0:T(8,128)(2,1)} %dynamic-slice_bitcast_fusion), channel_id=1, source_target_pairs={{0,4},{4,0},{8,12},{12,8},{16,20},{20,16},{24,28},{28,24},{1,5},{5... | collective-permute-start | bytes 995336 | tf_op jit(solution)/shard_map/ppermute | solution.py:1496
  544.3 55.1 %copy-start.8 = (bf16[288,1152]{1,0:T(8,128)(2,1)S(1)}, bf16[288,1152]{1,0:T(8,128)(2,1)}, u32[]{:S(2)}) copy-start(bf16[288,1152]{1,0:T(8,128)(2,1)} %reduce-scatter.12.cloned.1.call-done) | copy-start | bytes 1990660
  599.3 1.2 copy-start.2
  599.3 1.0 copy-start.13
  603.8 2.4 copy-start.4
  606.2 1.7 copy-start.3
  607.9 1.1 copy-start.29
  607.9 1.7 copy-start.28
  607.9 2.2 copy-start.27
  607.9 2.8 copy-start.26
  607.9 3.4 copy-start.25
  607.9 4.0 copy-start.24
  607.9 4.5 copy-start.23
  607.9 5.1 copy-start.21
  607.9 5.7 copy-start.22
Sparse Core Ops, SparseCore 0:
  10.2 45.5 all-gather.5
  57.9 32.1 all-gather.9
  92.2 54.4 all-gather.7
  148.7 54.1 all-gather.11
  237.7 53.2 all-gather.13
  334.6 49.9 reduce-scatter.5
  387.5 31.3 reduce-scatter.9
  421.2 51.4 reduce-scatter.7
  474.9 52.3 reduce-scatter.11
  530.0 32.3 reduce-scatter.13

commit v4 on v3

--- a/solution.py
+++ b/solution.py
@@ -320,6 +320,25 @@
         self.line.drain()
         for place in range(self.count):
             self.swap(place).wait_send()
+
+
+class Across:
+    def __init__(self, net, moves, part, scratch):
+        self.net, self.part = net, part
+        self.own, self.landed = scratch
+        self.load = moves.load(part.at[net.low], self.own)
+
+    def start(self):
+        self.copy = self.net.copy(self.part.at[1 - self.net.low], self.landed, self.net.half)
+
+    def finish(self, total):
+        self.load.wait()
+        self.copy.wait_recv()
+        total[...] = self.own[...].astype(F32) + self.landed[...].astype(F32)
+
+
+def across_scratch(part):
+    return [pltpu.VMEM(part.shape[1:], BF)] * 2
 
 
 def run(kernel, name, duration, inputs, outputs, scratch, identity, copies, moves):
@@ -446,6 +465,26 @@
         return carry
 
     lax.fori_loop(0, width // tile, one, 0)
+
+
+def packed_shape(rows, columns):
+    return (2, rows // 2 * columns // LANES, LANES)
+
+
+def pack_half(tiles, target):
+    rows = tiles[0].shape[0]
+    for index, tile in enumerate(tiles[:-1]):
+        target[index * rows : (index + 1) * rows, :] = tile.astype(BF)
+    tail = tiles[-1][:, : LANES // 2]
+    both = jnp.concatenate([tail[: rows // 2], tail[rows // 2 :]], axis=1)
+    target[(len(tiles) - 1) * rows :, :] = both.astype(BF)
+
+
+def unpack_half(packed, rows):
+    full = packed.shape[0] // rows
+    tiles = [packed[index * rows : (index + 1) * rows] for index in range(full)]
+    tail = packed[full * rows :]
+    return tiles + [jnp.concatenate([tail[:, : LANES // 2], tail[:, LANES // 2 :]], axis=0)]
 
 
 def project_kernel(*refs, layer, head_cols, factor, parts):
@@ -472,10 +511,18 @@
     def project(slots, chunk):
         result = dot(flat(normed[slots, chunk, :]), weight[...]) + bias[layer : layer + 1]
         shape = (slots.size, chunk.size, -1)
-        pairs[slots, chunk, :] = result[:, :pair_cols].astype(BF).reshape(shape)
+        halves = range(len(chunks)) if chunk.size == rows else [chunk.start // chunk.size]
+        step = rows // len(chunks)
+        for index in range(slots.size):
+            for place, half in enumerate(halves):
+                start = (index * len(halves) + place) * step
+                part = result[start : start + step]
+                tiles = [part[:, lane : lane + LANES] for lane in range(0, pair_cols, LANES)]
+                pack_half(tiles, pairs.at[slots.start + index, half])
+        halves = pl.ds(halves[0], len(halves))
         own = result[:, pair_cols : pair_cols + head_cols] * factor
         queries[slots, chunk, :] = own.astype(BF).reshape(shape)
-        source, target = pairs.at[slots, chunk], far_pairs.at[slots, chunk]
+        source, target = pairs.at[slots, halves], far_pairs.at[slots, halves]
         arrived.append(net.copy(source, target, net.half))
 
     whole = pl.ds(0, rows)
@@ -502,8 +549,8 @@
     outputs = [
         ((4, rows, width), BF, False),
         ((4, rows, head_cols), BF, False),
-        ((4, rows, 2 * head_cols), BF, False),
-        ((4, rows, 2 * head_cols), BF, False),
+        ((4,) + packed_shape(rows, 2 * head_cols), BF, False),
+        ((4,) + packed_shape(rows, 2 * head_cols), BF, False),
     ]
     scratch = [pltpu.VMEM((rows, width), F32), pltpu.VMEM((width, used), BF)]
     scratch += [pltpu.VMEM(shape, dtype) for shape, dtype, _ in outputs]
@@ -561,14 +608,16 @@
 
 
 def load_pairs(meta, own_pairs, far_pairs, key_scratch, value_scratch, heads):
-    rows = own_pairs.shape[1]
+    rows = 2 * (own_pairs.shape[2] * LANES // (2 * heads * HEAD_DIM))
     hid, half = meta[0], meta[1]
-    windows = pair_windows(own_pairs.shape[2])
+    windows = pair_windows(2 * heads * HEAD_DIM)
     for which, source in ((0, own_pairs), (1, far_pairs)):
         for slot in range(4):
             place = jnp.bitwise_xor(half, which) * 4 + jnp.bitwise_xor(hid, slot)
             start = pl.ds(pl.multiple_of(place * rows, rows), rows)
-            spread = spread_heads(source[slot], windows)
+            halves = [unpack_half(source[slot, index], rows // 2) for index in range(2)]
+            tiles = [jnp.concatenate(both, axis=0) for both in zip(*halves)]
+            spread = spread_heads(jnp.concatenate(tiles, axis=1), windows)
             for head in range(heads):
                 key_scratch[head, start, :] = spread[head]
                 value_scratch[head, start, :] = spread[heads + head]
@@ -738,7 +787,11 @@
             start = pl.ds(pl.multiple_of(place * rows, rows), rows)
             parts = [(grad_key[head, start, :] * LN2).astype(BF) for head in range(heads)]
             parts += [grad_value[head, start, :].astype(BF) for head in range(heads)]
-            target[slot] = join_heads(parts, pair_windows(2 * head_cols), 2 * head_cols).astype(BF)
+            joined = join_heads(parts, pair_windows(2 * head_cols), 2 * head_cols)
+            for index in range(2):
+                part = joined[index * (rows // 2) : (index + 1) * (rows // 2)]
+                tiles = [part[:, lane : lane + LANES] for lane in range(0, 2 * head_cols, LANES)]
+                pack_half(tiles, target.at[slot, index])
 
 
 def attend_back(meta, queries, own_pairs, far_pairs, query_ids, key_ids, grad_mixture, logsum):
@@ -752,8 +805,8 @@
         cost_estimate=micros(37),
         out_shape=[
             jax.ShapeDtypeStruct((4, rows, head_cols), BF),
-            jax.ShapeDtypeStruct((4, rows, 2 * head_cols), BF),
-            jax.ShapeDtypeStruct((4, rows, 2 * head_cols), BF),
+            jax.ShapeDtypeStruct(own_pairs.shape, BF),
+            jax.ShapeDtypeStruct(own_pairs.shape, BF),
         ],
         in_specs=[pl.BlockSpec(memory_space=pltpu.SMEM)] + [space] * 7,
         out_specs=[space] * 3,
@@ -888,17 +941,20 @@
     return run(kernel, "mlp", 48, inputs, outputs, scratch, 8 * layer + 1, 18, moves)
 
 
-def mlp_back_kernel(*refs, layer, parts, given, shard):
-    ins, outs, scratch = split_refs(refs, 7 + given + sum(parts), 7 + (shard > 0))
+def mlp_back_kernel(*refs, layer, parts, given, shard, crossing):
+    ins, outs, scratch = split_refs(
+        refs, 7 + given + sum(parts) + crossing, 7 + (shard > 0) + crossing
+    )
     gradient_hbm, after_hbm, vec, mixture_hbm, normed_hbm, active_hbm, slope_hbm = ins[:7]
-    mixed_hbm, up_hbm, down_hbm = split_refs(ins[7 + given :], parts[0], parts[1])
+    weights = ins[7 + given : 7 + given + sum(parts)]
+    mixed_hbm, up_hbm, down_hbm = split_refs(weights, parts[0], parts[1])
     after_out, mixture_out, down_out, out_out, sums, hidden_sums = outs[:6]
-    up_outs = outs[6:]
+    up_outs = outs[6 : 7 + (shard > 0)]
     gradient, after, out_weight, up_weight, down_weight, mixture, normed, active, slope = scratch[:9]
     grad_after, grad_mixture, grad_down, grad_up, grad_out = scratch[9:14]
     grad_rows, grad_hidden, grad_mid = scratch[14:17]
-    scatter_refs = scratch[17:25]
-    send_sems, recv_sems, move_sems = scratch[25:]
+    scatter_refs, across_refs = scratch[17:25], scratch[25:-3]
+    send_sems, recv_sems, move_sems = scratch[-3:]
     net, moves = Net(send_sems, recv_sems), Moves(move_sems)
     rows, width = gradient.shape
     hidden_cols = up_weight.shape[1]
@@ -916,7 +972,10 @@
     load_mixture = moves.load(mixture_hbm, mixture)
     if given:
         load_own = moves.load(gradient_hbm, gradient)
-    net.barrier([net.core, net.far])
+    across = Across(net, moves, ins[-1], across_refs) if crossing else None
+    net.barrier([net.core, net.far] + ([net.half] if crossing else []))
+    if crossing:
+        across.start()
     gain = vec[layer, 3:4]
     near, far, whole = pl.ds(0, 2), pl.ds(2, 2), pl.ds(0, rows)
     load_gradient.wait()
@@ -1001,13 +1060,15 @@
     load_mixture.wait()
     weight_grad(grad_mid, mixture, grad_out)
     moves.store(grad_out, out_out)
+    if crossing:
+        across.finish(outs[-1])
     net.finish()
     moves.finish()
 
 
 def mlp_back(
     layer, gradient, after, vec, mixed, up, down, mixture, normed, active, slope, given=(),
-    shard=0,
+    shard=0, crossing=(),
 ):
     rows, width = gradient.shape
     hidden = active.shape[2]
@@ -1041,31 +1102,42 @@
     ]
     outputs += half_outputs(width, hidden, shard)
     scratch = [pltpu.VMEM(shape, dtype) for shape, dtype in shapes] + scatter_scratch(rows, width)
+    for part in crossing:
+        outputs.append((part.shape[1:], F32, True))
+        scratch += across_scratch(part)
     inputs = [
         (gradient, False), (after, False), (vec, True), (mixture, False), (normed, False),
         (active, False), (slope, False),
-    ] + spaced([*given, *mixed, *up, *down])
+    ] + spaced([*given, *mixed, *up, *down, *crossing])
     parts = (len(mixed), len(up), len(down))
     kernel = functools.partial(
-        mlp_back_kernel, layer=layer, parts=parts, given=len(given), shard=shard
+        mlp_back_kernel,
+        layer=layer,
+        parts=parts,
+        given=len(given),
+        shard=shard,
+        crossing=len(crossing),
     )
-    moves = 13 + (3 * width // (2 * shard) if shard else 0)
+    moves = 14 + (3 * width // (2 * shard) if shard else 0)
     moves += weight_loads(mixed) + weight_loads(up) + weight_loads(down)
-    return run(kernel, "mlp_back", 48, inputs, outputs, scratch, 8 * layer + 2, 20, moves)
-
-
-def project_back_kernel(*refs, layer, parts, closing):
-    ins, outs, scratch = split_refs(refs, 8 + parts + closing, 4 + (closing > 0))
+    return run(kernel, "mlp_back", 48, inputs, outputs, scratch, 8 * layer + 2, 21, moves)
+
+
+def project_back_kernel(*refs, layer, parts, closing, crossing):
+    ins, outs, scratch = split_refs(
+        refs, 8 + parts + closing + crossing, 4 + (closing > 0) + crossing
+    )
     after_hbm, x_hbm, vec, normed_hbm, queries_hbm, own_hbm, far_hbm, out_hbm = ins[:8]
-    mixed_hbm, closing_ins = ins[8 : 8 + parts], ins[8 + parts :]
+    mixed_hbm, closing_ins = ins[8 : 8 + parts], ins[8 + parts : 8 + parts + closing]
     gradient_out, sums, column_sums, weight_out = outs[:4]
     grad_after, x, weight, normed, grad_queries, grad_own, grad_out = scratch[:7]
     landed, together, gradient, grad_weight = scratch[7:11]
-    scatter_refs, closing_refs = scratch[11:19], scratch[19:-3]
+    scatter_refs, closing_refs = scratch[11:19], scratch[19 : -3 - 2 * crossing]
+    across_refs = scratch[-3 - 2 * crossing : -3]
     send_sems, recv_sems, move_sems = scratch[-3:]
     net, moves = Net(send_sems, recv_sems), Moves(move_sems)
     rows, width = x.shape
-    pair_cols = grad_own.shape[2]
+    pair_cols = 2 * grad_queries.shape[2]
     used_cols = pair_cols + grad_queries.shape[2]
     all_cols = together.shape[2]
     chunks = chunks_of(rows, 2)
@@ -1083,6 +1155,7 @@
         load_after_two = moves.load(closing_ins[1], after)
         columns = pl.ds(0, down_weight.shape[1])
         load_down = load_weight(net, moves, closing_ins[2:], columns, down_weight)
+    across = Across(net, moves, ins[-1], across_refs) if crossing else None
     net.barrier([net.core, net.far, net.half])
     arriving = {
         slot: net.copy(far_hbm.at[slot], landed.at[slot], net.half) for slot in (3, 2, 1, 0)
@@ -1095,8 +1168,12 @@
 
     def join(slot):
         arriving[slot].wait_recv()
-        pair = grad_own[slot].astype(F32) + landed[slot].astype(F32)
-        together[slot, :, :pair_cols] = pair.astype(BF)
+        for index in range(2):
+            pair = grad_own[slot, index].astype(F32) + landed[slot, index].astype(F32)
+            part = pl.ds(index * (rows // 2), rows // 2)
+            for place, tile in enumerate(unpack_half(pair.astype(BF), rows // 2)):
+                columns = pl.ds(place * LANES, tile.shape[1])
+                together[slot, part, columns] = tile
 
     def back(slots, chunk):
         return dot(flat(together[slots, chunk, :]), weight[...], NT)
@@ -1124,6 +1201,8 @@
         scatter.far_send(key, chunk)
     join(1)
     join(0)
+    if crossing:
+        across.start()
     scatter.near_part(back(near, whole))
     load_normed.wait()
     load_out.wait()
@@ -1149,14 +1228,16 @@
         load_after_two.wait()
         for key, chunk in enumerate(chunks):
             final[chunk, :] = last.result(key, chunk) + after[chunk, :] + vec[layer, 5:6]
-        moves.store(final, outs[-1])
+        moves.store(final, outs[4])
+    if crossing:
+        across.finish(outs[-1])
     net.finish()
     moves.finish()
 
 
 def project_back(
     layer, grad_after, x, vec, mixed, normed, grad_queries, grad_own, grad_far, grad_out, all_cols,
-    closing=(),
+    closing=(), crossing=(),
 ):
     rows, width = x.shape
     outputs = [
@@ -1188,12 +1269,17 @@
         ]
         scratch += [pltpu.VMEM(shape, dtype) for shape, dtype in shapes] + scatter_scratch(rows, width)
         copies, moves = 18, moves + 3 + weight_loads(down)
+    for part in crossing:
+        outputs.append((part.shape[1:], F32, True))
+        scratch += across_scratch(part)
+        copies, moves = copies + 1, moves + 1
     inputs = [
         (grad_after, False), (x, False), (vec, True), (normed, False), (grad_queries, False),
         (grad_own, False), (grad_far, False), (grad_out, False),
-    ] + spaced([*mixed, *closing])
+    ] + spaced([*mixed, *closing, *crossing])
     kernel = functools.partial(
-        project_back_kernel, layer=layer, parts=len(mixed), closing=len(closing)
+        project_back_kernel, layer=layer, parts=len(mixed), closing=len(closing),
+        crossing=len(crossing),
     )
     return run(kernel, "project_back", 42, inputs, outputs, scratch, 8 * layer + 3, copies, moves)
 
@@ -1283,29 +1369,31 @@
 
 
 def finish_kernel(*refs, layers):
-    ins, outs, scratch = split_refs(refs, 3 + 4 * layers, 12)
-    final_rows, gradient_rows, grads = ins[:3]
-    layer_sums = [ins[3 + 4 * layer : 7 + 4 * layer] for layer in range(layers)]
+    ins, outs, scratch = split_refs(refs, 4 + 4 * layers, 13)
+    final_rows, gradient_rows, grads, down_grads = ins[:4]
+    layer_sums = [ins[4 + 4 * layer : 8 + 4 * layer] for layer in range(layers)]
     final_out, gradient_out, total = outs[:3]
     wide_outs, query_out, value_out, hidden_out = outs[3:9], outs[9], outs[10], outs[11]
-    final, gradient, wide, sums, hidden_sums = scratch[:5]
-    final_land, gradient_land, wide_land, across_land, along_land = scratch[5:10]
-    across_hidden, along_hidden = scratch[10:12]
-    job_refs = scratch[12:16]
-    send_sems, recv_sems, move_sems = scratch[16:]
+    down_total = outs[12]
+    final, gradient, final_land, gradient_land = scratch[:4]
+    sums, across_land, along, wide, wide_land = scratch[4:9]
+    job_refs, across_refs = scratch[9:13], scratch[13:15]
+    send_sems, recv_sems, move_sems = scratch[15:]
     net, moves = Net(send_sems, recv_sems), Moves(move_sems)
     count = grads.shape[0] // 2
+    rows, cols, last = final_rows.shape[0], wide.shape[2], count - 1
     others = [net.core, net.far, net.far_core]
+    top = layers * 8
+    sums[top:] = jnp.zeros((sums.shape[0] - top, sums.shape[1]), F32)
+    for layer, (one, two, column_sums, hidden) in enumerate(layer_sums):
+        sums[layer * 8 : layer * 8 + 8] = one[...] + two[...]
+        sums[top + layer : top + layer + 1, : column_sums.shape[1]] = column_sums[...]
+        sums[top + layers + layer : top + layers + layer + 1, : hidden.shape[1]] = hidden[...]
     net.line(count)
     net.barrier(others + [net.half], True)
+    swap = net.copy(sums, across_land, net.half)
     scattering = ScatterParts(net, moves, grads, job_refs)
-    cols, rows = wide.shape[2], final_rows.shape[0]
-    for layer, (one, two, _, _) in enumerate(layer_sums):
-        both = one[...] + two[...]
-        for place in range(4):
-            columns = slice(place * cols, (place + 1) * cols)
-            wide[place, layer * 8 : layer * 8 + 8] = both[:, columns]
-    summed = [net.copy(wide.at[device[1]], wide_land.at[net.hid], device) for device in others]
+    across = Across(net, moves, down_grads, across_refs)
     for target, source in ((final, final_rows), (gradient, gradient_rows)):
         target[...] = source[...].T.astype(BF).reshape(target.shape)
     moved = []
@@ -1313,117 +1401,93 @@
         for device in reversed(others):
             moved.append(net.copy(source.at[device[1]], target.at[net.hid], device))
         target[net.hid] = source[net.hid]
+    up, down = net.take(count), net.take(count)
+    own = along.at[net.high]
+    swap.wait()
+    along[net.high] = sums[...] + across_land[...]
+    pl.when(net.has_after)(net.make(up, own, own, net.after).start)
+    pl.when(net.has_before)(net.make(down, own, own, net.before).start)
+
+    def pass_on(step, place, base, device, has):
+        block = along.at[place]
+        net.make(base + step - 1, block, block, device).wait_recv()
+        if step < last:
+            pl.when(has)(net.make(base + step, block, block, device).start)
+
+    def pass_sums(step):
+        pl.when(net.high >= step)(
+            functools.partial(pass_on, step, net.high - step, up, net.after, net.has_after)
+        )
+        pl.when(net.high + step < count)(
+            functools.partial(pass_on, step, net.high + step, down, net.before, net.has_before)
+        )
+
+    for point in range(3):
+        scattering.forward(point, 3)
+        for step in range(1, count):
+            if (step - 1) * 3 // last == point:
+                pass_sums(step)
+    across.start()
+    reduced = along[0]
+    for place in range(1, count):
+        reduced += along[place]
+    sums[...] = reduced
+    for place in range(4):
+        wide[place] = sums[:top, place * cols : (place + 1) * cols]
     wide_land[net.hid] = wide[net.hid]
-    last = count - 1
-    pairs = ((sums, across_land, along_land), (hidden_sums, across_hidden, along_hidden))
-    bases = [(net.take(count), net.take(count)) for _ in pairs]
-
-    def send_sums():
-        for one in summed:
-            one.wait_recv()
-        top = wide.shape[1]
-        sums[:top] = wide_land[0] + wide_land[1] + wide_land[2] + wide_land[3]
-        sums[top:] = jnp.zeros((sums.shape[0] - top, cols), F32)
-        hidden_sums[...] = jnp.zeros_like(hidden_sums)
-        for layer, (_, _, column_sums, hidden) in enumerate(layer_sums):
-            for place in range(3):
-                row = top + layer * 3 + place
-                sums[row : row + 1] = column_sums[:, place * cols : (place + 1) * cols]
-            hidden_sums[layer : layer + 1] = hidden[...]
-        return [net.copy(value, across, net.half) for value, across, _ in pairs]
-
-    def spread_sums(swaps):
-        for one in swaps:
-            one.wait()
-        for (value, across, along), base in zip(pairs, bases):
-            value[...] += across[...]
-            own = along.at[net.high]
-            along[net.high] = value[...]
-            pl.when(net.has_after)(net.make(base[0], own, own, net.after).start)
-            pl.when(net.has_before)(net.make(base[1], own, own, net.before).start)
-
-    def pass_sums(step):
-        for (_, _, along), base in zip(pairs, bases):
-            below, above = along.at[net.high - step], along.at[net.high + step]
-
-            def pass_on(index, block, device, has):
-                net.make(index, block, block, device).wait_recv()
-                if step < last:
-                    pl.when(has)(net.make(index + 1, block, block, device).start)
-
-            pl.when(net.high >= step)(
-                functools.partial(pass_on, base[0] + step - 1, below, net.after, net.has_after)
-            )
-            pl.when(net.high + step < count)(
-                functools.partial(pass_on, base[1] + step - 1, above, net.before, net.has_before)
-            )
-
-    swaps = send_sums()
-    scattering.forward(0, 3)
-    scattering.forward(1, 3)
-    spread_sums(swaps)
-    scattering.forward(2, 3)
-    for step in range(1, count):
-        pass_sums(step)
-    for (value, _, along), base in zip(pairs, bases):
-        total_value = along[0]
-        for place in range(1, count):
-            total_value += along[place]
-        value[...] = total_value
-        own = along.at[net.high]
-        for step in range(count - 1):
-            up = jnp.logical_and(net.has_after, net.high >= step)
-            down = jnp.logical_and(net.has_before, net.high + step < count)
-            pl.when(up)(net.make(base[0] + step, own, own, net.after).wait_send)
-            pl.when(down)(net.make(base[1] + step, own, own, net.before).wait_send)
+    summed = [net.copy(wide.at[device[1]], wide_land.at[net.hid], device) for device in others]
     for one in moved:
         one.wait_recv()
     for source, target in ((final_land, final_out), (gradient_land, gradient_out)):
         for place in range(4):
             target[:, place * rows : (place + 1) * rows] = source[place].astype(F32)
+    for one in summed:
+        one.wait_recv()
+    narrow = wide_land[0] + wide_land[1] + wide_land[2] + wide_land[3]
     for layer in range(layers):
         one = slice(layer, layer + 1)
         for index, out in enumerate(wide_outs):
-            out[one, :] = sums[layer * 8 + index : layer * 8 + index + 1]
-        row = layers * 8 + layer * 3
-        value_out[one, :] = sums[row + 1 : row + 2]
-        query_out[one, :] = sums[row + 2 : row + 3]
-        hidden_out[one, :] = hidden_sums[one, : hidden_out.shape[1]]
+            out[one, :] = narrow[layer * 8 + index : layer * 8 + index + 1]
+        row = slice(top + layer, top + layer + 1)
+        value_out[one, :] = sums[row, cols : 2 * cols]
+        query_out[one, :] = sums[row, 2 * cols : 3 * cols]
+        row = slice(top + layers + layer, top + layers + layer + 1)
+        hidden_out[one, :] = sums[row, : hidden_out.shape[1]]
+    for step in range(last):
+        sent_up = jnp.logical_and(net.has_after, net.high >= step)
+        sent_down = jnp.logical_and(net.has_before, net.high + step < count)
+        pl.when(sent_up)(net.make(up + step, own, own, net.after).wait_send)
+        pl.when(sent_down)(net.make(down + step, own, own, net.before).wait_send)
     scattering.finish(total)
-    net.finish(swaps)
-
-
-def finish(final, gradient, grads, layer_sums, head_cols, feed):
+    across.finish(down_total)
+    net.finish([swap])
+
+
+def finish(final, gradient, grads, down_grads, layer_sums, head_cols, feed):
     count, layers = grads.shape[0] // 2, len(layer_sums)
-    rows = final.shape[0]
-    sums = (layers * 11 + -layers * 11 % 8, head_cols)
-    hidden = (layers + -layers % 8, layer_sums[0][3].shape[1])
+    rows, width = final.shape
+    sum_cols = max(width, layer_sums[0][2].shape[1], layer_sums[0][3].shape[1])
+    sums = (layers * 10 + -layers * 10 % 8, sum_cols)
     vector = ((layers, head_cols), F32, True)
     outputs = [
         ((head_cols, 4 * rows), F32, True),
         ((head_cols, 4 * rows), F32, True),
         (grads.shape[1:], F32, True),
     ] + [vector] * 8
-    outputs.append(((layers, feed), F32, True))
+    outputs += [((layers, feed), F32, True), (down_grads.shape[1:], F32, True)]
     blocks, wide = (4, head_cols, rows), (4, layers * 8, head_cols)
-    scratch = [
-        pltpu.VMEM(blocks, BF),
-        pltpu.VMEM(blocks, BF),
-        pltpu.VMEM(wide, F32),
+    scratch = [pltpu.VMEM(blocks, BF)] * 4 + [
         pltpu.VMEM(sums, F32),
-        pltpu.VMEM(hidden, F32),
-        pltpu.VMEM(blocks, BF),
-        pltpu.VMEM(blocks, BF),
-        pltpu.VMEM(wide, F32),
         pltpu.VMEM(sums, F32),
         pltpu.VMEM((count,) + sums, F32),
-        pltpu.VMEM(hidden, F32),
-        pltpu.VMEM((count,) + hidden, F32),
-    ] + part_scratch(*grads.shape)
-    inputs = [(final, True), (gradient, True), (grads, False)]
+        pltpu.VMEM(wide, F32),
+        pltpu.VMEM(wide, F32),
+    ]
+    scratch += part_scratch(*grads.shape) + across_scratch(down_grads)
+    inputs = [(final, True), (gradient, True), (grads, False), (down_grads, False)]
     inputs += [(one, True) for four in layer_sums for one in four]
     kernel = functools.partial(finish_kernel, layers=layers)
-    return run(kernel, "finish", 40, inputs, outputs, scratch, 5, 12 + 7 * count, 1 + count)
+    return run(kernel, "finish", 2, inputs, outputs, scratch, 5, 13 + 5 * count, 2 + count)
 
 
 def key_ranges(own_ids, row_ids, rows):
@@ -1568,6 +1632,9 @@
             parts = by_halves(part)
         return parts[0], swap(parts[1])
 
+    def by_half(part):
+        return jnp.pad(part.reshape(2, shard, part.shape[1]), ((0, 0), (0, shard_pad), (0, 0)))
+
     def added(own, other):
         return (own.astype(F32) + other.astype(F32)).astype(BF)
 
@@ -1582,18 +1649,16 @@
         x, normed, queries, own_pairs, far_pairs, mixture, logsum, after, normed_two, active, slope = saved[layer]
         mixed, up, down = weights[layer], ups[layer], downs[layer]
         last = layer + 1
+        crossing = ()
         if last < layers:
             gradient, down_grads[last] = hold(gradient, down_grads[last])
-            down_own, down_other = halves_of([down_grads[last]])
+            crossing = (by_half(down_grads[last]),)
         grad_after, grad_mixture, grad_down, grad_out, sums_two, hidden_sums, *grad_up = mlp_back(
             layer, gradient, after, vectors, mixed, up, down, mixture, normed_two, active, slope,
-            () if last < layers else (grad_rows,), split,
+            () if last < layers else (grad_rows,), split, crossing,
         )
         if last < layers:
-            down_other, up_grads[last], grad_mixture = hold(
-                down_other, up_grads[last], grad_mixture
-            )
-            down_grads[last] = added(down_own, down_other)[0]
+            down_grads[last] = grad_up.pop()
             grad_down, up_grads[last] = hold(grad_down, up_grads[last])
         down_grads[layer] = sum_along(grad_down)
         up_own, up_other = halves_of(grad_up)
@@ -1603,41 +1668,39 @@
         )
         up_other, grad_far = hold(up_other, grad_far)
         up_grad = added(up_own, up_other)
+        crossing = ()
         if last < layers:
             grad_after, mixed_grads[last] = hold(grad_after, mixed_grads[last])
-            mixed_own, mixed_other = halves_of([mixed_grads[last]])
+            crossing = (by_half(mixed_grads[last]),)
         grad_after, up_grad = hold(grad_after, up_grad)
         up_grads[layer] = sum_along(in_rows(up_grad))
         gradient, sums_one, column_sums, grads, *closed = project_back(
             layer, grad_after, x, vectors, mixed, normed, grad_queries, grad_own, grad_far,
-            grad_out, used_cols, () if last < layers else (active, after, *down),
+            grad_out, used_cols, () if last < layers else (active, after, *down), crossing,
         )
+        if last < layers:
+            mixed_grads[last] = closed.pop()
         final = closed[0] if closed else final
-        if last < layers:
-            mixed_other, gradient = hold(mixed_other, gradient)
-            mixed_grads[last] = added(mixed_own, mixed_other)[0]
         if layer > 0:
             mixed_grads[layer] = sum_along(grads)
         layer_sums[layer] = (sums_one, sums_two, column_sums, hidden_sums)
     gradient, down_grads[0] = hold(gradient, down_grads[0])
-    down_own, down_other = halves_of([down_grads[0]])
-    final, gradient, mixed_grad, *small = finish(
-        final, gradient, separate(grads), layer_sums, head_cols, feed
+    final, gradient, mixed_grads[0], *small = finish(
+        final, gradient, separate(grads), by_half(down_grads[0]), layer_sums, head_cols, feed
     )
-    down_other, up_grads[0], final, gradient, mixed_grad, *small = hold(
-        down_other, up_grads[0], final, gradient, mixed_grad, *small
+    up_grads[0], final, gradient, mixed_grads[0], *small = hold(
+        up_grads[0], final, gradient, mixed_grads[0], *small
     )
-    mixed_grads[0] = mixed_grad[:shard]
-    down_grads[0] = added(down_own, down_other)[0]
+    down_grads[0] = small.pop()
     first_gain, first_shift, output_bias, second_gain, second_shift, down_bias = small[:6]
     query_bias, value_bias, up_bias = small[6:]
 
     def mixed_columns(start):
         columns = slice(start * head_cols, (start + 1) * head_cols)
-        return jnp.stack([part[:, columns].astype(F32) for part in mixed_grads])
+        return jnp.stack([part[:shard, columns].astype(F32) for part in mixed_grads])
 
     def hidden_columns(parts):
-        return jnp.stack([part[:, :feed].astype(F32) for part in parts])
+        return jnp.stack([part[:shard, :feed].astype(F32) for part in parts])
 
     return (
         final.T,

time: 629 us -> 614 us (0.976)
  Pallas kernels: 551 us -> 538 us
    pallas_call x10, Pallas kernels: 453 us -> 440 us  [run(): pl.pallas_call(kernel, name=name, cost_estimate=micros(duration), out_sha...]
  transfers between devices with their start and end apart: 20 -> 17, of which waited for: 2 -> 3; matrix products, arithmetic and copies ran while one was open for 3% -> 3% of each run, Pallas kernels for 82% -> 82%
where the time goes in v4:
time: 614 us; the launch traced here: 606 us
  Pallas kernels  538 us (88%)
  local copies, waits for them, and re-layouts  21.8 us (4%)
  between operations  15.1 us (2%)
  other arithmetic  12.1 us (2%)
  waiting for transfers between devices  11.3 us (2%)
  starting transfers between devices  7.98 us (1%)
    pallas_call x10, Pallas kernels, run(): pl.pallas_call(kernel, name=name, cost_estimate=micros(duration), out_sha...  440 us
    pallas_call x2, Pallas kernels, attend_back(): pl.pallas_call(functools.partial(attend_back_kernel, heads=heads), name='...  61.5 us
    pallas_call x2, Pallas kernels, attend(): pl.pallas_call(functools.partial(attend_kernel, heads=heads), name='atten...  36.9 us
  transfers between devices with their start and end apart: 17, of which 3 were waited for; matrix products, arithmetic and copies ran while one was open for 3% of the time, Pallas kernels for 82%

profile of v4, /device:TPU:0, one launch (start us, length us, event | category | flops | bytes accessed | tf_op | source)
XLA Modules:
  0.0 606.4 jit_solution(13971213498893603640)
XLA Ops:
  7.2 1.2 slice_bitcast_fusion.4
  8.4 0.8 pad.15
  9.4 3.0 collective-permute-start
  12.7 1.0 concatenate.11
  13.7 1.0 concatenate.9.refs_5_
  14.7 62.2 %entry.1 = (f32[256,1152]{1,0:T(8,128)}, f32[256,1152]{1,0:T(8,128)}, bf16[4,256,1152]{2,1,0:T(8,128)(2,1)}, f32[2,8,1152]{2,1,0:T(8,128)}, f32[2,896]{1,0:T(2,1...) custom-call(bf16[288,1024]{1,0:T(8,128)(2,1)} %bitcast.136, bf16[288,1024]{1,0:T(8,128)(2,1)} %bitcast.137, ...), custom_call_target="tpu_custom_call" | custom-call | flops 49999998976 | tf_op jit(solution)/shard_map/entry/pallas_call | solution.py:348
  76.9 0.7 dynamic_slice.6
  77.7 0.7 dynamic_slice.7
  78.4 0.2 slice_reduce_fusion.1
  78.5 0.2 select_reduce_fusion.1
  78.8 0.1 copy.46
  79.0 1.0 copy.47.query_ids
  80.1 0.6 pad_add_fusion.1.meta
  80.8 0.9 pad_maximum_fusion
  81.7 30.9 %project.2 = (bf16[4,256,1152]{2,1,0:T(8,128)(2,1)}, bf16[4,256,288]{2,1,0:T(8,128)(2,1)}, bf16[4,2,576,128]{3,2,1,0:T(8,128)(2,1)}, bf16[4,2,576,128]{3,2,1,0:T(8,128)(2,1)}) custom-call(f32[256,1152]{1,0:T(8,128)} %get-tuple-element.131.refs_0_.refs_1_, f32[2,8,1152]{2,1,0:T(8,128)} %get-tuple-element.132.refs_1_.refs_2_, ...), custom_call_target="tpu_custom_call" | custom-call | flops 40000000000 | tf_op jit(solution)/shard_map/project/pallas_call | solution.py:348
  112.6 1.6 collective-permute-start.1
  114.2 18.5 %attend.2 = (bf16[4,256,384]{2,1,0:T(8,128)(2,1)}, f32[8,1024]{1,0:T(8,128)}) custom-call(s32[10]{0:T(128)} %pad_add_fusion.1.meta, bf16[4,256,288]{2,1,0:T(8,128)(2,1)} %get-tuple-element.135.queries, bf16[4,2,576,128]{3,2,1,0:T(8,128)(2,1)} %get-tuple-element.136.own_pairs, bf16[4,2,576,128]{3,2,1,0:T(8,128)(2,1)} %get-tuple-element.137.far_pairs, ...), custom_call_target="tpu_custom_call" | custom-call | flops 22000001024 | tf_op jit(solution)/shard_map/attend/pallas_call | solution.py:698
  132.7 0.1 select_bitcast_fusion.3
  132.8 0.9 pad_maximum_fusion.1
  133.7 0.3 all-gather.14.cloned.1.call-start
  134.1 2.1 collective-permute-start.2
  136.1 8.9 %collective-permute-done.1 = bf16[576,1152]{1,0:T(8,128)(2,1)} collective-permute-done((bf16[576,1152]{1,0:T(8,128)(2,1)}, bf16[576,1152]{1,0:T(8,128)(2,1)}, u32[]{:S(2)}, u32[]{:S(2)}) %collective-permute-start.1) | collective-permute-done | bytes 1327136 | tf_op jit(solution)/shard_map/ppermute | solution.py:1560
  145.1 1.6 all-gather.8.cloned.1.call-done.refs_7_.refs_10_
  146.7 46.8 %mlp.2 = (f32[256,1152]{1,0:T(8,128)}, bf16[4,256,1152]{2,1,0:T(8,128)(2,1)}, bf16[4,256,1152]{2,1,0:T(8,128)(2,1)}, bf16[4,256,1152]{2,1,0:T(8,128)(2,1)}, f32[256,1152]{1,0:T(8,128)}) custom-call(bf16[4,256,384]{2,1,0:T(8,128)(2,1)} %get-tuple-element.139.refs_0_.refs_3_, f32[256,1152]{1,0:T(8,128)} %get-tuple-element.131.refs_0_.refs_1_, ...), custom_call_target="tpu_custom_call" | custom-call | flops 48000000000 | tf_op jit(solution)/shard_map/mlp/pallas_call | solution.py:348
  193.5 40.1 %project.3 = (bf16[4,256,1152]{2,1,0:T(8,128)(2,1)}, bf16[4,256,288]{2,1,0:T(8,128)(2,1)}, bf16[4,2,576,128]{3,2,1,0:T(8,128)(2,1)}, bf16[4,2,576,128]{3,2,1,0:T(8,128)(2,1)}) custom-call(f32[256,1152]{1,0:T(8,128)} %get-tuple-element.143.refs_0_.refs_1_, f32[2,8,1152]{2,1,0:T(8,128)} %get-tuple-element.132.refs_1_.refs_2_, ...), custom_call_target="tpu_custom_call" | custom-call | flops 40000000000 | tf_op jit(solution)/shard_map/project/pallas_call | solution.py:348
  233.7 0.9 pad_maximum_fusion.2
  234.7 18.4 %attend.3 = (bf16[4,256,384]{2,1,0:T(8,128)(2,1)}, f32[8,1024]{1,0:T(8,128)}) custom-call(s32[10]{0:T(128)} %pad_add_fusion.1.meta, bf16[4,256,288]{2,1,0:T(8,128)(2,1)} %get-tuple-element.146.queries, bf16[4,2,576,128]{3,2,1,0:T(8,128)(2,1)} %get-tuple-element.147.own_pairs, bf16[4,2,576,128]{3,2,1,0:T(8,128)(2,1)} %get-tuple-element.148.far_pairs, ...), custom_call_target="tpu_custom_call" | custom-call | flops 22000001024 | tf_op jit(solution)/shard_map/attend/pallas_call | solution.py:698
  253.1 37.1 %mlp.3 = (f32[256,1152]{1,0:T(8,128)}, bf16[4,256,1152]{2,1,0:T(8,128)(2,1)}, bf16[4,256,1152]{2,1,0:T(8,128)(2,1)}, bf16[4,256,1152]{2,1,0:T(8,128)(2,1)}) custom-call(bf16[4,256,384]{2,1,0:T(8,128)(2,1)} %get-tuple-element.149.refs_0_.refs_3_, f32[256,1152]{1,0:T(8,128)} %get-tuple-element.143.refs_0_.refs_1_, ...), custom_call_target="tpu_custom_call" | custom-call | flops 48000000000 | tf_op jit(solution)/shard_map/mlp/pallas_call | solution.py:348
  290.3 41.5 %mlp_back.2 = (f32[256,1152]{1,0:T(8,128)}, bf16[4,256,384]{2,1,0:T(8,128)(2,1)}, bf16[1152,1152]{1,0:T(8,128)(2,1)}, bf16[1152,384]{1,0:T(8,128)(2,1)}, f32[8,1...) custom-call(f32[256,1152]{1,0:T(8,128)} %get-tuple-element.129.refs_0_, ...), custom_call_target="tpu_custom_call" | custom-call | flops 48000000000 | tf_op jit(solution)/shard_map/mlp_back/pallas_call | solution.py:348
  331.9 0.6 copy-done.14
  332.5 1.3 copy.49.key_ids
  333.8 31.1 %attend_back.2 = (bf16[4,256,288]{2,1,0:T(8,128)(2,1)}, bf16[4,2,576,128]{3,2,1,0:T(8,128)(2,1)}, bf16[4,2,576,128]{3,2,1,0:T(8,128)(2,1)}) custom-call(s32[10]{0:T(128)} %pad_add_fusion.1.meta, bf16[4,256,288]{2,1,0:T(8,128)(2,1)} %get-tuple-element.146.queries, bf16[4,2,576,128]{3,2,1,0:T(8,128)(2,1)} %get-tuple-element.147.own_pairs, ...), custom_call_target="tpu_custom_call" | custom-call | flops 36999999488 | tf_op jit(solution)/shard_map/attend_back/pallas_call | solution.py:802
  364.9 0.5 collective-permute-done.5
  365.4 1.4 add_convert_fusion.1
  366.9 39.8 %project_back.2 = (f32[256,1152]{1,0:T(8,128)}, f32[8,1152]{1,0:T(8,128)}, f32[1,896]{1,0:T(1,128)}, bf16[1152,1152]{1,0:T(8,128)(2,1)}, f32[256,1152]{1,0:T(8,128)}) custom-call(f32[256,1152]{1,0:T(8,128)} %get-tuple-element.164.refs_0_, f32[256,1152]{1,0:T(8,128)} %get-tuple-element.143.refs_0_.refs_1_, f32[2,8,1152]{2,1,0:T(8,128)} %get-tuple-element.132.refs_1_.refs_2_, ...), custom_call_target="tpu_custom_call" | custom-call | flops 41999998976 | tf_op jit(solution)/shard_map/project_back/pallas_call | solution.py:348
  406.8 47.3 %mlp_back.3 = (f32[256,1152]{1,0:T(8,128)}, bf16[4,256,384]{2,1,0:T(8,128)(2,1)}, bf16[1152,1152]{1,0:T(8,128)(2,1)}, bf16[1152,384]{1,0:T(8,128)(2,1)}, f32[8,1...) custom-call(f32[256,1152]{1,0:T(8,128)} %get-tuple-element.172.refs_, ...), custom_call_target="tpu_custom_call" | custom-call | flops 48000000000 | tf_op jit(solution)/shard_map/mlp_back/pallas_call | solution.py:348
  454.2 0.6 collective-permute-start.6
  454.8 30.4 %attend_back.3 = (bf16[4,256,288]{2,1,0:T(8,128)(2,1)}, bf16[4,2,576,128]{3,2,1,0:T(8,128)(2,1)}, bf16[4,2,576,128]{3,2,1,0:T(8,128)(2,1)}) custom-call(s32[10]{0:T(128)} %pad_add_fusion.1.meta, bf16[4,256,288]{2,1,0:T(8,128)(2,1)} %get-tuple-element.135.queries, bf16[4,2,576,128]{3,2,1,0:T(8,128)(2,1)} %get-tuple-element.136.own_pairs, ...), custom_call_target="tpu_custom_call" | custom-call | flops 36999999488 | tf_op jit(solution)/shard_map/attend_back/pallas_call | solution.py:802
  485.2 0.8 slice_bitcast_fusion.2
  485.9 1.1 slice_bitcast_fusion
  487.1 1.4 add_convert_fusion
  488.5 40.8 %project_back.3 = (f32[256,1152]{1,0:T(8,128)}, f32[8,1152]{1,0:T(8,128)}, f32[1,896]{1,0:T(1,128)}, bf16[1152,1152]{1,0:T(8,128)(2,1)}, f32[144,1152]{1,0:T(8,128)}) custom-call(f32[256,1152]{1,0:T(8,128)} %get-tuple-element.189.refs_0_, f32[256,1152]{1,0:T(8,128)} %get-tuple-element.131.refs_0_.refs_1_, f32[2,8,1152]{2,1,0:T(8,128)} %get-tuple-element.132.refs_1_.refs_2_, ...), custom_call_target="tpu_custom_call" | custom-call | flops 41999998976 | tf_op jit(solution)/shard_map/project_back/pallas_call | solution.py:348
  529.4 1.5 slice_bitcast_fusion.8
  530.9 53.1 %finish.1 = (f32[288,1024]{1,0:T(8,128)}, f32[288,1024]{1,0:T(8,128)}, f32[144,1152]{1,0:T(8,128)}, f32[2,288]{1,0:T(2,128)}, f32[2,288]{1,0:T(2,128)}, /*index=...) custom-call(f32[256,1152]{1,0:T(8,128)} %get-tuple-element.188.refs_, ...), custom_call_target="tpu_custom_call" | custom-call | flops 2000000000 | tf_op jit(solution)/shard_map/finish/pallas_call | solution.py:348
  584.0 1.2 slice_bitcast_fusion.1
  585.3 0.2 slice_bitcast_fusion.9
  585.6 1.1 maximum_bitcast_fusion
  586.7 1.2 maximum_convert_fusion
  587.9 0.8 maximum_bitcast_fusion.1
  588.7 0.8 pad_maximum_fusion.5
  589.5 0.8 pad_maximum_fusion.4
  590.3 0.8 pad_maximum_fusion.3
  591.1 1.0 copy.62
  592.1 0.7 copy-done.4
  592.8 1.0 copy.63
  593.9 0.6 copy.64
  594.4 0.6 copy.65
  595.0 0.6 copy.66
  595.6 0.6 copy.67
  596.2 0.6 copy.68
  596.8 0.6 copy.69
  597.3 0.6 copy.70
  597.9 0.6 copy.71
  598.5 0.6 copy.72
  (100 shorter events, 1.6 us)
Async XLA Ops:
  7.2 2.1 copy-start.6
  7.2 105.4 %all-gather.6.cloned.1.call-start = ((), (), s32[]{:S(2)}) async-start(), calls=%async_computation.5 | async-start | bytes 1658880 | tf_op jit(solution)/shard_map/all_gather | solution.py:1567
  9.2 3.3 copy-start.11
  9.2 3.4 copy-start.12
  9.2 124.8 %all-gather.10.cloned.1.call-start = ((), (), s32[]{:S(2)}) async-start(), calls=%async_computation.7 | async-start | bytes 1658880 | tf_op jit(solution)/shard_map/all_gather | solution.py:1567
  9.4 3.3 copy-start.9
  9.4 3.3 copy-start.10
  9.4 71.2 %collective-permute-start = (bf16[144,1152]{1,0:T(8,128)(2,1)S(1)}, bf16[144,1152]{1,0:T(8,128)(2,1)S(1)}, u32[]{:S(2)}, u32[]{:S(2)}) collective-permute-start(bf16[144,1152]{1,0:T(8,128)(2,1)S(1)} %pad.14), channel_id=1, source_target_pairs={{0,4},{4,0},{8,12},{12,8},{16,20},{20,16},{24,28},{28,24},{1,5},{5... | collective-permute-start | bytes 995336 | tf_op jit(solution)/shard_map/ppermute | solution.py:1560
  12.5 120.2 %collective-permute-start.4 = (bf16[144,1152]{1,0:T(8,128)(2,1)S(1)}, bf16[144,1152]{1,0:T(8,128)(2,1)S(1)}, u32[]{:S(2)}, u32[]{:S(2)}) collective-permute-start(bf16[144,1152]{1,0:T(8,128)(2,1)S(1)} %pad.16), channel_id=1, source_target_pairs={{0,4},{4,0},{8,12},{12,8},{16,20},{20,16},{24,28},{28,24},{1,5},{5... | collective-permute-start | bytes 995336 | tf_op jit(solution)/shard_map/ppermute | solution.py:1560
  13.7 133.0 %all-gather.8.cloned.1.call-start = ((), (), s32[]{:S(2)}) async-start(), calls=%async_computation.6 | async-start | bytes 3317760 | tf_op jit(solution)/shard_map/all_gather | solution.py:1567
  77.6 4.0 copy-start.13
  78.3 3.3 copy-start.15
  81.7 171.4 %all-gather.12.cloned.1.call-start = ((), (), s32[]{:S(2)}) async-start(), calls=%async_computation.8 | async-start | bytes 3317760 | tf_op jit(solution)/shard_map/all_gather | solution.py:1567
  112.6 32.4 %collective-permute-start.1 = (bf16[576,1152]{1,0:T(8,128)(2,1)}, bf16[576,1152]{1,0:T(8,128)(2,1)}, u32[]{:S(2)}, u32[]{:S(2)}) collective-permute-start(bf16[576,1152]{1,0:T(8,128)(2,1)} %all-gather.6.cloned.1.call-done), channel_id=1, source_target_pairs={{0,4},{4,0},{8,12},{12,8},{16,20},{20,16},{24,28},{28,24},{1,5},{5... | collective-permute-start | bytes 3981320 | tf_op jit(solution)/shard_map/ppermute | solution.py:1560
  132.7 100.9 %collective-permute-start.3 = (bf16[144,1152]{1,0:T(8,128)(2,1)S(1)}, bf16[144,1152]{1,0:T(8,128)(2,1)S(1)}, u32[]{:S(2)}, u32[]{:S(2)}) collective-permute-start(bf16[144,1152]{1,0:T(8,128)(2,1)S(1)} %pad.13), channel_id=1, source_target_pairs={{0,4},{4,0},{8,12},{12,8},{16,20},{20,16},{24,28},{28,24},{1,5},{5... | collective-permute-start | bytes 995336 | tf_op jit(solution)/shard_map/ppermute | solution.py:1560
  133.7 156.6 %all-gather.14.cloned.1.call-start = ((), (), s32[]{:S(2)}) async-start(), calls=%async_computation.9 | async-start | bytes 3317760 | tf_op jit(solution)/shard_map/all_gather | solution.py:1567
  134.1 59.4 %collective-permute-start.2 = (bf16[576,1152]{1,0:T(8,128)(2,1)}, bf16[576,1152]{1,0:T(8,128)(2,1)}, u32[]{:S(2)}, u32[]{:S(2)}) collective-permute-start(bf16[576,1152]{1,0:T(8,128)(2,1)} %all-gather.10.cloned.1.call-done), channel_id=1, source_target_pairs={{0,4},{4,0},{8,12},{12,8},{16,20},{20,16},{24,28},{28,24},{1,5},{5... | collective-permute-start | bytes 3981320 | tf_op jit(solution)/shard_map/ppermute | solution.py:1560
  234.6 172.1 %reduce-scatter.6.cloned.1.call-start = ((), (), s32[]{:S(2)}) async-start(), calls=%async_computation.10 | async-start | bytes 3317760 | tf_op jit(solution)/shard_map/reduce_scatter | solution.py:1625
  331.8 0.7 copy-start.14
  331.8 2.0 copy-start.25
  331.8 122.3 %reduce-scatter.12.cloned.1.call-start = ((), (), s32[]{:S(2)}) async-start(), calls=%async_computation.13 | async-start | bytes 1658880 | tf_op jit(solution)/shard_map/reduce_scatter | solution.py:1625
  333.8 31.6 %collective-permute-start.5 = (bf16[4,144,1152]{2,1,0:T(8,128)(2,1)S(1)}, bf16[4,144,1152]{2,1,0:T(8,128)(2,1)S(1)}, u32[]{:S(2)}, u32[]{:S(2)}) collective-permute-start(bf16[4,144,1152]{2,1,0:T(8,128)(2,1)S(1)} %copy-done.25), channel_id=1, source_target_pairs={{0,4},{4,0},{8,12},{12,8},{16,20},{20,16},{24,28},{28,24},{1,5},{5... | collective-permute-start | bytes 3981320 | tf_op jit(solution)/shard_map/ppermute | solution.py:1560
  333.8 31.6 %copy-start.1 = (bf16[4,144,1152]{2,1,0:T(8,128)(2,1)S(1)}, bf16[4,144,1152]{2,1,0:T(8,128)(2,1)}, u32[]{:S(2)}) copy-start(bf16[4,144,1152]{2,1,0:T(8,128)(2,1)} %get-tuple-element.158) | copy-start | bytes 3981316
  366.8 120.3 %reduce-scatter.8.cloned.1.call-start = ((), (), s32[]{:S(2)}) async-start(), calls=%async_computation.11 | async-start | bytes 3317760 | tf_op jit(solution)/shard_map/reduce_scatter | solution.py:1625
  406.7 124.2 %reduce-scatter.14.cloned.1.call-start = ((), (), s32[]{:S(2)}) async-start(), calls=%async_computation.14 | async-start | bytes 3317760 | tf_op jit(solution)/shard_map/reduce_scatter | solution.py:1625
  454.2 129.8 %reduce-scatter.10.cloned.1.call-start = ((), (), s32[]{:S(2)}) async-start(), calls=%async_computation.12 | async-start | bytes 1658880 | tf_op jit(solution)/shard_map/reduce_scatter | solution.py:1625
  454.2 32.8 %collective-permute-start.6 = (bf16[4,144,1152]{2,1,0:T(8,128)(2,1)}, bf16[4,144,1152]{2,1,0:T(8,128)(2,1)S(1)}, u32[]{:S(2)}, u32[]{:S(2)}) collective-permute-start(bf16[4,144,1152]{2,1,0:T(8,128)(2,1)} %get-tuple-element.182), channel_id=1, source_target_pairs={{0,4},{4,0},{8,12},{12,8},{16,20},{20,16},{24,28},{28,24},{1,5},{5... | collective-permute-start | bytes 3981320 | tf_op jit(solution)/shard_map/ppermute | solution.py:1560
  454.8 30.4 %copy-start.7 = (bf16[144,1152]{1,0:T(8,128)(2,1)S(1)}, bf16[144,1152]{1,0:T(8,128)(2,1)}, u32[]{:S(2)}) copy-start(bf16[144,1152]{1,0:T(8,128)(2,1)} %reduce-scatter.12.cloned.1.call-done) | copy-start | bytes 995332
  485.2 1.9 copy-start
  584.0 1.4 copy-start.3
  584.0 1.2 copy-start.8
  585.6 1.2 copy-start.2
  588.7 2.4 copy-start.5
  591.1 1.7 copy-start.4
  592.8 1.1 copy-start.24
  592.8 1.7 copy-start.23
  592.8 2.2 copy-start.22
  592.8 2.8 copy-start.21
  592.8 3.4 copy-start.20
  592.8 4.0 copy-start.19
  592.8 4.5 copy-start.18
  592.8 5.1 copy-start.16
  592.8 5.7 copy-start.17
Sparse Core Ops, SparseCore 0:
  10.2 45.5 all-gather.5
  57.9 32.1 all-gather.9
  92.2 54.3 all-gather.7
  148.7 54.1 all-gather.11
  234.8 53.0 all-gather.13
  332.0 49.8 reduce-scatter.5
  384.8 31.3 reduce-scatter.11
  418.4 51.4 reduce-scatter.7
  472.2 52.3 reduce-scatter.13
  527.3 48.0 reduce-scatter.9

commit v5 on v4

--- a/solution.py
+++ b/solution.py
@@ -607,7 +607,7 @@
     return together.T[:8]
 
 
-def load_pairs(meta, own_pairs, far_pairs, key_scratch, value_scratch, heads):
+def load_pairs(meta, own_pairs, far_pairs, key_marks, key_scratch, value_scratch, heads):
     rows = 2 * (own_pairs.shape[2] * LANES // (2 * heads * HEAD_DIM))
     hid, half = meta[0], meta[1]
     windows = pair_windows(2 * heads * HEAD_DIM)
@@ -615,22 +615,23 @@
         for slot in range(4):
             place = jnp.bitwise_xor(half, which) * 4 + jnp.bitwise_xor(hid, slot)
             start = pl.ds(pl.multiple_of(place * rows, rows), rows)
+            marks = key_marks[start, :]
             halves = [unpack_half(source[slot, index], rows // 2) for index in range(2)]
             tiles = [jnp.concatenate(both, axis=0) for both in zip(*halves)]
             spread = spread_heads(jnp.concatenate(tiles, axis=1), windows)
             for head in range(heads):
-                key_scratch[head, start, :] = spread[head]
+                key_scratch[head, start, :] = spread[head] + marks
                 value_scratch[head, start, :] = spread[heads + head]
 
 
 def attend_kernel(
-    meta, queries, own_pairs, far_pairs, query_ids, key_ids, mixture, logsum,
+    meta, queries, own_pairs, far_pairs, query_marks, key_marks, mixture, logsum,
     key_scratch, value_scratch, score_scratch, high_scratch, total_scratch, sum_scratch, query_scratch,
     *, heads
 ):
     rows = queries.shape[1]
     head_cols = heads * HEAD_DIM
-    load_pairs(meta, own_pairs, far_pairs, key_scratch, value_scratch, heads)
+    load_pairs(meta, own_pairs, far_pairs, key_marks, key_scratch, value_scratch, heads)
     query_windows = pair_windows(head_cols)
     mixed_windows = pair_windows(mixture.shape[2], mixture.shape[2] - head_cols)
 
@@ -638,19 +639,17 @@
         slot = jnp.bitwise_xor(meta[0], block)
         first, last = meta[2 + 2 * block], meta[3 + 2 * block]
         own = pl.ds(pl.multiple_of(block * rows, rows), rows)
-        ids = query_ids[own, :]
+        marks = query_marks[own, :]
         for head, query in enumerate(spread_heads(queries[slot], query_windows)):
-            query_scratch[head] = query
+            query_scratch[head] = query + marks
         high_scratch[...] = jnp.full_like(high_scratch, -3e38)
         sum_scratch[...] = jnp.zeros_like(sum_scratch)
         total_scratch[...] = jnp.zeros_like(total_scratch)
 
         def scores_of(key_block, inner):
             keys = pl.ds(pl.multiple_of(key_block * KEYS, KEYS), KEYS)
-            same = ids == key_ids[:, keys]
             for head in range(heads):
                 scores = dot(query_scratch[head], key_scratch[head, keys, :], NT)
-                scores = jnp.where(same, scores, MASKED)
                 score_scratch[head, :, keys] = scores
                 high = high_scratch[head]
                 for lane in range(0, KEYS, LANES):
@@ -690,7 +689,7 @@
     lax.fori_loop(0, 4, one_block, 0)
 
 
-def attend(meta, queries, own_pairs, far_pairs, query_ids, key_ids, lead):
+def attend(meta, queries, own_pairs, far_pairs, query_marks, key_marks, lead):
     _, rows, head_cols = queries.shape
     heads = head_cols // HEAD_DIM
     own, count = 4 * rows, 8 * rows
@@ -715,11 +714,11 @@
             pltpu.VMEM((heads, rows, LANES), BF),
         ],
         compiler_params=pltpu.CompilerParams(vmem_limit_bytes=VMEM_LIMIT),
-    )(meta, queries, own_pairs, far_pairs, query_ids, key_ids)
+    )(meta, queries, own_pairs, far_pairs, query_marks, key_marks)
 
 
 def attend_back_kernel(
-    meta, queries, own_pairs, far_pairs, query_ids, key_ids, grad_mixture, logsum,
+    meta, queries, own_pairs, far_pairs, query_marks, key_marks, grad_mixture, logsum,
     grad_queries, grad_own, grad_far,
     key_scratch, value_scratch, grad_key, grad_value, grad_query, query_scratch, grad_scratch,
     prob_scratch, grad_prob_scratch, delta_scratch,
@@ -727,7 +726,7 @@
 ):
     rows = queries.shape[1]
     head_cols = heads * HEAD_DIM
-    load_pairs(meta, own_pairs, far_pairs, key_scratch, value_scratch, heads)
+    load_pairs(meta, own_pairs, far_pairs, key_marks, key_scratch, value_scratch, heads)
     query_windows = pair_windows(head_cols)
     mixed_windows = pair_windows(grad_mixture.shape[2], grad_mixture.shape[2] - head_cols)
     grad_key[...] = jnp.zeros_like(grad_key)
@@ -737,9 +736,9 @@
         slot = jnp.bitwise_xor(meta[0], block)
         first, last = meta[2 + 2 * block], meta[3 + 2 * block]
         own = pl.ds(pl.multiple_of(block * rows, rows), rows)
-        ids = query_ids[:, own]
+        marks = query_marks[own, :]
         for head, query in enumerate(spread_heads(queries[slot], query_windows)):
-            query_scratch[head] = query
+            query_scratch[head] = query + marks
         for head, grad in enumerate(spread_heads(grad_mixture[slot], mixed_windows)):
             grad_scratch[head] = grad
         logs = logsum[:, own]
@@ -748,11 +747,10 @@
 
         def probs_of(key_block, inner):
             keys = pl.ds(pl.multiple_of(key_block * KEYS, KEYS), KEYS)
-            same = key_ids[keys, :] == ids
             for head in range(heads):
                 grad = grad_scratch[head]
                 scores = dot(key_scratch[head, keys, :], query_scratch[head], NT)
-                probs = jnp.where(same, jnp.exp2(scores - logs[head : head + 1]), 0.0)
+                probs = jnp.exp2(scores - logs[head : head + 1])
                 grad_probs = dot(value_scratch[head, keys, :], grad, NT)
                 prob_scratch[head, keys, :] = probs
                 grad_prob_scratch[head, keys, :] = grad_probs
@@ -775,7 +773,11 @@
             return inner
 
         lax.fori_loop(first, last, one_key, 0)
-        scaled = [(grad_query[head] * HEAD_DIM ** (-0.5)).astype(BF) for head in range(heads)]
+        real = lax.broadcasted_iota(jnp.int32, (rows, LANES), 1) < HEAD_DIM
+        scaled = [
+            jnp.where(real, grad_query[head] * HEAD_DIM ** (-0.5), 0.0).astype(BF)
+            for head in range(heads)
+        ]
         grad_queries[slot] = join_heads(scaled, query_windows, head_cols).astype(BF)
         return carry
 
@@ -794,7 +796,9 @@
                 pack_half(tiles, target.at[slot, index])
 
 
-def attend_back(meta, queries, own_pairs, far_pairs, query_ids, key_ids, grad_mixture, logsum):
+def attend_back(
+    meta, queries, own_pairs, far_pairs, query_marks, key_marks, grad_mixture, logsum
+):
     _, rows, head_cols = queries.shape
     heads = head_cols // HEAD_DIM
     count = 8 * rows
@@ -823,7 +827,7 @@
             pltpu.VMEM((heads, 8, rows), F32),
         ],
         compiler_params=pltpu.CompilerParams(vmem_limit_bytes=VMEM_LIMIT),
-    )(meta, queries, own_pairs, far_pairs, query_ids, key_ids, grad_mixture, logsum)
+    )(meta, queries, own_pairs, far_pairs, query_marks, key_marks, grad_mixture, logsum)
 
 
 def mlp_kernel(*refs, layer, parts, last):
@@ -838,7 +842,7 @@
     rows = x.shape[0]
     hidden_cols = up_weight.shape[1]
     out_cols = out_weight.shape[1]
-    chunks = chunks_of(rows, 2)
+    chunks = chunks_of(rows, 4)
     out_part = pl.ds(x.shape[1] - out_cols, out_cols)
     loads = [
         moves.load(mixture_hbm, mixture), load_weight(net, moves, mixed_hbm, out_part, out_weight),
@@ -938,7 +942,7 @@
     parts = (len(mixed), len(up), len(down))
     kernel = functools.partial(mlp_kernel, layer=layer, parts=parts, last=last)
     moves = 8 + sum(weight_loads(part) for part in (mixed, up, down) if part)
-    return run(kernel, "mlp", 48, inputs, outputs, scratch, 8 * layer + 1, 18, moves)
+    return run(kernel, "mlp", 48, inputs, outputs, scratch, 8 * layer + 1, 32, moves)
 
 
 def mlp_back_kernel(*refs, layer, parts, given, shard, crossing):
@@ -1524,6 +1528,13 @@
     place = jnp.stack([hid, tok % 2]).astype(jnp.int32)
     meta = jnp.concatenate([place, key_ranges(own_ids, row_ids, rows)])
 
+    starts = jnp.concatenate([jnp.zeros(1, jnp.int32), (row_ids[1:] != row_ids[:-1]).astype(jnp.int32)])
+    number = jnp.cumsum(starts)[:, None] + HEAD_DIM
+    lane = lax.broadcasted_iota(jnp.int32, (row_ids.shape[0], LANES), 1)
+    key_marks = jnp.where((lane == number) | (lane < HEAD_DIM), 0.0, MASKED).astype(BF)
+    own_number = lax.dynamic_slice_in_dim(number, tok % 2 * token_count, token_count)
+    query_marks = (lane[:token_count] == own_number).astype(BF)
+
     def side_by_side(*parts):
         return jnp.concatenate(parts, axis=1)
 
@@ -1603,7 +1614,7 @@
             queries, coming, coming_other = hold(queries, coming, coming_other)
             downs.append([along(pair_rows(coming, coming_other))])
         mixture, logsum = attend(
-            meta, queries, own_pairs, far_pairs, own_ids[:, None], row_ids[None, :], lead
+            meta, queries, own_pairs, far_pairs, query_marks, key_marks, lead
         )
         if more:
             coming, mixture = hold(down_part(layer + 1), mixture)
@@ -1663,8 +1674,7 @@
         down_grads[layer] = sum_along(grad_down)
         up_own, up_other = halves_of(grad_up)
         grad_queries, grad_own, grad_far = attend_back(
-            meta, queries, own_pairs, far_pairs, own_ids[None, :], row_ids[:, None],
-            grad_mixture, logsum,
+            meta, queries, own_pairs, far_pairs, query_marks, key_marks, grad_mixture, logsum
         )
         up_other, grad_far = hold(up_other, grad_far)
         up_grad = added(up_own, up_other)

time: 614 us -> 606 us (0.987)
  Pallas kernels: 538 us -> 513 us
  waiting for transfers between devices: 11.3 us -> 24.1 us
    pallas_call x2, Pallas kernels: 61.5 us -> 49.3 us  [attend_back(): pl.pallas_call(functools.partial(attend_back_kernel, heads=heads), name='...]
    ppermute x7, waiting for transfers between devices: 9.44 us -> 20.5 us  [swap(): return lax.ppermute(part, 'tok', halves)]
    pallas_call x10, Pallas kernels: 440 us -> 432 us  [run(): pl.pallas_call(kernel, name=name, cost_estimate=micros(duration), out_sha...]
  transfers between devices with their start and end apart: 17 -> 17, of which waited for: 3 -> 5; matrix products, arithmetic and copies ran while one was open for 3% -> 3% of each run, Pallas kernels for 82% -> 79%
where the time goes in v5:
time: 606 us; the launch traced here: 597 us
  Pallas kernels  513 us (85%)
  waiting for transfers between devices  24.1 us (4%)
  local copies, waits for them, and re-layouts  20 us (3%)
  between operations  14.9 us (2%)
  other arithmetic  14.8 us (2%)
  starting transfers between devices  10.6 us (2%)
    pallas_call x10, Pallas kernels, run(): pl.pallas_call(kernel, name=name, cost_estimate=micros(duration), out_sha...  432 us
    pallas_call x2, Pallas kernels, attend_back(): pl.pallas_call(functools.partial(attend_back_kernel, heads=heads), name='...  49.3 us
    pallas_call x2, Pallas kernels, attend(): pl.pallas_call(functools.partial(attend_kernel, heads=heads), name='atten...  31.5 us
    ppermute x7, waiting for transfers between devices, swap(): return lax.ppermute(part, 'tok', halves)  20.5 us
  transfers between devices with their start and end apart: 17, of which 5 were waited for; matrix products, arithmetic and copies ran while one was open for 3% of the time, Pallas kernels for 79%

profile of v5, /device:TPU:0, one launch (start us, length us, event | category | flops | bytes accessed | tf_op | source)
XLA Modules:
  0.0 597.3 jit_solution(3920751431116863030)
XLA Ops:
  7.2 1.2 slice_bitcast_fusion.4
  8.4 0.8 pad.15
  9.3 3.0 collective-permute-start.4
  12.7 1.0 concatenate.16
  14.2 0.3 reduce-window.9
  14.4 0.2 select_reduce_fusion.1
  15.2 1.0 concatenate.13.refs_5_
  16.2 62.2 %entry.1 = (f32[256,1152]{1,0:T(8,128)}, f32[256,1152]{1,0:T(8,128)}, bf16[4,256,1152]{2,1,0:T(8,128)(2,1)}, f32[2,8,1152]{2,1,0:T(8,128)}, f32[2,896]{1,0:T(2,1...) custom-call(bf16[288,1024]{1,0:T(8,128)(2,1)} %bitcast.134, bf16[288,1024]{1,0:T(8,128)(2,1)} %bitcast.135, ...), custom_call_target="tpu_custom_call" | custom-call | flops 49999998976 | tf_op jit(solution)/shard_map/entry/pallas_call | solution.py:348
  78.5 1.2 select_convert_fusion.key_marks
  79.6 0.6 pad_add_fusion.1.meta
  80.2 0.9 fusion.1.query_marks
  81.2 0.9 pad_maximum_fusion
  82.2 30.9 %project.2 = (bf16[4,256,1152]{2,1,0:T(8,128)(2,1)}, bf16[4,256,288]{2,1,0:T(8,128)(2,1)}, bf16[4,2,576,128]{3,2,1,0:T(8,128)(2,1)}, bf16[4,2,576,128]{3,2,1,0:T(8,128)(2,1)}) custom-call(f32[256,1152]{1,0:T(8,128)} %get-tuple-element.131.refs_0_.refs_1_, f32[2,8,1152]{2,1,0:T(8,128)} %get-tuple-element.132.refs_1_.refs_2_, ...), custom_call_target="tpu_custom_call" | custom-call | flops 40000000000 | tf_op jit(solution)/shard_map/project/pallas_call | solution.py:348
  113.1 1.5 collective-permute-start.1
  114.7 15.8 %attend.2 = (bf16[4,256,384]{2,1,0:T(8,128)(2,1)}, f32[8,1024]{1,0:T(8,128)}) custom-call(s32[10]{0:T(128)} %pad_add_fusion.1.meta, bf16[4,256,288]{2,1,0:T(8,128)(2,1)} %get-tuple-element.135.queries, bf16[4,2,576,128]{3,2,1,0:T(8,128)(2,1)} %get-tuple-element.136.own_pairs, bf16[4,2,576,128]{3,2,1,0:T(8,128)(2,1)} %get-tuple-element.137.far_pairs, ...), custom_call_target="tpu_custom_call" | custom-call | flops 22000001024 | tf_op jit(solution)/shard_map/attend/pallas_call | solution.py:697
  130.4 0.5 collective-permute-start.3
  131.1 0.9 pad_maximum_fusion.1
  132.0 0.5 all-gather.14.cloned.1.call-start
  132.5 1.6 collective-permute-start.2
  134.1 11.5 %collective-permute-done.1 = bf16[576,1152]{1,0:T(8,128)(2,1)} collective-permute-done((bf16[576,1152]{1,0:T(8,128)(2,1)}, bf16[576,1152]{1,0:T(8,128)(2,1)}, u32[]{:S(2)}, u32[]{:S(2)}) %collective-permute-start.1) | collective-permute-done | bytes 1327136 | tf_op jit(solution)/shard_map/ppermute | solution.py:1571
  145.6 1.7 all-gather.8.cloned.1.call-done.refs_7_.refs_10_
  147.3 46.1 %mlp.2 = (f32[256,1152]{1,0:T(8,128)}, bf16[4,256,1152]{2,1,0:T(8,128)(2,1)}, bf16[4,256,1152]{2,1,0:T(8,128)(2,1)}, bf16[4,256,1152]{2,1,0:T(8,128)(2,1)}, f32[256,1152]{1,0:T(8,128)}) custom-call(bf16[4,256,384]{2,1,0:T(8,128)(2,1)} %get-tuple-element.139.refs_0_.refs_3_, f32[256,1152]{1,0:T(8,128)} %get-tuple-element.131.refs_0_.refs_1_, ...), custom_call_target="tpu_custom_call" | custom-call | flops 48000000000 | tf_op jit(solution)/shard_map/mlp/pallas_call | solution.py:348
  193.4 32.7 %project.3 = (bf16[4,256,1152]{2,1,0:T(8,128)(2,1)}, bf16[4,256,288]{2,1,0:T(8,128)(2,1)}, bf16[4,2,576,128]{3,2,1,0:T(8,128)(2,1)}, bf16[4,2,576,128]{3,2,1,0:T(8,128)(2,1)}) custom-call(f32[256,1152]{1,0:T(8,128)} %get-tuple-element.143.refs_0_.refs_1_, f32[2,8,1152]{2,1,0:T(8,128)} %get-tuple-element.132.refs_1_.refs_2_, ...), custom_call_target="tpu_custom_call" | custom-call | flops 40000000000 | tf_op jit(solution)/shard_map/project/pallas_call | solution.py:348
  226.2 0.9 pad_maximum_fusion.2
  227.2 15.7 %attend.3 = (bf16[4,256,384]{2,1,0:T(8,128)(2,1)}, f32[8,1024]{1,0:T(8,128)}) custom-call(s32[10]{0:T(128)} %pad_add_fusion.1.meta, bf16[4,256,288]{2,1,0:T(8,128)(2,1)} %get-tuple-element.146.queries, bf16[4,2,576,128]{3,2,1,0:T(8,128)(2,1)} %get-tuple-element.147.own_pairs, bf16[4,2,576,128]{3,2,1,0:T(8,128)(2,1)} %get-tuple-element.148.far_pairs, ...), custom_call_target="tpu_custom_call" | custom-call | flops 22000001024 | tf_op jit(solution)/shard_map/attend/pallas_call | solution.py:697
  242.9 35.3 %mlp.3 = (f32[256,1152]{1,0:T(8,128)}, bf16[4,256,1152]{2,1,0:T(8,128)(2,1)}, bf16[4,256,1152]{2,1,0:T(8,128)(2,1)}, bf16[4,256,1152]{2,1,0:T(8,128)(2,1)}) custom-call(bf16[4,256,384]{2,1,0:T(8,128)(2,1)} %get-tuple-element.149.refs_0_.refs_3_, f32[256,1152]{1,0:T(8,128)} %get-tuple-element.143.refs_0_.refs_1_, ...), custom_call_target="tpu_custom_call" | custom-call | flops 48000000000 | tf_op jit(solution)/shard_map/mlp/pallas_call | solution.py:348
  278.3 1.5 all-gather.14.cloned.1.call-done.refs_11_.refs_12_
  279.8 40.8 %mlp_back.2 = (f32[256,1152]{1,0:T(8,128)}, bf16[4,256,384]{2,1,0:T(8,128)(2,1)}, bf16[1152,1152]{1,0:T(8,128)(2,1)}, bf16[1152,384]{1,0:T(8,128)(2,1)}, f32[8,1...) custom-call(f32[256,1152]{1,0:T(8,128)} %get-tuple-element.129.refs_0_, ...), custom_call_target="tpu_custom_call" | custom-call | flops 48000000000 | tf_op jit(solution)/shard_map/mlp_back/pallas_call | solution.py:348
  320.7 1.2 copy-done.22
  321.9 1.5 collective-permute-start.5
  323.4 24.7 %attend_back.2 = (bf16[4,256,288]{2,1,0:T(8,128)(2,1)}, bf16[4,2,576,128]{3,2,1,0:T(8,128)(2,1)}, bf16[4,2,576,128]{3,2,1,0:T(8,128)(2,1)}) custom-call(s32[10]{0:T(128)} %pad_add_fusion.1.meta, bf16[4,256,288]{2,1,0:T(8,128)(2,1)} %get-tuple-element.146.queries, bf16[4,2,576,128]{3,2,1,0:T(8,128)(2,1)} %get-tuple-element.147.own_pairs, ...), custom_call_target="tpu_custom_call" | custom-call | flops 36999999488 | tf_op jit(solution)/shard_map/attend_back/pallas_call | solution.py:806
  348.0 5.6 collective-permute-done.5
  353.6 1.4 add_convert_fusion.1
  355.1 39.1 %project_back.2 = (f32[256,1152]{1,0:T(8,128)}, f32[8,1152]{1,0:T(8,128)}, f32[1,896]{1,0:T(1,128)}, bf16[1152,1152]{1,0:T(8,128)(2,1)}, f32[256,1152]{1,0:T(8,128)}) custom-call(f32[256,1152]{1,0:T(8,128)} %get-tuple-element.164.refs_0_, f32[256,1152]{1,0:T(8,128)} %get-tuple-element.143.refs_0_.refs_1_, f32[2,8,1152]{2,1,0:T(8,128)} %get-tuple-element.132.refs_1_.refs_2_, ...), custom_call_target="tpu_custom_call" | custom-call | flops 41999998976 | tf_op jit(solution)/shard_map/project_back/pallas_call | solution.py:348
  394.3 47.3 %mlp_back.3 = (f32[256,1152]{1,0:T(8,128)}, bf16[4,256,384]{2,1,0:T(8,128)(2,1)}, bf16[1152,1152]{1,0:T(8,128)(2,1)}, bf16[1152,384]{1,0:T(8,128)(2,1)}, f32[8,1...) custom-call(f32[256,1152]{1,0:T(8,128)} %get-tuple-element.172.refs_, ...), custom_call_target="tpu_custom_call" | custom-call | flops 48000000000 | tf_op jit(solution)/shard_map/mlp_back/pallas_call | solution.py:348
  441.7 1.5 collective-permute-start.6
  443.2 24.6 %attend_back.3 = (bf16[4,256,288]{2,1,0:T(8,128)(2,1)}, bf16[4,2,576,128]{3,2,1,0:T(8,128)(2,1)}, bf16[4,2,576,128]{3,2,1,0:T(8,128)(2,1)}) custom-call(s32[10]{0:T(128)} %pad_add_fusion.1.meta, bf16[4,256,288]{2,1,0:T(8,128)(2,1)} %get-tuple-element.135.queries, bf16[4,2,576,128]{3,2,1,0:T(8,128)(2,1)} %get-tuple-element.136.own_pairs, ...), custom_call_target="tpu_custom_call" | custom-call | flops 36999999488 | tf_op jit(solution)/shard_map/attend_back/pallas_call | solution.py:806
  467.9 0.8 slice_bitcast_fusion.2
  468.6 1.3 slice_bitcast_fusion
  470.0 3.5 collective-permute-done.6
  473.5 1.4 add_convert_fusion
  474.9 40.8 %project_back.3 = (f32[256,1152]{1,0:T(8,128)}, f32[8,1152]{1,0:T(8,128)}, f32[1,896]{1,0:T(1,128)}, bf16[1152,1152]{1,0:T(8,128)(2,1)}, f32[144,1152]{1,0:T(8,128)}) custom-call(f32[256,1152]{1,0:T(8,128)} %get-tuple-element.189.refs_0_, f32[256,1152]{1,0:T(8,128)} %get-tuple-element.131.refs_0_.refs_1_, f32[2,8,1152]{2,1,0:T(8,128)} %get-tuple-element.132.refs_1_.refs_2_, ...), custom_call_target="tpu_custom_call" | custom-call | flops 41999998976 | tf_op jit(solution)/shard_map/project_back/pallas_call | solution.py:348
  515.7 1.5 slice_bitcast_fusion.8
  517.3 57.0 %finish.1 = (f32[288,1024]{1,0:T(8,128)}, f32[288,1024]{1,0:T(8,128)}, f32[144,1152]{1,0:T(8,128)}, f32[2,288]{1,0:T(2,128)}, f32[2,288]{1,0:T(2,128)}, /*index=...) custom-call(f32[256,1152]{1,0:T(8,128)} %get-tuple-element.188.refs_, ...), custom_call_target="tpu_custom_call" | custom-call | flops 2000000000 | tf_op jit(solution)/shard_map/finish/pallas_call | solution.py:348
  574.3 1.1 slice_bitcast_fusion.3
  575.3 1.2 slice_bitcast_fusion.1
  576.8 1.2 maximum_convert_fusion
  577.9 1.1 maximum_bitcast_fusion
  579.1 0.8 maximum_bitcast_fusion.1
  579.9 0.8 pad_maximum_fusion.5
  580.7 0.8 pad_maximum_fusion.4
  581.5 0.8 pad_maximum_fusion.3
  582.3 1.0 copy.50
  583.3 0.7 copy-done.4
  584.0 1.0 copy.51
  585.0 0.6 copy.52
  585.6 0.6 copy.53
  586.2 0.6 copy.54
  586.8 0.6 copy.55
  587.4 0.6 copy.56
  587.9 0.6 copy.57
  588.5 0.6 copy.58
  589.1 0.6 copy.59
  589.7 0.6 copy.60
  (104 shorter events, 2.6 us)
Async XLA Ops:
  7.2 5.2 copy-start.6
  7.2 105.9 %all-gather.6.cloned.1.call-start = ((), (), s32[]{:S(2)}) async-start(), calls=%async_computation.5 | async-start | bytes 1658880 | tf_op jit(solution)/shard_map/all_gather | solution.py:1578
  9.2 123.3 %all-gather.10.cloned.1.call-start = ((), (), s32[]{:S(2)}) async-start(), calls=%async_computation.7 | async-start | bytes 1658880 | tf_op jit(solution)/shard_map/all_gather | solution.py:1578
  9.3 3.3 copy-start.10
  9.3 3.3 copy-start.11
  9.3 3.3 copy-start.8
  9.3 3.3 copy-start.9
  9.3 121.6 %collective-permute-start.4 = (bf16[144,1152]{1,0:T(8,128)(2,1)S(1)}, bf16[144,1152]{1,0:T(8,128)(2,1)S(1)}, u32[]{:S(2)}, u32[]{:S(2)}) collective-permute-start(bf16[144,1152]{1,0:T(8,128)(2,1)S(1)} %pad.16), channel_id=1, source_target_pairs={{0,4},{4,0},{8,12},{12,8},{16,20},{20,16},{24,28},{28,24},{1,5},{5... | collective-permute-start | bytes 995336 | tf_op jit(solution)/shard_map/ppermute | solution.py:1571
  12.4 68.7 %collective-permute-start = (bf16[144,1152]{1,0:T(8,128)(2,1)S(1)}, bf16[144,1152]{1,0:T(8,128)(2,1)S(1)}, u32[]{:S(2)}, u32[]{:S(2)}) collective-permute-start(bf16[144,1152]{1,0:T(8,128)(2,1)S(1)} %pad.14), channel_id=1, source_target_pairs={{0,4},{4,0},{8,12},{12,8},{16,20},{20,16},{24,28},{28,24},{1,5},{5... | collective-permute-start | bytes 995336 | tf_op jit(solution)/shard_map/ppermute | solution.py:1571
  12.6 1.2 copy-start.12
  13.7 133.6 %all-gather.8.cloned.1.call-start = ((), (), s32[]{:S(2)}) async-start(), calls=%async_computation.6 | async-start | bytes 3317760 | tf_op jit(solution)/shard_map/all_gather | solution.py:1578
  82.2 160.8 %all-gather.12.cloned.1.call-start = ((), (), s32[]{:S(2)}) async-start(), calls=%async_computation.8 | async-start | bytes 3317760 | tf_op jit(solution)/shard_map/all_gather | solution.py:1578
  113.1 32.4 %collective-permute-start.1 = (bf16[576,1152]{1,0:T(8,128)(2,1)}, bf16[576,1152]{1,0:T(8,128)(2,1)}, u32[]{:S(2)}, u32[]{:S(2)}) collective-permute-start(bf16[576,1152]{1,0:T(8,128)(2,1)} %all-gather.6.cloned.1.call-done), channel_id=1, source_target_pairs={{0,4},{4,0},{8,12},{12,8},{16,20},{20,16},{24,28},{28,24},{1,5},{5... | collective-permute-start | bytes 3981320 | tf_op jit(solution)/shard_map/ppermute | solution.py:1571
  130.4 95.7 %collective-permute-start.3 = (bf16[144,1152]{1,0:T(8,128)(2,1)S(1)}, bf16[144,1152]{1,0:T(8,128)(2,1)S(1)}, u32[]{:S(2)}, u32[]{:S(2)}) collective-permute-start(bf16[144,1152]{1,0:T(8,128)(2,1)S(1)} %pad.13), channel_id=1, source_target_pairs={{0,4},{4,0},{8,12},{12,8},{16,20},{20,16},{24,28},{28,24},{1,5},{5... | collective-permute-start | bytes 995336 | tf_op jit(solution)/shard_map/ppermute | solution.py:1571
  132.0 147.8 %all-gather.14.cloned.1.call-start = ((), (), s32[]{:S(2)}) async-start(), calls=%async_computation.9 | async-start | bytes 3317760 | tf_op jit(solution)/shard_map/all_gather | solution.py:1578
  132.5 60.9 %collective-permute-start.2 = (bf16[576,1152]{1,0:T(8,128)(2,1)}, bf16[576,1152]{1,0:T(8,128)(2,1)}, u32[]{:S(2)}, u32[]{:S(2)}) collective-permute-start(bf16[576,1152]{1,0:T(8,128)(2,1)} %all-gather.10.cloned.1.call-done), channel_id=1, source_target_pairs={{0,4},{4,0},{8,12},{12,8},{16,20},{20,16},{24,28},{28,24},{1,5},{5... | collective-permute-start | bytes 3981320 | tf_op jit(solution)/shard_map/ppermute | solution.py:1571
  227.1 167.2 %reduce-scatter.6.cloned.1.call-start = ((), (), s32[]{:S(2)}) async-start(), calls=%async_computation.10 | async-start | bytes 3317760 | tf_op jit(solution)/shard_map/reduce_scatter | solution.py:1636
  320.6 1.3 copy-start.22
  320.6 121.0 %reduce-scatter.12.cloned.1.call-start = ((), (), s32[]{:S(2)}) async-start(), calls=%async_computation.13 | async-start | bytes 1658880 | tf_op jit(solution)/shard_map/reduce_scatter | solution.py:1636
  321.9 31.7 %collective-permute-start.5 = (bf16[4,144,1152]{2,1,0:T(8,128)(2,1)S(1)}, bf16[4,144,1152]{2,1,0:T(8,128)(2,1)S(1)}, u32[]{:S(2)}, u32[]{:S(2)}) collective-permute-start(bf16[4,144,1152]{2,1,0:T(8,128)(2,1)S(1)} %copy-done.22), channel_id=1, source_target_pairs={{0,4},{4,0},{8,12},{12,8},{16,20},{20,16},{24,28},{28,24},{1,5},{5... | collective-permute-start | bytes 3981320 | tf_op jit(solution)/shard_map/ppermute | solution.py:1571
  323.4 30.2 %copy-start.1 = (bf16[4,144,1152]{2,1,0:T(8,128)(2,1)S(1)}, bf16[4,144,1152]{2,1,0:T(8,128)(2,1)}, u32[]{:S(2)}) copy-start(bf16[4,144,1152]{2,1,0:T(8,128)(2,1)} %get-tuple-element.158) | copy-start | bytes 3981316
  355.0 114.9 %reduce-scatter.8.cloned.1.call-start = ((), (), s32[]{:S(2)}) async-start(), calls=%async_computation.11 | async-start | bytes 3317760 | tf_op jit(solution)/shard_map/reduce_scatter | solution.py:1636
  394.2 123.0 %reduce-scatter.14.cloned.1.call-start = ((), (), s32[]{:S(2)}) async-start(), calls=%async_computation.14 | async-start | bytes 3317760 | tf_op jit(solution)/shard_map/reduce_scatter | solution.py:1636
  441.7 132.6 %reduce-scatter.10.cloned.1.call-start = ((), (), s32[]{:S(2)}) async-start(), calls=%async_computation.12 | async-start | bytes 1658880 | tf_op jit(solution)/shard_map/reduce_scatter | solution.py:1636
  441.7 31.8 %collective-permute-start.6 = (bf16[4,144,1152]{2,1,0:T(8,128)(2,1)}, bf16[4,144,1152]{2,1,0:T(8,128)(2,1)S(1)}, u32[]{:S(2)}, u32[]{:S(2)}) collective-permute-start(bf16[4,144,1152]{2,1,0:T(8,128)(2,1)} %get-tuple-element.182), channel_id=1, source_target_pairs={{0,4},{4,0},{8,12},{12,8},{16,20},{20,16},{24,28},{28,24},{1,5},{5... | collective-permute-start | bytes 3981320 | tf_op jit(solution)/shard_map/ppermute | solution.py:1571
  443.2 24.7 %copy-start.7 = (bf16[144,1152]{1,0:T(8,128)(2,1)S(1)}, bf16[144,1152]{1,0:T(8,128)(2,1)}, u32[]{:S(2)}) copy-start(bf16[144,1152]{1,0:T(8,128)(2,1)} %reduce-scatter.12.cloned.1.call-done) | copy-start | bytes 995332
  467.9 5.6 copy-start
  574.2 2.3 copy-start.3
  575.3 1.4 copy-start.2
  579.9 2.4 copy-start.5
  582.3 1.7 copy-start.4
  584.0 1.1 copy-start.21
  584.0 1.7 copy-start.20
  584.0 2.2 copy-start.19
  584.0 2.8 copy-start.18
  584.0 3.4 copy-start.17
  584.0 4.0 copy-start.16
  584.0 4.5 copy-start.15
  584.0 5.1 copy-start.13
  584.0 5.7 copy-start.14
Sparse Core Ops, SparseCore 0:
  10.2 45.3 all-gather.5
  57.7 33.0 all-gather.9
  92.9 54.3 all-gather.7
  149.3 54.1 all-gather.11
  227.2 52.5 all-gather.13
  320.7 52.3 reduce-scatter.5
  376.0 31.3 reduce-scatter.11
  409.7 51.4 reduce-scatter.7
  463.5 52.3 reduce-scatter.13
  518.6 48.0 reduce-scatter.9

commit v6 on v5

--- a/solution.py
+++ b/solution.py
@@ -611,17 +611,25 @@
     rows = 2 * (own_pairs.shape[2] * LANES // (2 * heads * HEAD_DIM))
     hid, half = meta[0], meta[1]
     windows = pair_windows(2 * heads * HEAD_DIM)
+    lowest, highest = meta[2], meta[3]
+    for block in range(1, 4):
+        lowest = jnp.minimum(lowest, meta[2 + 2 * block])
+        highest = jnp.maximum(highest, meta[3 + 2 * block])
     for which, source in ((0, own_pairs), (1, far_pairs)):
         for slot in range(4):
             place = jnp.bitwise_xor(half, which) * 4 + jnp.bitwise_xor(hid, slot)
-            start = pl.ds(pl.multiple_of(place * rows, rows), rows)
-            marks = key_marks[start, :]
-            halves = [unpack_half(source[slot, index], rows // 2) for index in range(2)]
-            tiles = [jnp.concatenate(both, axis=0) for both in zip(*halves)]
-            spread = spread_heads(jnp.concatenate(tiles, axis=1), windows)
-            for head in range(heads):
-                key_scratch[head, start, :] = spread[head] + marks
-                value_scratch[head, start, :] = spread[heads + head]
+            step = place * rows // KEYS
+
+            @pl.when(jnp.logical_and(step >= lowest, step < highest))
+            def load(source=source, slot=slot, place=place):
+                start = pl.ds(pl.multiple_of(place * rows, rows), rows)
+                marks = key_marks[start, :]
+                halves = [unpack_half(source[slot, index], rows // 2) for index in range(2)]
+                tiles = [jnp.concatenate(both, axis=0) for both in zip(*halves)]
+                spread = spread_heads(jnp.concatenate(tiles, axis=1), windows)
+                for head in range(heads):
+                    key_scratch[head, start, :] = spread[head] + marks
+                    value_scratch[head, start, :] = spread[heads + head]
 
 
 def attend_kernel(

time: 606 us -> 607 us (level)
  transfers between devices with their start and end apart: 17 -> 17, of which waited for: 5 -> 5; matrix products, arithmetic and copies ran while one was open for 3% -> 3% of each run, Pallas kernels for 79% -> 80%
where the time goes in v6:
time: 607 us; the launch traced here: 598 us
  Pallas kernels  517 us (85%)
  waiting for transfers between devices  21.3 us (4%)
  local copies, waits for them, and re-layouts  20 us (3%)
  between operations  15.1 us (2%)
  other arithmetic  14.8 us (2%)
  starting transfers between devices  9.82 us (2%)
    pallas_call x10, Pallas kernels, run(): pl.pallas_call(kernel, name=name, cost_estimate=micros(duration), out_sha...  433 us
    pallas_call x2, Pallas kernels, attend_back(): pl.pallas_call(functools.partial(attend_back_kernel, heads=heads), name='...  51.1 us
    pallas_call x2, Pallas kernels, attend(): pl.pallas_call(functools.partial(attend_kernel, heads=heads), name='atten...  33.3 us
    ppermute x7, waiting for transfers between devices, swap(): return lax.ppermute(part, 'tok', halves)  18.5 us
  transfers between devices with their start and end apart: 17, of which 5 were waited for; matrix products, arithmetic and copies ran while one was open for 3% of the time, Pallas kernels for 80%

profile of v6, /device:TPU:0, one launch (start us, length us, event | category | flops | bytes accessed | tf_op | source)
XLA Modules:
  0.0 598.1 jit_solution(672034709614457831)
XLA Ops:
  7.2 1.2 slice_bitcast_fusion.4
  8.4 0.8 pad.15
  9.3 3.0 collective-permute-start.4
  12.7 1.0 concatenate.16
  14.2 0.3 reduce-window.9
  14.4 0.2 select_reduce_fusion.1
  15.2 1.0 concatenate.13.refs_5_
  16.2 62.2 %entry.1 = (f32[256,1152]{1,0:T(8,128)}, f32[256,1152]{1,0:T(8,128)}, bf16[4,256,1152]{2,1,0:T(8,128)(2,1)}, f32[2,8,1152]{2,1,0:T(8,128)}, f32[2,896]{1,0:T(2,1...) custom-call(bf16[288,1024]{1,0:T(8,128)(2,1)} %bitcast.134, bf16[288,1024]{1,0:T(8,128)(2,1)} %bitcast.135, ...), custom_call_target="tpu_custom_call" | custom-call | flops 49999998976 | tf_op jit(solution)/shard_map/entry/pallas_call | solution.py:348
  78.5 1.2 select_convert_fusion.key_marks
  79.6 0.6 pad_add_fusion.1.meta
  80.2 0.9 fusion.1.query_marks
  81.2 0.9 pad_maximum_fusion
  82.2 30.9 %project.2 = (bf16[4,256,1152]{2,1,0:T(8,128)(2,1)}, bf16[4,256,288]{2,1,0:T(8,128)(2,1)}, bf16[4,2,576,128]{3,2,1,0:T(8,128)(2,1)}, bf16[4,2,576,128]{3,2,1,0:T(8,128)(2,1)}) custom-call(f32[256,1152]{1,0:T(8,128)} %get-tuple-element.131.refs_0_.refs_1_, f32[2,8,1152]{2,1,0:T(8,128)} %get-tuple-element.132.refs_1_.refs_2_, ...), custom_call_target="tpu_custom_call" | custom-call | flops 40000000000 | tf_op jit(solution)/shard_map/project/pallas_call | solution.py:348
  113.1 1.5 collective-permute-start.1
  114.7 16.7 %attend.2 = (bf16[4,256,384]{2,1,0:T(8,128)(2,1)}, f32[8,1024]{1,0:T(8,128)}) custom-call(s32[10]{0:T(128)} %pad_add_fusion.1.meta, bf16[4,256,288]{2,1,0:T(8,128)(2,1)} %get-tuple-element.135.queries, bf16[4,2,576,128]{3,2,1,0:T(8,128)(2,1)} %get-tuple-element.136.own_pairs, bf16[4,2,576,128]{3,2,1,0:T(8,128)(2,1)} %get-tuple-element.137.far_pairs, ...), custom_call_target="tpu_custom_call" | custom-call | flops 22000001024 | tf_op jit(solution)/shard_map/attend/pallas_call | solution.py:705
  131.5 0.9 pad_maximum_fusion.1
  132.4 0.3 all-gather.14.cloned.1.call-start
  132.7 2.1 collective-permute-start.2
  134.8 10.8 %collective-permute-done.1 = bf16[576,1152]{1,0:T(8,128)(2,1)} collective-permute-done((bf16[576,1152]{1,0:T(8,128)(2,1)}, bf16[576,1152]{1,0:T(8,128)(2,1)}, u32[]{:S(2)}, u32[]{:S(2)}) %collective-permute-start.1) | collective-permute-done | bytes 1327136 | tf_op jit(solution)/shard_map/ppermute | solution.py:1579
  145.6 1.7 all-gather.8.cloned.1.call-done.refs_7_.refs_10_
  147.3 46.1 %mlp.2 = (f32[256,1152]{1,0:T(8,128)}, bf16[4,256,1152]{2,1,0:T(8,128)(2,1)}, bf16[4,256,1152]{2,1,0:T(8,128)(2,1)}, bf16[4,256,1152]{2,1,0:T(8,128)(2,1)}, f32[256,1152]{1,0:T(8,128)}) custom-call(bf16[4,256,384]{2,1,0:T(8,128)(2,1)} %get-tuple-element.139.refs_0_.refs_3_, f32[256,1152]{1,0:T(8,128)} %get-tuple-element.131.refs_0_.refs_1_, ...), custom_call_target="tpu_custom_call" | custom-call | flops 48000000000 | tf_op jit(solution)/shard_map/mlp/pallas_call | solution.py:348
  193.4 32.7 %project.3 = (bf16[4,256,1152]{2,1,0:T(8,128)(2,1)}, bf16[4,256,288]{2,1,0:T(8,128)(2,1)}, bf16[4,2,576,128]{3,2,1,0:T(8,128)(2,1)}, bf16[4,2,576,128]{3,2,1,0:T(8,128)(2,1)}) custom-call(f32[256,1152]{1,0:T(8,128)} %get-tuple-element.143.refs_0_.refs_1_, f32[2,8,1152]{2,1,0:T(8,128)} %get-tuple-element.132.refs_1_.refs_2_, ...), custom_call_target="tpu_custom_call" | custom-call | flops 40000000000 | tf_op jit(solution)/shard_map/project/pallas_call | solution.py:348
  226.2 0.9 pad_maximum_fusion.2
  227.2 16.7 %attend.3 = (bf16[4,256,384]{2,1,0:T(8,128)(2,1)}, f32[8,1024]{1,0:T(8,128)}) custom-call(s32[10]{0:T(128)} %pad_add_fusion.1.meta, bf16[4,256,288]{2,1,0:T(8,128)(2,1)} %get-tuple-element.146.queries, bf16[4,2,576,128]{3,2,1,0:T(8,128)(2,1)} %get-tuple-element.147.own_pairs, bf16[4,2,576,128]{3,2,1,0:T(8,128)(2,1)} %get-tuple-element.148.far_pairs, ...), custom_call_target="tpu_custom_call" | custom-call | flops 22000001024 | tf_op jit(solution)/shard_map/attend/pallas_call | solution.py:705
  243.8 35.4 %mlp.3 = (f32[256,1152]{1,0:T(8,128)}, bf16[4,256,1152]{2,1,0:T(8,128)(2,1)}, bf16[4,256,1152]{2,1,0:T(8,128)(2,1)}, bf16[4,256,1152]{2,1,0:T(8,128)(2,1)}) custom-call(bf16[4,256,384]{2,1,0:T(8,128)(2,1)} %get-tuple-element.149.refs_0_.refs_3_, f32[256,1152]{1,0:T(8,128)} %get-tuple-element.143.refs_0_.refs_1_, ...), custom_call_target="tpu_custom_call" | custom-call | flops 48000000000 | tf_op jit(solution)/shard_map/mlp/pallas_call | solution.py:348
  279.2 0.8 all-gather.14.cloned.1.call-done.refs_11_.refs_12_
  280.0 40.8 %mlp_back.2 = (f32[256,1152]{1,0:T(8,128)}, bf16[4,256,384]{2,1,0:T(8,128)(2,1)}, bf16[1152,1152]{1,0:T(8,128)(2,1)}, bf16[1152,384]{1,0:T(8,128)(2,1)}, f32[8,1...) custom-call(f32[256,1152]{1,0:T(8,128)} %get-tuple-element.129.refs_0_, ...), custom_call_target="tpu_custom_call" | custom-call | flops 48000000000 | tf_op jit(solution)/shard_map/mlp_back/pallas_call | solution.py:348
  320.9 1.2 copy-done.22
  322.1 1.5 collective-permute-start.5
  323.6 25.6 %attend_back.2 = (bf16[4,256,288]{2,1,0:T(8,128)(2,1)}, bf16[4,2,576,128]{3,2,1,0:T(8,128)(2,1)}, bf16[4,2,576,128]{3,2,1,0:T(8,128)(2,1)}) custom-call(s32[10]{0:T(128)} %pad_add_fusion.1.meta, bf16[4,256,288]{2,1,0:T(8,128)(2,1)} %get-tuple-element.146.queries, bf16[4,2,576,128]{3,2,1,0:T(8,128)(2,1)} %get-tuple-element.147.own_pairs, ...), custom_call_target="tpu_custom_call" | custom-call | flops 36999999488 | tf_op jit(solution)/shard_map/attend_back/pallas_call | solution.py:814
  349.2 4.6 collective-permute-done.5
  353.8 1.4 add_convert_fusion.1
  355.3 39.9 %project_back.2 = (f32[256,1152]{1,0:T(8,128)}, f32[8,1152]{1,0:T(8,128)}, f32[1,896]{1,0:T(1,128)}, bf16[1152,1152]{1,0:T(8,128)(2,1)}, f32[256,1152]{1,0:T(8,128)}) custom-call(f32[256,1152]{1,0:T(8,128)} %get-tuple-element.164.refs_0_, f32[256,1152]{1,0:T(8,128)} %get-tuple-element.143.refs_0_.refs_1_, f32[2,8,1152]{2,1,0:T(8,128)} %get-tuple-element.132.refs_1_.refs_2_, ...), custom_call_target="tpu_custom_call" | custom-call | flops 41999998976 | tf_op jit(solution)/shard_map/project_back/pallas_call | solution.py:348
  395.3 47.2 %mlp_back.3 = (f32[256,1152]{1,0:T(8,128)}, bf16[4,256,384]{2,1,0:T(8,128)(2,1)}, bf16[1152,1152]{1,0:T(8,128)(2,1)}, bf16[1152,384]{1,0:T(8,128)(2,1)}, f32[8,1...) custom-call(f32[256,1152]{1,0:T(8,128)} %get-tuple-element.172.refs_, ...), custom_call_target="tpu_custom_call" | custom-call | flops 48000000000 | tf_op jit(solution)/shard_map/mlp_back/pallas_call | solution.py:348
  442.6 1.0 collective-permute-start.6
  443.6 25.5 %attend_back.3 = (bf16[4,256,288]{2,1,0:T(8,128)(2,1)}, bf16[4,2,576,128]{3,2,1,0:T(8,128)(2,1)}, bf16[4,2,576,128]{3,2,1,0:T(8,128)(2,1)}) custom-call(s32[10]{0:T(128)} %pad_add_fusion.1.meta, bf16[4,256,288]{2,1,0:T(8,128)(2,1)} %get-tuple-element.135.queries, bf16[4,2,576,128]{3,2,1,0:T(8,128)(2,1)} %get-tuple-element.136.own_pairs, ...), custom_call_target="tpu_custom_call" | custom-call | flops 36999999488 | tf_op jit(solution)/shard_map/attend_back/pallas_call | solution.py:814
  469.1 0.8 slice_bitcast_fusion.2
  469.9 1.3 slice_bitcast_fusion
  471.2 3.2 collective-permute-done.6
  474.3 1.4 add_convert_fusion
  475.8 40.5 %project_back.3 = (f32[256,1152]{1,0:T(8,128)}, f32[8,1152]{1,0:T(8,128)}, f32[1,896]{1,0:T(1,128)}, bf16[1152,1152]{1,0:T(8,128)(2,1)}, f32[144,1152]{1,0:T(8,128)}) custom-call(f32[256,1152]{1,0:T(8,128)} %get-tuple-element.189.refs_0_, f32[256,1152]{1,0:T(8,128)} %get-tuple-element.131.refs_0_.refs_1_, f32[2,8,1152]{2,1,0:T(8,128)} %get-tuple-element.132.refs_1_.refs_2_, ...), custom_call_target="tpu_custom_call" | custom-call | flops 41999998976 | tf_op jit(solution)/shard_map/project_back/pallas_call | solution.py:348
  516.3 1.5 slice_bitcast_fusion.8
  517.8 56.9 %finish.1 = (f32[288,1024]{1,0:T(8,128)}, f32[288,1024]{1,0:T(8,128)}, f32[144,1152]{1,0:T(8,128)}, f32[2,288]{1,0:T(2,128)}, f32[2,288]{1,0:T(2,128)}, /*index=...) custom-call(f32[256,1152]{1,0:T(8,128)} %get-tuple-element.188.refs_, ...), custom_call_target="tpu_custom_call" | custom-call | flops 2000000000 | tf_op jit(solution)/shard_map/finish/pallas_call | solution.py:348
  574.8 1.1 slice_bitcast_fusion.3
  575.8 1.2 slice_bitcast_fusion.1
  577.0 0.2 slice_bitcast_fusion.9
  577.3 1.2 maximum_convert_fusion
  578.4 1.1 maximum_bitcast_fusion
  579.6 0.8 maximum_bitcast_fusion.1
  580.4 0.8 pad_maximum_fusion.5
  581.2 0.8 pad_maximum_fusion.4
  582.0 0.8 pad_maximum_fusion.3
  582.8 1.0 copy.50
  583.8 0.7 copy-done.4
  584.5 1.0 copy.51
  585.5 0.6 copy.52
  586.1 0.6 copy.53
  586.7 0.6 copy.54
  587.3 0.6 copy.55
  587.9 0.6 copy.56
  588.4 0.6 copy.57
  589.0 0.6 copy.58
  589.6 0.6 copy.59
  590.2 0.6 copy.60
  (104 shorter events, 2.4 us)
Async XLA Ops:
  7.2 5.2 copy-start.6
  7.2 105.9 %all-gather.6.cloned.1.call-start = ((), (), s32[]{:S(2)}) async-start(), calls=%async_computation.5 | async-start | bytes 1658880 | tf_op jit(solution)/shard_map/all_gather | solution.py:1586
  9.2 123.5 %all-gather.10.cloned.1.call-start = ((), (), s32[]{:S(2)}) async-start(), calls=%async_computation.7 | async-start | bytes 1658880 | tf_op jit(solution)/shard_map/all_gather | solution.py:1586
  9.3 3.3 copy-start.10
  9.3 3.3 copy-start.11
  9.3 3.3 copy-start.8
  9.3 3.3 copy-start.9
  9.3 122.0 %collective-permute-start.4 = (bf16[144,1152]{1,0:T(8,128)(2,1)S(1)}, bf16[144,1152]{1,0:T(8,128)(2,1)S(1)}, u32[]{:S(2)}, u32[]{:S(2)}) collective-permute-start(bf16[144,1152]{1,0:T(8,128)(2,1)S(1)} %pad.16), channel_id=1, source_target_pairs={{0,4},{4,0},{8,12},{12,8},{16,20},{20,16},{24,28},{28,24},{1,5},{5... | collective-permute-start | bytes 995336 | tf_op jit(solution)/shard_map/ppermute | solution.py:1579
  12.4 68.7 %collective-permute-start = (bf16[144,1152]{1,0:T(8,128)(2,1)S(1)}, bf16[144,1152]{1,0:T(8,128)(2,1)S(1)}, u32[]{:S(2)}, u32[]{:S(2)}) collective-permute-start(bf16[144,1152]{1,0:T(8,128)(2,1)S(1)} %pad.14), channel_id=1, source_target_pairs={{0,4},{4,0},{8,12},{12,8},{16,20},{20,16},{24,28},{28,24},{1,5},{5... | collective-permute-start | bytes 995336 | tf_op jit(solution)/shard_map/ppermute | solution.py:1579
  12.6 1.2 copy-start.12
  13.7 133.6 %all-gather.8.cloned.1.call-start = ((), (), s32[]{:S(2)}) async-start(), calls=%async_computation.6 | async-start | bytes 3317760 | tf_op jit(solution)/shard_map/all_gather | solution.py:1586
  82.2 161.7 %all-gather.12.cloned.1.call-start = ((), (), s32[]{:S(2)}) async-start(), calls=%async_computation.8 | async-start | bytes 3317760 | tf_op jit(solution)/shard_map/all_gather | solution.py:1586
  113.1 32.4 %collective-permute-start.1 = (bf16[576,1152]{1,0:T(8,128)(2,1)}, bf16[576,1152]{1,0:T(8,128)(2,1)}, u32[]{:S(2)}, u32[]{:S(2)}) collective-permute-start(bf16[576,1152]{1,0:T(8,128)(2,1)} %all-gather.6.cloned.1.call-done), channel_id=1, source_target_pairs={{0,4},{4,0},{8,12},{12,8},{16,20},{20,16},{24,28},{28,24},{1,5},{5... | collective-permute-start | bytes 3981320 | tf_op jit(solution)/shard_map/ppermute | solution.py:1579
  131.3 94.7 %collective-permute-start.3 = (bf16[144,1152]{1,0:T(8,128)(2,1)S(1)}, bf16[144,1152]{1,0:T(8,128)(2,1)S(1)}, u32[]{:S(2)}, u32[]{:S(2)}) collective-permute-start(bf16[144,1152]{1,0:T(8,128)(2,1)S(1)} %pad.13), channel_id=1, source_target_pairs={{0,4},{4,0},{8,12},{12,8},{16,20},{20,16},{24,28},{28,24},{1,5},{5... | collective-permute-start | bytes 995336 | tf_op jit(solution)/shard_map/ppermute | solution.py:1579
  132.4 147.6 %all-gather.14.cloned.1.call-start = ((), (), s32[]{:S(2)}) async-start(), calls=%async_computation.9 | async-start | bytes 3317760 | tf_op jit(solution)/shard_map/all_gather | solution.py:1586
  132.7 60.7 %collective-permute-start.2 = (bf16[576,1152]{1,0:T(8,128)(2,1)}, bf16[576,1152]{1,0:T(8,128)(2,1)}, u32[]{:S(2)}, u32[]{:S(2)}) collective-permute-start(bf16[576,1152]{1,0:T(8,128)(2,1)} %all-gather.10.cloned.1.call-done), channel_id=1, source_target_pairs={{0,4},{4,0},{8,12},{12,8},{16,20},{20,16},{24,28},{28,24},{1,5},{5... | collective-permute-start | bytes 3981320 | tf_op jit(solution)/shard_map/ppermute | solution.py:1579
  227.1 168.2 %reduce-scatter.6.cloned.1.call-start = ((), (), s32[]{:S(2)}) async-start(), calls=%async_computation.10 | async-start | bytes 3317760 | tf_op jit(solution)/shard_map/reduce_scatter | solution.py:1644
  320.8 1.3 copy-start.22
  320.9 121.7 %reduce-scatter.12.cloned.1.call-start = ((), (), s32[]{:S(2)}) async-start(), calls=%async_computation.13 | async-start | bytes 1658880 | tf_op jit(solution)/shard_map/reduce_scatter | solution.py:1644
  322.1 31.7 %collective-permute-start.5 = (bf16[4,144,1152]{2,1,0:T(8,128)(2,1)S(1)}, bf16[4,144,1152]{2,1,0:T(8,128)(2,1)S(1)}, u32[]{:S(2)}, u32[]{:S(2)}) collective-permute-start(bf16[4,144,1152]{2,1,0:T(8,128)(2,1)S(1)} %copy-done.22), channel_id=1, source_target_pairs={{0,4},{4,0},{8,12},{12,8},{16,20},{20,16},{24,28},{28,24},{1,5},{5... | collective-permute-start | bytes 3981320 | tf_op jit(solution)/shard_map/ppermute | solution.py:1579
  323.6 30.2 %copy-start.1 = (bf16[4,144,1152]{2,1,0:T(8,128)(2,1)S(1)}, bf16[4,144,1152]{2,1,0:T(8,128)(2,1)}, u32[]{:S(2)}) copy-start(bf16[4,144,1152]{2,1,0:T(8,128)(2,1)} %get-tuple-element.158) | copy-start | bytes 3981316
  355.2 115.9 %reduce-scatter.8.cloned.1.call-start = ((), (), s32[]{:S(2)}) async-start(), calls=%async_computation.11 | async-start | bytes 3317760 | tf_op jit(solution)/shard_map/reduce_scatter | solution.py:1644
  395.2 122.6 %reduce-scatter.14.cloned.1.call-start = ((), (), s32[]{:S(2)}) async-start(), calls=%async_computation.14 | async-start | bytes 3317760 | tf_op jit(solution)/shard_map/reduce_scatter | solution.py:1644
  442.6 132.2 %reduce-scatter.10.cloned.1.call-start = ((), (), s32[]{:S(2)}) async-start(), calls=%async_computation.12 | async-start | bytes 1658880 | tf_op jit(solution)/shard_map/reduce_scatter | solution.py:1644
  442.6 31.7 %collective-permute-start.6 = (bf16[4,144,1152]{2,1,0:T(8,128)(2,1)}, bf16[4,144,1152]{2,1,0:T(8,128)(2,1)S(1)}, u32[]{:S(2)}, u32[]{:S(2)}) collective-permute-start(bf16[4,144,1152]{2,1,0:T(8,128)(2,1)} %get-tuple-element.182), channel_id=1, source_target_pairs={{0,4},{4,0},{8,12},{12,8},{16,20},{20,16},{24,28},{28,24},{1,5},{5... | collective-permute-start | bytes 3981320 | tf_op jit(solution)/shard_map/ppermute | solution.py:1579
  443.6 25.5 %copy-start.7 = (bf16[144,1152]{1,0:T(8,128)(2,1)S(1)}, bf16[144,1152]{1,0:T(8,128)(2,1)}, u32[]{:S(2)}) copy-start(bf16[144,1152]{1,0:T(8,128)(2,1)} %reduce-scatter.12.cloned.1.call-done) | copy-start | bytes 995332
  469.1 5.2 copy-start
  574.7 2.3 copy-start.3
  575.8 1.4 copy-start.2
  580.4 2.4 copy-start.5
  582.8 1.7 copy-start.4
  584.5 1.1 copy-start.21
  584.5 1.7 copy-start.20
  584.5 2.2 copy-start.19
  584.5 2.8 copy-start.18
  584.5 3.4 copy-start.17
  584.5 4.0 copy-start.16
  584.5 4.5 copy-start.15
  584.5 5.1 copy-start.13
  584.5 5.7 copy-start.14
Sparse Core Ops, SparseCore 0:
  10.2 45.3 all-gather.5
  57.7 33.0 all-gather.9
  92.9 54.3 all-gather.7
  149.3 54.1 all-gather.11
  227.2 52.7 all-gather.13
  321.0 53.3 reduce-scatter.5
  377.2 31.3 reduce-scatter.11
  410.9 51.4 reduce-scatter.7
  464.7 52.3 reduce-scatter.13
  519.8 47.6 reduce-scatter.9
